TPU v7x, 32 devices: a whole 2x2x4 slice. The times are simulated.
32 devices in a mesh: dp: 8 (over z, core), mp: 4 (over y, x).
Axes of the slice: x: 2, y: 2, z: 4, core: 2. Of those that a mesh axis runs over, the one named last changes fastest.
Arguments:
- tokens: bfloat16 [4096, 1280], P('dp'), may hold values from -6 to 6
- norm_gain: float32 [1280], replicated, may hold values from 0.25 to 1.75
- widen_weight: bfloat16 [1280, 5120], P(None, 'mp'), may hold values from -0.15625 to 0.15625
- narrow_weight: bfloat16 [5120, 1280], P('mp'), may hold values from -0.078125 to 0.078125
- final_gain: float32 [1280], replicated, may hold values from 0.25 to 1.75
- adaptor_in: bfloat16 [3, 1280, 1280], P(None, None, 'mp'), may hold values from -0.15625 to 0.15625
- head_dino: bfloat16 [1280, 1536], P('mp'), may hold values from -0.15625 to 0.15625
- head_siglip: bfloat16 [1280, 1152], P('mp'), may hold values from -0.15625 to 0.15625
- head_sam: bfloat16 [1280, 1280], P('mp'), may hold values from -0.15625 to 0.15625
- teacher_dino: bfloat16 [2, 4096, 1536], P(None, 'dp', 'mp'), may hold values from -6 to 6
- teacher_siglip: bfloat16 [2, 4096, 1152], P(None, 'dp', 'mp'), may hold values from -6 to 6
- teacher_sam: bfloat16 [2, 4096, 1280], P(None, 'dp', 'mp'), may hold values from -6 to 6
- step_lags: int32 [3], replicated, may hold values from 1 to 2, as said below
- owner_slot: int32 [128], replicated, may hold values from 0 to 127, as said below
Outputs:
- grad_widen: float32 [5120, 1280], P('mp', 'dp')
- grad_narrow: float32 [5120, 1280], P('mp', 'dp')
- grad_adaptor: float32 [3, 1280, 1280], P(None, 'dp', 'mp')
- grad_dino: float32 [1280, 1536], P('mp', 'dp')
- grad_siglip: float32 [1280, 1152], P('mp', 'dp')
- grad_sam: float32 [1280, 1280], P('mp', 'dp')
Inputs may be any that keep to these rules, and one draw needn't show every extreme that they name: owner_slot is a permutation; of the 16 images in each aligned block of 16 images, exactly 2 have slots in each aligned block of 16 slots. `step_lags`: the three lags are not all equal.
All inputs are finite; a program needn't handle non-finite values.
Results may differ from a plain program's by a relative error of at most 0.02.
Values may be sent and summed in bfloat16 or wider, within the bound.
No kernel may reach another device: no remote copies, remote signals or barrier semaphores. Data moves between devices by JAX's collectives and lax.ppermute only.
A program may use at most 128 MiB of HBM per device.

v0:
```python
import functools

import jax
import jax.numpy as jnp
from jax import lax
from jax.experimental import pallas as pl
from jax.experimental.pallas import tpu as pltpu
from jax.sharding import PartitionSpec as P

PATCH = 32


slope_coef = 0.7978845608028654
cubic_coef = 0.044715


def smooth(value):
    return 0.5 * value * (1.0 + jnp.tanh(slope_coef * (value + cubic_coef * value * value * value)))


def smooth_slope(value):
    tangent = jnp.tanh(slope_coef * (value + cubic_coef * value * value * value))
    return 0.5 * (1.0 + tangent) + 0.5 * value * (1.0 - tangent * tangent) * slope_coef * (
        1.0 + 3.0 * cubic_coef * value * value
    )


def normalize(value, gain):
    centre = value - jnp.mean(value, axis=-1, keepdims=True)
    inverse = lax.rsqrt(jnp.mean(centre * centre, axis=-1, keepdims=True) + 1e-06)
    normal = centre * inverse
    return (normal * gain, normal, inverse)


def normalize_back(upstream, gain, normal, inverse):
    scaled = upstream * gain
    return inverse * (
        scaled
        - jnp.mean(scaled, axis=-1, keepdims=True)
        - normal * jnp.mean(scaled * normal, axis=-1, keepdims=True)
    )


def finish(product, square_student, square_target, student, target):
    joint = lax.rsqrt(square_student * square_target)
    cosine = product * joint
    slope = cosine[:, None] * student / square_student[:, None] - target * joint[:, None]
    return (cosine, slope)


def swap(value, axis, offset):
    count = lax.axis_size(axis)
    return lax.ppermute(value, axis, [(i, i ^ offset) for i in range(count)])


def ordered(value, count, position):
    cut = value.reshape((count, value.shape[0] // count) + value.shape[1:])
    return [
        lax.dynamic_index_in_dim(cut, position ^ j, 0, keepdims=False) for j in range(count)
    ]


def scatter_sum(blocks, axis):
    total = blocks[0]
    arrived = [
        swap(blocks[j].astype(jnp.bfloat16), axis, j) for j in range(1, len(blocks))
    ]
    for piece in arrived:
        total = total + piece.astype(jnp.float32)
    return total


def gather(piece, axis):
    return jnp.concatenate(
        [piece] + [swap(piece, axis, j) for j in range(1, lax.axis_size(axis))], axis=0
    )


def bits_of(count, low_first):
    bits = [1 << k for k in range(count.bit_length() - 1)]
    return bits if low_first else bits[::-1]


def scatter_halving(blocks, axis, low_first):
    held = dict(enumerate(blocks))
    size = blocks[0].shape[0]
    bits = bits_of(len(blocks), low_first)
    for bit in bits:
        leaving = [j for j in sorted(held) if j & bit]
        packed = jnp.concatenate([held.pop(j).astype(jnp.bfloat16) for j in leaving], axis=0)
        packed = swap(packed, axis, bit)
        if bit == bits[-1]:
            return held[0], packed
        for k, j in enumerate(leaving):
            held[j ^ bit] = held[j ^ bit] + packed[k * size : (k + 1) * size].astype(jnp.float32)


def gather_doubling(piece, axis, low_first):
    held = {0: piece}
    size = piece.shape[0]
    for bit in bits_of(lax.axis_size(axis), low_first):
        order = sorted(held)
        packed = held[0] if len(order) == 1 else jnp.concatenate([held[j] for j in order], axis=0)
        packed = swap(packed, axis, bit)
        for k, j in enumerate(order):
            held[j ^ bit] = packed[k * size : (k + 1) * size]
    return jnp.concatenate([held[j] for j in sorted(held)], axis=0)


def reverse_bits(value, count):
    result = 0
    for k in range(count.bit_length() - 1):
        result = result * 2 + (value >> k) % 2
    return result


def limits(flops=0, moved=0):
    return dict(
        compiler_params=pltpu.CompilerParams(vmem_limit_bytes=48 * 2**20),
        cost_estimate=pl.CostEstimate(flops=flops, bytes_accessed=moved, transcendentals=0),
    )


IN_VMEM = pl.BlockSpec(memory_space=pltpu.VMEM)
IN_SMEM = pl.BlockSpec(memory_space=pltpu.SMEM)
IN_PLACE = pl.BlockSpec(memory_space=pl.ANY)


def pack_kernel(groups, images, turned, lag_ref, slot_ref, group_ref, *refs):
    count = len(turned)
    teachers, (keep_ref, send_ref) = refs[:count], refs[count : count + 2]
    held, sems = refs[count + 2 : -1], refs[-1]
    share = images // groups
    group = group_ref[0]
    copies = [
        pltpu.make_async_copy(teachers[t].at[lag_ref[t] - 1], held[t], sems.at[t])
        for t in range(count)
    ]
    for copy in copies:
        copy.start()
    slots = [slot_ref[group * images + i] for i in range(images)]
    places = []
    for i in range(images):
        rank = sum((slots[j] < slots[i]).astype(jnp.int32) for j in range(images) if j != i)
        away = lax.div(slots[i], images) ^ group
        spot = (away >> 1) * share + lax.rem(rank, share)
        places.append((away & 1, pl.ds(pl.multiple_of(spot * PATCH, PATCH), PATCH)))
    start = 0
    for t in range(count):
        copies[t].wait()
        value = held[t][...]
        if turned[t]:
            value = value.T
        columns = slice(start, start + value.shape[1])
        start += value.shape[1]
        for i, (side, to) in enumerate(places):
            piece = value[i * PATCH : (i + 1) * PATCH, :]

            @pl.when(side == 0)
            def _(piece=piece, to=to, columns=columns):
                keep_ref[to, columns] = piece

            @pl.when(side != 0)
            def _(piece=piece, to=to, columns=columns):
                send_ref[to, columns] = piece


def pack(step_lags, owner_slot, group, teachers, groups, images):
    rows = images * PATCH
    width = sum(teacher.shape[-1] for teacher in teachers)
    turned = [teacher.shape[-1] % 128 != 0 for teacher in teachers]
    teachers = [
        jnp.swapaxes(teacher, 1, 2) if turn else teacher for teacher, turn in zip(teachers, turned)
    ]
    half = jax.ShapeDtypeStruct((rows // 2, width), jnp.bfloat16)
    return pl.pallas_call(
        functools.partial(pack_kernel, groups, images, turned),
        out_shape=(half, half),
        in_specs=[IN_SMEM] * 3 + [IN_PLACE] * len(teachers),
        out_specs=(IN_VMEM, IN_VMEM),
        scratch_shapes=[pltpu.VMEM(teacher.shape[1:], jnp.bfloat16) for teacher in teachers]
        + [pltpu.SemaphoreType.DMA((len(teachers),))],
        name="pack",
        **limits(moved=4 * rows * width),
    )(step_lags, owner_slot, group.reshape(1), *teachers)


def place_kernel(images, place_ref, *refs):
    out_ref = refs[-1]
    each = images // (len(refs) - 1)
    for a in range(images):
        to = pl.ds(pl.multiple_of(place_ref[a] * PATCH, PATCH), PATCH)
        k = a % each
        out_ref[to, :] = refs[a // each][k * PATCH : (k + 1) * PATCH, :]


def loss_kernel(start, width, count, member_ref, *refs):
    parts, terms = refs[:count], refs[count:]
    sides = len(terms) // 3
    terms, slope_refs = terms[: 2 * sides], terms[2 * sides :]
    member = member_ref[0]
    pieces = [part[:, start : start + width].astype(jnp.float32) for part in parts]
    for bit in bits_of(count, True):
        flipped = (member & bit) != 0
        pieces = [jnp.where(flipped, pieces[j ^ bit], pieces[j]) for j in range(count)]
    target = jnp.concatenate(pieces, axis=-1)
    student = [
        terms[2 * k][...] + terms[2 * k + 1][...].astype(jnp.float32) for k in range(sides)
    ]
    student = student[0] if sides == 1 else jnp.concatenate(student, axis=-1)
    product = jnp.sum(student * target, axis=-1, keepdims=True)
    square_student = jnp.sum(student * student, axis=-1, keepdims=True) + 1e-06
    square_target = jnp.sum(target * target, axis=-1, keepdims=True) + 1e-06
    joint = lax.rsqrt(square_student * square_target)
    cosine = product * joint
    slope = ((cosine / square_student) * student - target * joint).astype(jnp.bfloat16)
    wide = slope.shape[1] // sides
    for k in range(sides):
        slope_refs[k][...] = slope[:, k * wide : (k + 1) * wide]


def loss(member, terms, parts, start, width):
    flat = [value for pair in terms for value in pair]
    return pl.pallas_call(
        functools.partial(loss_kernel, start, width, len(parts)),
        out_shape=[jax.ShapeDtypeStruct(last.shape, jnp.bfloat16) for _, last in terms],
        in_specs=[IN_SMEM] + [IN_VMEM] * (len(parts) + len(flat)),
        out_specs=[IN_VMEM] * len(terms),
        name="loss",
        **limits(moved=10 * sum(last.size for _, last in terms)),
    )(member.reshape(1), *parts, *flat)


def beside(refs):
    return refs[0][...] if len(refs) == 1 else jnp.concatenate([r[...] for r in refs], axis=1)


def product_kernel(groups, shape, spot_ref, *refs):
    keep_ref, send_ref = refs[-2:]
    side, base = spot_ref[0] != 0, spot_ref[1]
    tall = keep_ref.shape[1]
    used = column = 0
    for lefts, rights in shape:
        left = beside(refs[used : used + lefts])
        right = beside(refs[used + lefts : used + lefts + rights])
        used += lefts + rights
        cut, wide = left.shape[1] // groups, right.shape[1]
        columns = slice(column, column + wide)
        column += wide
        full = lax.dot_general(
            left, right, (((0,), (0,)), ((), ())), preferred_element_type=jnp.float32
        )
        for pair in range(groups // 2):
            even = full[2 * pair * cut : (2 * pair + 1) * cut, :]
            odd = full[(2 * pair + 1) * cut : (2 * pair + 2) * cut, :]
            at = base ^ reverse_bits(pair, groups // 2)
            keep_ref[at, :cut, columns] = jnp.where(side, odd, even).astype(jnp.bfloat16)
            send_ref[at, :cut, columns] = jnp.where(side, even, odd).astype(jnp.bfloat16)
            if cut < tall:
                rest = jnp.zeros((tall - cut, wide), jnp.bfloat16)
                keep_ref[at, cut:, columns] = rest
                send_ref[at, cut:, columns] = rest


def product(pairs, groups, group):
    talls = [sum(left.shape[1] for left in lefts) for lefts, _ in pairs]
    wides = [sum(right.shape[1] for right in rights) for _, rights in pairs]
    tall, wide = max(talls) // groups, sum(wides)
    half = jax.ShapeDtypeStruct((groups // 2, tall, wide), jnp.bfloat16)
    spot = jnp.stack([group % 2, reverse_bits(group // 2, groups // 2)]).astype(jnp.int32)
    flat = [value for lefts, rights in pairs for value in (*lefts, *rights)]
    return pl.pallas_call(
        functools.partial(product_kernel, groups, [(len(l), len(r)) for l, r in pairs]),
        out_shape=(half, half),
        in_specs=[IN_SMEM] + [IN_VMEM] * len(flat),
        out_specs=(IN_VMEM, IN_VMEM),
        name="product",
        **limits(2 * flat[0].shape[0] * tall * groups * wide, 4 * tall * groups * wide),
    )(spot, *flat)


def pin(*values):
    return lax.optimization_barrier(values)


def begin(halves):
    keep, send = halves
    return (keep, swap(send, "dp", 1), 1)


def advance(state):
    keep, came, bit = state
    if keep.shape[0] == 1:
        return state
    held = keep.astype(jnp.float32) + came.astype(jnp.float32)
    half = held.shape[0] // 2
    return (held[:half], swap(held[half:].astype(jnp.bfloat16), "dp", 2 * bit), 2 * bit)


def complete(state):
    while state[0].shape[0] > 1:
        state = advance(state)
    keep, came, _ = state
    return keep[0].astype(jnp.float32) + came[0].astype(jnp.float32)


def arrive(state, came):
    return (state[0], came, state[2])


def local(
    tokens,
    norm_gain,
    widen_weight,
    narrow_weight,
    final_gain,
    adaptor_in,
    head_dino,
    head_siglip,
    head_sam,
    teacher_dino,
    teacher_siglip,
    teacher_sam,
    step_lags,
    owner_slot,
):
    groups = lax.axis_size("dp")
    members = lax.axis_size("mp")
    group = lax.axis_index("dp")
    member = lax.axis_index("mp")
    rows = tokens.shape[0]
    images = rows // PATCH
    share = images // groups
    block = rows // members
    heads = (head_dino, head_siglip, head_sam)
    teachers = (teacher_dino, teacher_siglip, teacher_sam)
    widths = [teacher.shape[-1] for teacher in teachers]
    exact = dict(preferred_element_type=jnp.float32)

    slots = owner_slot.reshape(groups, images)
    rank = jnp.sum(slots[:, :, None] > slots[:, None, :], axis=2, dtype=jnp.int32) % share
    source = lax.broadcasted_iota(jnp.int32, (groups, images), 0)
    landing = (source ^ group) * share + rank
    slot_rows = group * images + lax.broadcasted_iota(jnp.int32, (images,), 0)
    found = slots.reshape(1, -1) == slot_rows[:, None]
    landed = jnp.sum(jnp.where(found, landing.reshape(1, -1), 0), axis=1)
    position = lax.broadcasted_iota(jnp.int32, (images,), 0) ^ (member * (images // members))
    at = lax.broadcasted_iota(jnp.int32, (images, images), 0)
    place = jnp.sum(jnp.where(landed[None, :] == at, position[None, :], 0), axis=1)

    tokens = jnp.concatenate(ordered(tokens, members, member), axis=0)
    first, _, _ = normalize(tokens.astype(jnp.float32), norm_gain)
    first = lax.optimization_barrier(first.astype(jnp.bfloat16))
    widened = jnp.dot(first, widen_weight, **exact)
    active = smooth(widened).astype(jnp.bfloat16)
    mixed = jnp.dot(active, narrow_weight, **exact).reshape(members, block, -1)
    mixed, step_lags = pin(mixed, step_lags)
    hidden = tokens[:block].astype(jnp.float32) + scatter_sum(list(mixed), "mp")

    kept, crossing = pack(step_lags, owner_slot, group, teachers, groups, images)
    pairs = jnp.stack(
        [
            kept.reshape(groups // 2, share * PATCH, -1),
            swap(crossing, "dp", 1).reshape(groups // 2, share * PATCH, -1),
        ],
        axis=1,
    ).reshape(groups // 2, 2 * share * PATCH, -1)
    arrived = [pairs[0]] + [swap(pairs[o], "dp", 2 * o) for o in range(1, groups // 2)]
    owned = pl.pallas_call(
        functools.partial(place_kernel, images),
        out_shape=jax.ShapeDtypeStruct((rows, sum(widths)), jnp.bfloat16),
        in_specs=[IN_SMEM] + [IN_VMEM] * len(arrived),
        out_specs=IN_VMEM,
        name="place",
        **limits(moved=4 * rows * sum(widths)),
    )(place, *arrived)

    final_rows, normal_rows, inverse_rows = normalize(hidden, final_gain)
    final = gather(final_rows.astype(jnp.bfloat16), "mp")

    owned = owned.reshape(members, block, -1)
    parts = [owned[0]] + [swap(owned[j], "mp", j) for j in range(1, members)]

    ways = ((True, False), (True,), (False,))
    befores, lifteds, students = [], [], []
    for index in range(3):
        before = jnp.dot(final, adaptor_in[index], **exact)
        lifted = smooth(before).astype(jnp.bfloat16)
        partial = jnp.dot(lifted, heads[index], **exact).reshape(members, block, -1)
        befores.append(before)
        lifteds.append(lifted)
        wide = partial.shape[-1] // len(ways[index])
        students.append(
            [
                scatter_halving(list(partial[:, :, k * wide : (k + 1) * wide]), "mp", way)
                for k, way in enumerate(ways[index])
            ]
        )
    slopes = []
    start = 0
    for index in range(3):
        made = loss(member, students[index], parts, start, widths[index])
        start += widths[index]
        slopes.append([gather_doubling(s, "mp", way) for s, way in zip(made, ways[index])])
    inners = []
    upstream = 0.0
    for index in range(3):
        back = 0.0
        wide = slopes[index][0].shape[1]
        for k, slope in enumerate(slopes[index]):
            head = heads[index][:, k * wide : (k + 1) * wide]
            back = back + jnp.einsum("rc,hc->rh", slope, head, **exact)
        inner = (back * smooth_slope(befores[index])).astype(jnp.bfloat16)
        inners.append(inner)
        upstream = upstream + jnp.einsum("rh,dh->rd", inner, adaptor_in[index], **exact)
    upstream = upstream.reshape(members, block, -1)
    came = [swap(upstream[j].astype(jnp.bfloat16), "mp", j) for j in range(1, members)]

    of_heads = begin(product(list(zip(slopes, [[l] for l in lifteds])), groups, group))
    *came, arrived = pin(*came, of_heads[1])
    of_heads = advance(arrive(of_heads, arrived))
    total = upstream[0]
    for piece in came:
        total = total + piece.astype(jnp.float32)
    through_rows = normalize_back(total, final_gain, normal_rows, inverse_rows)
    through_rows = through_rows.astype(jnp.bfloat16)
    came = [swap(through_rows, "mp", j) for j in range(1, members)]
    of_adaptor = begin(product([([final], inners)], groups, group))
    *came, one, two = pin(*came, of_heads[1], of_adaptor[1])
    of_heads = advance(arrive(of_heads, one))
    of_adaptor = advance(arrive(of_adaptor, two))
    through = jnp.concatenate([through_rows, *came], axis=0)

    of_narrow = begin(product([([through], [active])], groups, group))
    back_two = jnp.einsum("rd,fd->rf", through, narrow_weight, **exact)
    inner_two = (back_two * smooth_slope(widened)).astype(jnp.bfloat16)
    inner_two, arrived = pin(inner_two, of_narrow[1])
    of_narrow = advance(arrive(of_narrow, arrived))
    of_widen = begin(product([([first], [inner_two])], groups, group))
    one, two = pin(of_adaptor[1], of_widen[1])
    of_adaptor = advance(arrive(of_adaptor, one))
    of_widen = advance(arrive(of_widen, two))
    one, two = pin(of_narrow[1], of_heads[1])
    of_narrow = advance(arrive(of_narrow, one))
    of_heads = arrive(of_heads, two)
    one, two = pin(of_widen[1], of_adaptor[1])
    of_widen = advance(arrive(of_widen, one))
    of_adaptor = arrive(of_adaptor, two)
    reduced = complete(of_heads)
    wide = lifteds[0].shape[1]
    head_grads = [
        reduced[: heads[k].shape[1] // groups, k * wide : (k + 1) * wide].T for k in range(3)
    ]
    grad_adaptor = jnp.stack(jnp.split(complete(of_adaptor), 3, axis=-1))
    grad_narrow = complete(of_narrow).T
    grad_widen = complete(of_widen).T
    return (grad_widen, grad_narrow, grad_adaptor, *head_grads)


def solution(mesh):
    placed = (
        P("dp", None),
        P(),
        P(None, "mp"),
        P("mp", None),
        P(),
        P(None, None, "mp"),
        P("mp", None),
        P("mp", None),
        P("mp", None),
        P(None, "dp", "mp"),
        P(None, "dp", "mp"),
        P(None, "dp", "mp"),
        P(),
        P(),
    )
    return jax.shard_map(
        local,
        mesh=mesh,
        in_specs=placed,
        out_specs=(
            P("mp", "dp"),
            P("mp", "dp"),
            P(None, "dp", "mp"),
            P("mp", "dp"),
            P("mp", "dp"),
            P("mp", "dp"),
        ),
        check_vma=False,
    )
```

profile of v0, /device:TPU:0, one launch (start us, length us, event | category | flops | bytes accessed | tf_op | source)
XLA Modules:
  0.0 301.6 jit_solution(6151750122320902849)
XLA Ops:
  3.5 3.6 %multiply_convert_fusion = (bf16[512,1280]{1,0:T(8,128)(2,1)S(1)}, f32[512,1280]{1,0:T(8,128)}) fusion(bf16[512,1280]{1,0:T(8,128)(2,1)S(1)} %fusion.5.refs_0_, bf16[1280,1280]{1,0:T(8,128)(2,1)S(1)} %copy-done), kind=kOutput, calls=%fused_computation.22 | convolution fusion | flops 1683619840 | bytes 8519680 | tf_op jit(solution)/shard_map/dot_general | solution.py:354
  7.1 1.9 fusion.83
  11.6 2.9 collective-permute-start
  16.1 3.5 %pack.1 = (bf16[256,992]{1,0:T(8,128)(2,1)S(1)}, bf16[256,992]{1,0:T(8,128)(2,1)S(1)}) custom-call(s32[3]{0:T(128)S(1)} %copy-done.8, s32[128]{0:T(128)S(1)} %copy-done.7, s32[1]{0:T(128)} %bitcast.13.group_ref, bf16[2,512,384]{2,1,0:T(8,128)(2,1)S(1)} %copy-done.4, bf16[2,288,512]{2,1,0:T(8,128)(2,1)S(1)} %bitcast.136, bf16[2,320,512]{2,1,0:T(8,128)(2,1)S(1)} %bitcast.135), custom_call_target="tpu_custom_call" | custom-call | bytes 2031616 | tf_op jit(solution)/shard_map/pack/pallas_call | solution.py:176
  20.5 2.8 collective-permute-done
  23.4 7.7 %collective-permute-done.1 = bf16[128,1280]{1,0:T(8,128)(2,1)} collective-permute-done((bf16[128,1280]{1,0:T(8,128)(2,1)}, bf16[128,1280]{1,0:T(8,128)(2,1)}, u32[]{:S(2)}, u32[]{:S(2)}) %collective-permute-start.1) | collective-permute-done | bytes 327712 | tf_op jit(solution)/shard_map/ppermute | solution.py:53
  31.0 1.7 fusion.74
  37.0 1.6 collective-permute-start.4
  38.7 2.6 collective-permute-start.5
  41.3 2.6 collective-permute-done.10
  43.9 3.6 %collective-permute-start.6 = (bf16[128,992]{1,0:T(8,128)(2,1)S(1)}, bf16[128,992]{1,0:T(8,128)(2,1)S(1)}, u32[]{:S(2)}, u32[]{:S(2)}) collective-permute-start(bf16[128,992]{1,0:T(8,128)(2,1)S(1)} %bitcast.144), channel_id=1, source_target_pairs={{0,24},{4,28},{8,16},{12,20},{16,8},{20,12},{24,0},{28,4},{1,25},{... | collective-permute-start | bytes 761864 | tf_op jit(solution)/shard_map/ppermute | solution.py:53
  47.5 2.3 collective-permute-done.11
  49.8 1.8 multiply_convert_fusion.2
  53.1 1.8 multiply_convert_fusion.3
  59.1 1.8 multiply_convert_fusion.1
  62.4 1.6 collective-permute-start.25
  65.3 11.6 %collective-permute-done.13 = bf16[256,768]{1,0:T(8,128)(2,1)} collective-permute-done((bf16[256,768]{1,0:T(8,128)(2,1)}, bf16[256,768]{1,0:T(8,128)(2,1)}, u32[]{:S(2)}, u32[]{:S(2)}) %collective-permute-start.13) | collective-permute-done | bytes 393248 | tf_op jit(solution)/shard_map/ppermute | solution.py:53
  80.8 1.6 collective-permute-done.7.refs_1_
  85.8 12.7 %collective-permute-done.8.refs_2_ = bf16[128,992]{1,0:T(8,128)(2,1)S(1)} collective-permute-done((bf16[128,992]{1,0:T(8,128)(2,1)S(1)}, bf16[128,992]{1,0:T(8,128)(2,1)S(1)}, u32[]{:S(2)}, u32[]{:S(2)}) %collective-permute-start.8) | collective-permute-done | bytes 253984 | tf_op jit(solution)/shard_map/ppermute | solution.py:53
  99.0 3.7 %collective-permute-done.14.refs_5_ = bf16[128,768]{1,0:T(8,128)(2,1)S(1)} collective-permute-done((bf16[128,768]{1,0:T(8,128)(2,1)S(1)}, bf16[128,768]{1,0:T(8,128)(2,1)S(1)}, u32[]{:S(2)}, u32[]{:S(2)}) %collective-permute-start.14) | collective-permute-done | bytes 196640 | tf_op jit(solution)/shard_map/ppermute | solution.py:53
  106.4 1.7 collective-permute-start.23
  108.1 2.0 collective-permute-done.19
  110.1 2.7 collective-permute-start.20
  113.0 3.7 %collective-permute-done.26.refs_5_ = bf16[128,1280]{1,0:T(8,128)(2,1)S(1)} collective-permute-done((bf16[128,1280]{1,0:T(8,128)(2,1)S(1)}, bf16[128,1280]{1,0:T(8,128)(2,1)S(1)}, u32[]{:S(2)}, u32[]{:S(2)}) %collective-permute-start.26) | collective-permute-done | bytes 327712 | tf_op jit(solution)/shard_map/ppermute | solution.py:53
  121.4 4.8 %collective-permute-done.20 = bf16[256,768]{1,0:T(8,128)(2,1)S(1)} collective-permute-done((bf16[256,768]{1,0:T(8,128)(2,1)S(1)}, bf16[256,768]{1,0:T(8,128)(2,1)S(1)}, u32[]{:S(2)}, u32[]{:S(2)}) %collective-permute-start.20) | collective-permute-done | bytes 393248 | tf_op jit(solution)/shard_map/ppermute | solution.py:53
  132.1 5.4 %collective-permute-done.24 = bf16[256,1152]{1,0:T(8,128)(2,1)S(1)} collective-permute-done((bf16[256,1152]{1,0:T(8,128)(2,1)S(1)}, bf16[256,1152]{1,0:T(8,128)(2,1)S(1)}, u32[]{:S(2)}, u32[]{:S(2)}) %collective-permute-start.24) | collective-permute-done | bytes 589856 | tf_op jit(solution)/shard_map/ppermute | solution.py:53
  139.9 2.1 collective-permute-done.28
  142.1 4.6 %product.4 = (bf16[4,192,960]{2,1,0:T(8,128)(2,1)}, bf16[4,192,960]{2,1,0:T(8,128)(2,1)}) custom-call(s32[2]{0:T(128)S(1)} %pad_add_fusion.spot_ref, bf16[512,768]{1,0:T(8,128)(2,1)S(1)} %constant_dynamic-update-slice_fusion.refs_0_, bf16[512,768]{1,0:T(8,128)(2,1)S(1)} %pad_maximum_fusion.5.refs_1_, bf16[512,320]{1,0:T(8,128)(2,1)S(1)} %get-tuple-element.116.refs_2_, ...), custom_call_target="tpu_custom_call" | custom-call | flops 1509949440 | bytes 5898240 | tf_op jit(solution)/shard_map/product/pallas_call | solution.py:272
  147.8 3.6 %fusion.82 = (bf16[512,1280]{1,0:T(8,128)(2,1)S(1)}, f32[512,1280]{1,0:T(8,128)}) fusion(f32[512,1280]{1,0:T(8,128)S(1)} %convolution_add_fusion.1, bf16[512,320]{1,0:T(8,128)(2,1)S(1)} %fusion.12.refs_3_, bf16[3,1280,320]{1,2,0:T(8,128)(2,1)} %param.19), kind=kOutput, calls=%fused_computation.194 | convolution fusion | flops 420741120 | bytes 7700480 | tf_op jit(solution)/shard_map/rh,dh->rd/dot_general | solution.py:415
  152.4 2.6 collective-permute-start.31
  155.1 2.2 product.5
  157.4 4.6 %collective-permute-done.29 = bf16[128,1280]{1,0:T(8,128)(2,1)S(1)} collective-permute-done((bf16[128,1280]{1,0:T(8,128)(2,1)S(1)}, bf16[128,1280]{1,0:T(8,128)(2,1)S(1)}, u32[]{:S(2)}, u32[]{:S(2)}) %collective-permute-start.29) | collective-permute-done | bytes 327712 | tf_op jit(solution)/shard_map/ppermute | solution.py:53
  162.0 7.2 %collective-permute-done.30 = bf16[128,1280]{1,0:T(8,128)(2,1)S(1)} collective-permute-done((bf16[128,1280]{1,0:T(8,128)(2,1)S(1)}, bf16[128,1280]{1,0:T(8,128)(2,1)S(1)}, u32[]{:S(2)}, u32[]{:S(2)}) %collective-permute-start.30) | collective-permute-done | bytes 327712 | tf_op jit(solution)/shard_map/ppermute | solution.py:53
  169.2 2.0 convert_add_fusion.2
  171.4 1.7 collective-permute-start.36
  178.4 7.2 %collective-permute-done.33 = bf16[128,1280]{1,0:T(8,128)(2,1)S(1)} collective-permute-done((bf16[128,1280]{1,0:T(8,128)(2,1)S(1)}, bf16[128,1280]{1,0:T(8,128)(2,1)S(1)}, u32[]{:S(2)}, u32[]{:S(2)}) %collective-permute-start.33) | collective-permute-done | bytes 327712 | tf_op jit(solution)/shard_map/ppermute | solution.py:53
  185.5 6.0 %collective-permute-done.34 = bf16[128,1280]{1,0:T(8,128)(2,1)S(1)} collective-permute-done((bf16[128,1280]{1,0:T(8,128)(2,1)S(1)}, bf16[128,1280]{1,0:T(8,128)(2,1)S(1)}, u32[]{:S(2)}, u32[]{:S(2)}) %collective-permute-start.34) | collective-permute-done | bytes 327712 | tf_op jit(solution)/shard_map/ppermute | solution.py:53
  191.7 2.5 product.6
  194.3 6.0 %fusion.2.refs_1_ = bf16[512,1280]{1,0:T(8,128)(2,1)S(1)} fusion(bf16[1280,1280]{1,0:T(8,128)(2,1)} %param.17, f32[512,1280]{1,0:T(8,128)} %get-tuple-element.115, bf16[128,1280]{1,0:T(8,128)(2,1)S(1)} %collective-permute-done.35, bf16[128,1280]{1,0:T(8,128)(2,1)S(1)} %collective-permute-done.34, bf16[128,1280]{1,0:T(8,128)(2,1)S(1)} %collective-permute-done.33, ...), kind=kOutput, calls=%fused_computation.12 | convolution fusion | flops 1695416320 | bytes 8519680 | tf_op jit(solution)/shard_map/rd,fd->rf/dot_general | solution.py:435
  201.9 2.6 collective-permute-start.45
  204.5 2.5 product.7
  209.3 19.1 %collective-permute-done.45 = bf16[1,192,960]{2,1,0:T(8,128)(2,1)} collective-permute-done((bf16[1,192,960]{2,1,0:T(8,128)(2,1)S(1)}, bf16[1,192,960]{2,1,0:T(8,128)(2,1)}, u32[]{:S(2)}, u32[]{:S(2)}) %collective-permute-start.45) | collective-permute-done | bytes 368672 | tf_op jit(solution)/shard_map/ppermute | solution.py:53
  228.3 2.1 collective-permute-done.44
  236.6 16.1 %collective-permute-done.39 = bf16[2,160,960]{2,1,0:T(8,128)(2,1)S(1)} collective-permute-done((bf16[2,160,960]{2,1,0:T(8,128)(2,1)S(1)}, bf16[2,160,960]{2,1,0:T(8,128)(2,1)S(1)}, u32[]{:S(2)}, u32[]{:S(2)}) %collective-permute-start.39) | collective-permute-done | bytes 614432 | tf_op jit(solution)/shard_map/ppermute | solution.py:53
  253.5 3.1 %collective-permute-start.42 = (bf16[1,160,960]{2,1,0:T(8,128)(2,1)S(1)}, bf16[1,160,960]{2,1,0:T(8,128)(2,1)S(1)}, u32[]{:S(2)}, u32[]{:S(2)}) collective-permute-start(bf16[1,160,960]{2,1,0:T(8,128)(2,1)S(1)} %slice.390), channel_id=1, source_target_pairs={{0,16},{4,20},{8,24},{12,28},{16,0},{20,4},{24,8},{28,12},{1,17},{... | collective-permute-start | bytes 921608 | tf_op jit(solution)/shard_map/ppermute | solution.py:53
  257.5 20.4 %collective-permute-done.42 = bf16[1,160,960]{2,1,0:T(8,128)(2,1)S(1)} collective-permute-done((bf16[1,160,960]{2,1,0:T(8,128)(2,1)S(1)}, bf16[1,160,960]{2,1,0:T(8,128)(2,1)S(1)}, u32[]{:S(2)}, u32[]{:S(2)}) %collective-permute-start.42) | collective-permute-done | bytes 307232 | tf_op jit(solution)/shard_map/ppermute | solution.py:53
  277.9 2.2 collective-permute-done.41
  282.7 17.5 %collective-permute-done.43 = bf16[1,160,1280]{2,1,0:T(8,128)(2,1)S(1)} collective-permute-done((bf16[1,160,1280]{2,1,0:T(8,128)(2,1)S(1)}, bf16[1,160,1280]{2,1,0:T(8,128)(2,1)S(1)}, u32[]{:S(2)}, u32[]{:S(2)}) %collective-permute-start.43) | collective-permute-done | bytes 409632 | tf_op jit(solution)/shard_map/ppermute | solution.py:53
  (231 shorter events, 68.1 us)
Async XLA Ops:
  10.6 20.4 %copy-start.12 = (bf16[128,1280]{1,0:T(8,128)(2,1)S(1)}, bf16[128,1280]{1,0:T(8,128)(2,1)}, u32[]{:S(2)}) copy-start(bf16[128,1280]{1,0:T(8,128)(2,1)} %copy-done.11) | copy-start | bytes 983044
  11.6 11.8 %collective-permute-start = (bf16[128,1280]{1,0:T(8,128)(2,1)}, bf16[128,1280]{1,0:T(8,128)(2,1)}, u32[]{:S(2)}, u32[]{:S(2)}) collective-permute-start(bf16[128,1280]{1,0:T(8,128)(2,1)} %get-tuple-element.90), channel_id=1, source_target_pairs={{0,1},{1,0},{2,3},{3,2},{4,5},{5,4},{6,7},{7,6},{8,9},{9,8},{10,11... | collective-permute-start | bytes 983048 | tf_op jit(solution)/shard_map/ppermute | solution.py:53
  14.5 16.5 %collective-permute-start.1 = (bf16[128,1280]{1,0:T(8,128)(2,1)}, bf16[128,1280]{1,0:T(8,128)(2,1)}, u32[]{:S(2)}, u32[]{:S(2)}) collective-permute-start(bf16[128,1280]{1,0:T(8,128)(2,1)} %get-tuple-element.92), channel_id=1, source_target_pairs={{0,2},{1,3},{2,0},{3,1},{4,6},{5,7},{6,4},{7,5},{8,10},{9,11},{10,... | collective-permute-start | bytes 983048 | tf_op jit(solution)/shard_map/ppermute | solution.py:53
  16.1 15.0 %collective-permute-start.2 = (bf16[128,1280]{1,0:T(8,128)(2,1)}, bf16[128,1280]{1,0:T(8,128)(2,1)}, u32[]{:S(2)}, u32[]{:S(2)}) collective-permute-start(bf16[128,1280]{1,0:T(8,128)(2,1)} %get-tuple-element.91), channel_id=1, source_target_pairs={{0,3},{1,2},{2,1},{3,0},{4,7},{5,6},{6,5},{7,4},{8,11},{9,10},{10,... | collective-permute-start | bytes 983048 | tf_op jit(solution)/shard_map/ppermute | solution.py:53
  19.6 17.3 %collective-permute-start.3 = (bf16[256,992]{1,0:T(8,128)(2,1)S(1)}, bf16[256,992]{1,0:T(8,128)(2,1)S(1)}, u32[]{:S(2)}, u32[]{:S(2)}) collective-permute-start(bf16[256,992]{1,0:T(8,128)(2,1)S(1)} %get-tuple-element.40), channel_id=1, source_target_pairs={{0,4},{4,0},{8,12},{12,8},{16,20},{20,16},{24,28},{28,24},{1,5},{5... | collective-permute-start | bytes 1523720 | tf_op jit(solution)/shard_map/ppermute | solution.py:53
  33.2 10.7 %collective-permute-start.10 = (bf16[128,1280]{1,0:T(8,128)(2,1)S(1)}, bf16[128,1280]{1,0:T(8,128)(2,1)S(1)}, u32[]{:S(2)}, u32[]{:S(2)}) collective-permute-start(bf16[128,1280]{1,0:T(8,128)(2,1)S(1)} %multiply_convert_fusion.5), channel_id=1, source_target_pairs={{0,1},{1,0},{2,3},{3,2},{4,5},{5,4},{6,7},{7,6},{8,9},{9,8},{10,11... | collective-permute-start | bytes 983048 | tf_op jit(solution)/shard_map/ppermute | solution.py:53
  34.5 15.3 %collective-permute-start.11 = (bf16[128,1280]{1,0:T(8,128)(2,1)S(1)}, bf16[128,1280]{1,0:T(8,128)(2,1)S(1)}, u32[]{:S(2)}, u32[]{:S(2)}) collective-permute-start(bf16[128,1280]{1,0:T(8,128)(2,1)S(1)} %multiply_convert_fusion.5), channel_id=1, source_target_pairs={{0,2},{1,3},{2,0},{3,1},{4,6},{5,7},{6,4},{7,5},{8,10},{9,11},{10,... | collective-permute-start | bytes 983048 | tf_op jit(solution)/shard_map/ppermute | solution.py:53
  35.3 14.5 %collective-permute-start.12 = (bf16[128,1280]{1,0:T(8,128)(2,1)S(1)}, bf16[128,1280]{1,0:T(8,128)(2,1)S(1)}, u32[]{:S(2)}, u32[]{:S(2)}) collective-permute-start(bf16[128,1280]{1,0:T(8,128)(2,1)S(1)} %multiply_convert_fusion.5), channel_id=1, source_target_pairs={{0,3},{1,2},{2,1},{3,0},{4,7},{5,6},{6,5},{7,4},{8,11},{9,10},{10,... | collective-permute-start | bytes 983048 | tf_op jit(solution)/shard_map/ppermute | solution.py:53
  37.0 23.9 %collective-permute-start.4 = (bf16[128,992]{1,0:T(8,128)(2,1)S(1)}, bf16[128,992]{1,0:T(8,128)(2,1)S(1)}, u32[]{:S(2)}, u32[]{:S(2)}) collective-permute-start(bf16[128,992]{1,0:T(8,128)(2,1)S(1)} %bitcast.146), channel_id=1, source_target_pairs={{0,8},{4,12},{8,0},{12,4},{16,24},{20,28},{24,16},{28,20},{1,9},{5... | collective-permute-start | bytes 761864 | tf_op jit(solution)/shard_map/ppermute | solution.py:53
  38.7 23.7 %collective-permute-start.5 = (bf16[128,992]{1,0:T(8,128)(2,1)S(1)}, bf16[128,992]{1,0:T(8,128)(2,1)S(1)}, u32[]{:S(2)}, u32[]{:S(2)}) collective-permute-start(bf16[128,992]{1,0:T(8,128)(2,1)S(1)} %bitcast.145), channel_id=1, source_target_pairs={{0,16},{4,20},{8,24},{12,28},{16,0},{20,4},{24,8},{28,12},{1,17},{... | collective-permute-start | bytes 761864 | tf_op jit(solution)/shard_map/ppermute | solution.py:53
  43.9 20.1 %collective-permute-start.6 = (bf16[128,992]{1,0:T(8,128)(2,1)S(1)}, bf16[128,992]{1,0:T(8,128)(2,1)S(1)}, u32[]{:S(2)}, u32[]{:S(2)}) collective-permute-start(bf16[128,992]{1,0:T(8,128)(2,1)S(1)} %bitcast.144), channel_id=1, source_target_pairs={{0,24},{4,28},{8,16},{12,20},{16,8},{20,12},{24,0},{28,4},{1,25},{... | collective-permute-start | bytes 761864 | tf_op jit(solution)/shard_map/ppermute | solution.py:53
  52.5 30.9 %collective-permute-start.21 = (bf16[256,1152]{1,0:T(8,128)(2,1)S(1)}, bf16[256,1152]{1,0:T(8,128)(2,1)}, u32[]{:S(2)}, u32[]{:S(2)}) collective-permute-start(bf16[256,1152]{1,0:T(8,128)(2,1)S(1)} %pad_maximum_fusion.8), channel_id=1, source_target_pairs={{0,1},{1,0},{2,3},{3,2},{4,5},{5,4},{6,7},{7,6},{8,9},{9,8},{10,11... | collective-permute-start | bytes 1769480 | tf_op jit(solution)/shard_map/ppermute | solution.py:53
  56.9 20.0 %collective-permute-start.13 = (bf16[256,768]{1,0:T(8,128)(2,1)}, bf16[256,768]{1,0:T(8,128)(2,1)}, u32[]{:S(2)}, u32[]{:S(2)}) collective-permute-start(bf16[256,768]{1,0:T(8,128)(2,1)} %pad_maximum_fusion.10), channel_id=1, source_target_pairs={{0,1},{1,0},{2,3},{3,2},{4,5},{5,4},{6,7},{7,6},{8,9},{9,8},{10,11... | collective-permute-start | bytes 1179656 | tf_op jit(solution)/shard_map/ppermute | solution.py:53
  60.9 17.0 %collective-permute-start.15 = (bf16[256,768]{1,0:T(8,128)(2,1)}, bf16[256,768]{1,0:T(8,128)(2,1)}, u32[]{:S(2)}, u32[]{:S(2)}) collective-permute-start(bf16[256,768]{1,0:T(8,128)(2,1)} %pad_maximum_fusion.11), channel_id=1, source_target_pairs={{0,2},{1,3},{2,0},{3,1},{4,6},{5,7},{6,4},{7,5},{8,10},{9,11},{10,... | collective-permute-start | bytes 1179656 | tf_op jit(solution)/shard_map/ppermute | solution.py:53
  62.4 42.5 %collective-permute-start.25 = (bf16[256,1280]{1,0:T(8,128)(2,1)S(1)}, bf16[256,1280]{1,0:T(8,128)(2,1)S(1)}, u32[]{:S(2)}, u32[]{:S(2)}) collective-permute-start(bf16[256,1280]{1,0:T(8,128)(2,1)S(1)} %slice.386), channel_id=1, source_target_pairs={{0,2},{1,3},{2,0},{3,1},{4,6},{5,7},{6,4},{7,5},{8,10},{9,11},{10,... | collective-permute-start | bytes 1966088 | tf_op jit(solution)/shard_map/ppermute | solution.py:53
  64.7 17.7 %collective-permute-start.7 = (bf16[128,992]{1,0:T(8,128)(2,1)S(1)}, bf16[128,992]{1,0:T(8,128)(2,1)S(1)}, u32[]{:S(2)}, u32[]{:S(2)}) collective-permute-start(bf16[128,992]{1,0:T(8,128)(2,1)S(1)} %get-tuple-element.101), channel_id=1, source_target_pairs={{0,1},{1,0},{2,3},{3,2},{4,5},{5,4},{6,7},{7,6},{8,9},{9,8},{10,11... | collective-permute-start | bytes 761864 | tf_op jit(solution)/shard_map/ppermute | solution.py:53
  76.9 21.6 %collective-permute-start.8 = (bf16[128,992]{1,0:T(8,128)(2,1)S(1)}, bf16[128,992]{1,0:T(8,128)(2,1)S(1)}, u32[]{:S(2)}, u32[]{:S(2)}) collective-permute-start(bf16[128,992]{1,0:T(8,128)(2,1)S(1)} %get-tuple-element.100), channel_id=1, source_target_pairs={{0,2},{1,3},{2,0},{3,1},{4,6},{5,7},{6,4},{7,5},{8,10},{9,11},{10,... | collective-permute-start | bytes 761864 | tf_op jit(solution)/shard_map/ppermute | solution.py:53
  77.9 21.1 %collective-permute-start.9 = (bf16[128,992]{1,0:T(8,128)(2,1)S(1)}, bf16[128,992]{1,0:T(8,128)(2,1)S(1)}, u32[]{:S(2)}, u32[]{:S(2)}) collective-permute-start(bf16[128,992]{1,0:T(8,128)(2,1)S(1)} %get-tuple-element.99), channel_id=1, source_target_pairs={{0,3},{1,2},{2,1},{3,0},{4,7},{5,6},{6,5},{7,4},{8,11},{9,10},{10,... | collective-permute-start | bytes 761864 | tf_op jit(solution)/shard_map/ppermute | solution.py:53
  82.4 20.3 %collective-permute-start.14 = (bf16[128,768]{1,0:T(8,128)(2,1)S(1)}, bf16[128,768]{1,0:T(8,128)(2,1)S(1)}, u32[]{:S(2)}, u32[]{:S(2)}) collective-permute-start(bf16[128,768]{1,0:T(8,128)(2,1)S(1)} %get-tuple-element.80), channel_id=1, source_target_pairs={{0,2},{1,3},{2,0},{3,1},{4,6},{5,7},{6,4},{7,5},{8,10},{9,11},{10,... | collective-permute-start | bytes 589832 | tf_op jit(solution)/shard_map/ppermute | solution.py:53
  83.4 19.3 %collective-permute-start.16 = (bf16[128,768]{1,0:T(8,128)(2,1)S(1)}, bf16[128,768]{1,0:T(8,128)(2,1)S(1)}, u32[]{:S(2)}, u32[]{:S(2)}) collective-permute-start(bf16[128,768]{1,0:T(8,128)(2,1)S(1)} %get-tuple-element.73), channel_id=1, source_target_pairs={{0,1},{1,0},{2,3},{3,2},{4,5},{5,4},{6,7},{7,6},{8,9},{9,8},{10,11... | collective-permute-start | bytes 589832 | tf_op jit(solution)/shard_map/ppermute | solution.py:53
  98.5 7.5 %collective-permute-start.22 = (bf16[128,1152]{1,0:T(8,128)(2,1)S(1)}, bf16[128,1152]{1,0:T(8,128)(2,1)S(1)}, u32[]{:S(2)}, u32[]{:S(2)}) collective-permute-start(bf16[128,1152]{1,0:T(8,128)(2,1)S(1)} %get-tuple-element.81), channel_id=1, source_target_pairs={{0,2},{1,3},{2,0},{3,1},{4,6},{5,7},{6,4},{7,5},{8,10},{9,11},{10,... | collective-permute-start | bytes 884744 | tf_op jit(solution)/shard_map/ppermute | solution.py:53
  103.1 9.7 %collective-permute-start.17 = (bf16[128,768]{1,0:T(8,128)(2,1)S(1)}, bf16[128,768]{1,0:T(8,128)(2,1)S(1)}, u32[]{:S(2)}, u32[]{:S(2)}) collective-permute-start(bf16[128,768]{1,0:T(8,128)(2,1)S(1)} %get-tuple-element.41), channel_id=1, source_target_pairs={{0,1},{1,0},{2,3},{3,2},{4,5},{5,4},{6,7},{7,6},{8,9},{9,8},{10,11... | collective-permute-start | bytes 589832 | tf_op jit(solution)/shard_map/ppermute | solution.py:53
  103.8 6.3 %collective-permute-start.19 = (bf16[128,768]{1,0:T(8,128)(2,1)S(1)}, bf16[128,768]{1,0:T(8,128)(2,1)S(1)}, u32[]{:S(2)}, u32[]{:S(2)}) collective-permute-start(bf16[128,768]{1,0:T(8,128)(2,1)S(1)} %get-tuple-element.42), channel_id=1, source_target_pairs={{0,2},{1,3},{2,0},{3,1},{4,6},{5,7},{6,4},{7,5},{8,10},{9,11},{10,... | collective-permute-start | bytes 589832 | tf_op jit(solution)/shard_map/ppermute | solution.py:53
  105.1 11.6 %collective-permute-start.26 = (bf16[128,1280]{1,0:T(8,128)(2,1)S(1)}, bf16[128,1280]{1,0:T(8,128)(2,1)S(1)}, u32[]{:S(2)}, u32[]{:S(2)}) collective-permute-start(bf16[128,1280]{1,0:T(8,128)(2,1)S(1)} %get-tuple-element.77), channel_id=1, source_target_pairs={{0,1},{1,0},{2,3},{3,2},{4,5},{5,4},{6,7},{7,6},{8,9},{9,8},{10,11... | collective-permute-start | bytes 983048 | tf_op jit(solution)/shard_map/ppermute | solution.py:53
  106.4 13.4 %collective-permute-start.23 = (bf16[128,1152]{1,0:T(8,128)(2,1)S(1)}, bf16[128,1152]{1,0:T(8,128)(2,1)S(1)}, u32[]{:S(2)}, u32[]{:S(2)}) collective-permute-start(bf16[128,1152]{1,0:T(8,128)(2,1)S(1)} %loss.4), channel_id=1, source_target_pairs={{0,1},{1,0},{2,3},{3,2},{4,5},{5,4},{6,7},{7,6},{8,9},{9,8},{10,11... | collective-permute-start | bytes 884744 | tf_op jit(solution)/shard_map/ppermute | solution.py:53
  110.1 16.1 %collective-permute-start.20 = (bf16[256,768]{1,0:T(8,128)(2,1)S(1)}, bf16[256,768]{1,0:T(8,128)(2,1)S(1)}, u32[]{:S(2)}, u32[]{:S(2)}) collective-permute-start(bf16[256,768]{1,0:T(8,128)(2,1)S(1)} %pad_maximum_fusion.13), channel_id=1, source_target_pairs={{0,1},{1,0},{2,3},{3,2},{4,5},{5,4},{6,7},{7,6},{8,9},{9,8},{10,11... | collective-permute-start | bytes 1179656 | tf_op jit(solution)/shard_map/ppermute | solution.py:53
  112.9 13.4 %collective-permute-start.18 = (bf16[256,768]{1,0:T(8,128)(2,1)S(1)}, bf16[256,768]{1,0:T(8,128)(2,1)S(1)}, u32[]{:S(2)}, u32[]{:S(2)}) collective-permute-start(bf16[256,768]{1,0:T(8,128)(2,1)S(1)} %pad_maximum_fusion.12), channel_id=1, source_target_pairs={{0,2},{1,3},{2,0},{3,1},{4,6},{5,7},{6,4},{7,5},{8,10},{9,11},{10,... | collective-permute-start | bytes 1179656 | tf_op jit(solution)/shard_map/ppermute | solution.py:53
  117.2 14.0 %collective-permute-start.27 = (bf16[128,1280]{1,0:T(8,128)(2,1)S(1)}, bf16[128,1280]{1,0:T(8,128)(2,1)S(1)}, u32[]{:S(2)}, u32[]{:S(2)}) collective-permute-start(bf16[128,1280]{1,0:T(8,128)(2,1)S(1)} %loss.5), channel_id=1, source_target_pairs={{0,2},{1,3},{2,0},{3,1},{4,6},{5,7},{6,4},{7,5},{8,10},{9,11},{10,... | collective-permute-start | bytes 983048 | tf_op jit(solution)/shard_map/ppermute | solution.py:53
  119.9 17.6 %collective-permute-start.24 = (bf16[256,1152]{1,0:T(8,128)(2,1)S(1)}, bf16[256,1152]{1,0:T(8,128)(2,1)S(1)}, u32[]{:S(2)}, u32[]{:S(2)}) collective-permute-start(bf16[256,1152]{1,0:T(8,128)(2,1)S(1)} %pad_maximum_fusion.9), channel_id=1, source_target_pairs={{0,2},{1,3},{2,0},{3,1},{4,6},{5,7},{6,4},{7,5},{8,10},{9,11},{10,... | collective-permute-start | bytes 1769480 | tf_op jit(solution)/shard_map/ppermute | solution.py:53
  131.3 10.7 %collective-permute-start.28 = (bf16[256,1280]{1,0:T(8,128)(2,1)S(1)}, bf16[256,1280]{1,0:T(8,128)(2,1)S(1)}, u32[]{:S(2)}, u32[]{:S(2)}) collective-permute-start(bf16[256,1280]{1,0:T(8,128)(2,1)S(1)} %pad_maximum_fusion.7), channel_id=1, source_target_pairs={{0,1},{1,0},{2,3},{3,2},{4,5},{5,4},{6,7},{7,6},{8,9},{9,8},{10,11... | collective-permute-start | bytes 1966088 | tf_op jit(solution)/shard_map/ppermute | solution.py:53
  146.7 22.5 %collective-permute-start.32 = (bf16[4,192,960]{2,1,0:T(8,128)(2,1)}, bf16[4,192,960]{2,1,0:T(8,128)(2,1)}, u32[]{:S(2)}, u32[]{:S(2)}) collective-permute-start(bf16[4,192,960]{2,1,0:T(8,128)(2,1)} %get-tuple-element.43), channel_id=1, source_target_pairs={{0,4},{4,0},{8,12},{12,8},{16,20},{20,16},{24,28},{28,24},{1,5},{5... | collective-permute-start | bytes 4423688 | tf_op jit(solution)/shard_map/ppermute | solution.py:53
  151.5 10.6 %collective-permute-start.29 = (bf16[128,1280]{1,0:T(8,128)(2,1)S(1)}, bf16[128,1280]{1,0:T(8,128)(2,1)S(1)}, u32[]{:S(2)}, u32[]{:S(2)}) collective-permute-start(bf16[128,1280]{1,0:T(8,128)(2,1)S(1)} %get-tuple-element.89), channel_id=1, source_target_pairs={{0,1},{1,0},{2,3},{3,2},{4,5},{5,4},{6,7},{7,6},{8,9},{9,8},{10,11... | collective-permute-start | bytes 983048 | tf_op jit(solution)/shard_map/ppermute | solution.py:53
  152.4 16.9 %collective-permute-start.30 = (bf16[128,1280]{1,0:T(8,128)(2,1)S(1)}, bf16[128,1280]{1,0:T(8,128)(2,1)S(1)}, u32[]{:S(2)}, u32[]{:S(2)}) collective-permute-start(bf16[128,1280]{1,0:T(8,128)(2,1)S(1)} %get-tuple-element.88), channel_id=1, source_target_pairs={{0,2},{1,3},{2,0},{3,1},{4,6},{5,7},{6,4},{7,5},{8,10},{9,11},{10,... | collective-permute-start | bytes 983048 | tf_op jit(solution)/shard_map/ppermute | solution.py:53
  152.4 16.8 %collective-permute-start.31 = (bf16[128,1280]{1,0:T(8,128)(2,1)S(1)}, bf16[128,1280]{1,0:T(8,128)(2,1)S(1)}, u32[]{:S(2)}, u32[]{:S(2)}) collective-permute-start(bf16[128,1280]{1,0:T(8,128)(2,1)S(1)} %get-tuple-element.87), channel_id=1, source_target_pairs={{0,3},{1,2},{2,1},{3,0},{4,7},{5,6},{6,5},{7,4},{8,11},{9,10},{10,... | collective-permute-start | bytes 983048 | tf_op jit(solution)/shard_map/ppermute | solution.py:53
  157.4 21.0 %collective-permute-start.37 = (bf16[4,160,960]{2,1,0:T(8,128)(2,1)S(1)}, bf16[4,160,960]{2,1,0:T(8,128)(2,1)S(1)}, u32[]{:S(2)}, u32[]{:S(2)}) collective-permute-start(bf16[4,160,960]{2,1,0:T(8,128)(2,1)S(1)} %get-tuple-element.49), channel_id=1, source_target_pairs={{0,4},{4,0},{8,12},{12,8},{16,20},{20,16},{24,28},{28,24},{1,5},{5... | collective-permute-start | bytes 3686408 | tf_op jit(solution)/shard_map/ppermute | solution.py:53
  171.4 20.1 %collective-permute-start.36 = (bf16[2,192,960]{2,1,0:T(8,128)(2,1)S(1)}, bf16[2,192,960]{2,1,0:T(8,128)(2,1)S(1)}, u32[]{:S(2)}, u32[]{:S(2)}) collective-permute-start(bf16[2,192,960]{2,1,0:T(8,128)(2,1)S(1)} %slice.384), channel_id=1, source_target_pairs={{0,8},{4,12},{8,0},{12,4},{16,24},{20,28},{24,16},{28,20},{1,9},{5... | collective-permute-start | bytes 2211848 | tf_op jit(solution)/shard_map/ppermute | solution.py:53
  174.8 10.7 %collective-permute-start.33 = (bf16[128,1280]{1,0:T(8,128)(2,1)S(1)}, bf16[128,1280]{1,0:T(8,128)(2,1)S(1)}, u32[]{:S(2)}, u32[]{:S(2)}) collective-permute-start(bf16[128,1280]{1,0:T(8,128)(2,1)S(1)} %multiply_convert_fusion.4), channel_id=1, source_target_pairs={{0,1},{1,0},{2,3},{3,2},{4,5},{5,4},{6,7},{7,6},{8,9},{9,8},{10,11... | collective-permute-start | bytes 983048 | tf_op jit(solution)/shard_map/ppermute | solution.py:53
  176.1 15.5 %collective-permute-start.34 = (bf16[128,1280]{1,0:T(8,128)(2,1)S(1)}, bf16[128,1280]{1,0:T(8,128)(2,1)S(1)}, u32[]{:S(2)}, u32[]{:S(2)}) collective-permute-start(bf16[128,1280]{1,0:T(8,128)(2,1)S(1)} %multiply_convert_fusion.4), channel_id=1, source_target_pairs={{0,2},{1,3},{2,0},{3,1},{4,6},{5,7},{6,4},{7,5},{8,10},{9,11},{10,... | collective-permute-start | bytes 983048 | tf_op jit(solution)/shard_map/ppermute | solution.py:53
  176.9 14.7 %collective-permute-start.35 = (bf16[128,1280]{1,0:T(8,128)(2,1)S(1)}, bf16[128,1280]{1,0:T(8,128)(2,1)S(1)}, u32[]{:S(2)}, u32[]{:S(2)}) collective-permute-start(bf16[128,1280]{1,0:T(8,128)(2,1)S(1)} %multiply_convert_fusion.4), channel_id=1, source_target_pairs={{0,3},{1,2},{2,1},{3,0},{4,7},{5,6},{6,5},{7,4},{8,11},{9,10},{10,... | collective-permute-start | bytes 983048 | tf_op jit(solution)/shard_map/ppermute | solution.py:53
  194.2 6.1 %collective-permute-start.38 = (bf16[4,160,1280]{2,1,0:T(8,128)(2,1)S(1)}, bf16[4,160,1280]{2,1,0:T(8,128)(2,1)S(1)}, u32[]{:S(2)}, u32[]{:S(2)}) collective-permute-start(bf16[4,160,1280]{2,1,0:T(8,128)(2,1)S(1)} %get-tuple-element.53), channel_id=1, source_target_pairs={{0,4},{4,0},{8,12},{12,8},{16,20},{20,16},{24,28},{28,24},{1,5},{5... | collective-permute-start | bytes 4915208 | tf_op jit(solution)/shard_map/ppermute | solution.py:53
  200.8 29.6 %collective-permute-start.44 = (bf16[2,160,1280]{2,1,0:T(8,128)(2,1)S(1)}, bf16[2,160,1280]{2,1,0:T(8,128)(2,1)}, u32[]{:S(2)}, u32[]{:S(2)}) collective-permute-start(bf16[2,160,1280]{2,1,0:T(8,128)(2,1)S(1)} %slice.382), channel_id=1, source_target_pairs={{0,8},{4,12},{8,0},{12,4},{16,24},{20,28},{24,16},{28,20},{1,9},{5... | collective-permute-start | bytes 2457608 | tf_op jit(solution)/shard_map/ppermute | solution.py:53
  201.9 26.4 %collective-permute-start.45 = (bf16[1,192,960]{2,1,0:T(8,128)(2,1)S(1)}, bf16[1,192,960]{2,1,0:T(8,128)(2,1)}, u32[]{:S(2)}, u32[]{:S(2)}) collective-permute-start(bf16[1,192,960]{2,1,0:T(8,128)(2,1)S(1)} %slice.389), channel_id=1, source_target_pairs={{0,16},{4,20},{8,24},{12,28},{16,0},{20,4},{24,8},{28,12},{1,17},{... | collective-permute-start | bytes 1105928 | tf_op jit(solution)/shard_map/ppermute | solution.py:53
  207.1 45.6 %collective-permute-start.40 = (bf16[4,160,1280]{2,1,0:T(8,128)(2,1)S(1)}, bf16[4,160,1280]{2,1,0:T(8,128)(2,1)S(1)}, u32[]{:S(2)}, u32[]{:S(2)}) collective-permute-start(bf16[4,160,1280]{2,1,0:T(8,128)(2,1)S(1)} %get-tuple-element.58), channel_id=1, source_target_pairs={{0,4},{4,0},{8,12},{12,8},{16,20},{20,16},{24,28},{28,24},{1,5},{5... | collective-permute-start | bytes 4915208 | tf_op jit(solution)/shard_map/ppermute | solution.py:53
  208.0 44.8 %collective-permute-start.39 = (bf16[2,160,960]{2,1,0:T(8,128)(2,1)S(1)}, bf16[2,160,960]{2,1,0:T(8,128)(2,1)S(1)}, u32[]{:S(2)}, u32[]{:S(2)}) collective-permute-start(bf16[2,160,960]{2,1,0:T(8,128)(2,1)S(1)} %slice.385), channel_id=1, source_target_pairs={{0,8},{4,12},{8,0},{12,4},{16,24},{20,28},{24,16},{28,20},{1,9},{5... | collective-permute-start | bytes 1843208 | tf_op jit(solution)/shard_map/ppermute | solution.py:53
  231.8 24.7 %collective-permute-start.46 = (bf16[1,160,1280]{2,1,0:T(8,128)(2,1)S(1)}, bf16[1,160,1280]{2,1,0:T(8,128)(2,1)S(1)}, u32[]{:S(2)}, u32[]{:S(2)}) collective-permute-start(bf16[1,160,1280]{2,1,0:T(8,128)(2,1)S(1)} %slice.387), channel_id=1, source_target_pairs={{0,16},{4,20},{8,24},{12,28},{16,0},{20,4},{24,8},{28,12},{1,17},{... | collective-permute-start | bytes 1228808 | tf_op jit(solution)/shard_map/ppermute | solution.py:53
  253.2 26.9 %collective-permute-start.41 = (bf16[2,160,1280]{2,1,0:T(8,128)(2,1)S(1)}, bf16[2,160,1280]{2,1,0:T(8,128)(2,1)S(1)}, u32[]{:S(2)}, u32[]{:S(2)}) collective-permute-start(bf16[2,160,1280]{2,1,0:T(8,128)(2,1)S(1)} %slice.383), channel_id=1, source_target_pairs={{0,8},{4,12},{8,0},{12,4},{16,24},{20,28},{24,16},{28,20},{1,9},{5... | collective-permute-start | bytes 2457608 | tf_op jit(solution)/shard_map/ppermute | solution.py:53
  253.5 24.4 %collective-permute-start.42 = (bf16[1,160,960]{2,1,0:T(8,128)(2,1)S(1)}, bf16[1,160,960]{2,1,0:T(8,128)(2,1)S(1)}, u32[]{:S(2)}, u32[]{:S(2)}) collective-permute-start(bf16[1,160,960]{2,1,0:T(8,128)(2,1)S(1)} %slice.390), channel_id=1, source_target_pairs={{0,16},{4,20},{8,24},{12,28},{16,0},{20,4},{24,8},{28,12},{1,17},{... | collective-permute-start | bytes 921608 | tf_op jit(solution)/shard_map/ppermute | solution.py:53
  280.3 19.9 %collective-permute-start.43 = (bf16[1,160,1280]{2,1,0:T(8,128)(2,1)S(1)}, bf16[1,160,1280]{2,1,0:T(8,128)(2,1)S(1)}, u32[]{:S(2)}, u32[]{:S(2)}) collective-permute-start(bf16[1,160,1280]{2,1,0:T(8,128)(2,1)S(1)} %slice.388), channel_id=1, source_target_pairs={{0,16},{4,20},{8,24},{12,28},{16,0},{20,4},{24,8},{28,12},{1,17},{... | collective-permute-start | bytes 1228808 | tf_op jit(solution)/shard_map/ppermute | solution.py:53
  (39 other events, 260.7 us)
where the time goes:
time: 307 us; the launch traced here: 302 us
  waiting for transfers between devices  168 us (55%)
  starting transfers between devices  56.5 us (18%)
  matrix products  28.6 us (9%)
  other arithmetic  20.1 us (7%)
  Pallas kernels  17.4 us (6%)
  local copies, waits for them, and re-layouts  9.24 us (3%)
    ppermute x47, waiting for transfers between devices, swap(): return lax.ppermute(value, axis, [(i, i ^ offset) for i in range(count)])  168 us
    ppermute x47, starting transfers between devices, swap(): return lax.ppermute(value, axis, [(i, i ^ offset) for i in range(count)])  56.5 us
    pallas_call x4, Pallas kernels, product(): pl.pallas_call(functools.partial(product_kernel, groups, [(len(l), len(r)...  11.9 us
  transfers between devices with their start and end apart: 47, of which 25 were waited for; matrix products, arithmetic and copies ran while one was open for 15% of the time, Pallas kernels for 3%

commit v1 on v0

--- a/solution.py
+++ b/solution.py
@@ -60,16 +60,6 @@
     ]
 
 
-def scatter_sum(blocks, axis):
-    total = blocks[0]
-    arrived = [
-        swap(blocks[j].astype(jnp.bfloat16), axis, j) for j in range(1, len(blocks))
-    ]
-    for piece in arrived:
-        total = total + piece.astype(jnp.float32)
-    return total
-
-
 def gather(piece, axis):
     return jnp.concatenate(
         [piece] + [swap(piece, axis, j) for j in range(1, lax.axis_size(axis))], axis=0
@@ -81,18 +71,25 @@
     return bits if low_first else bits[::-1]
 
 
-def scatter_halving(blocks, axis, low_first):
-    held = dict(enumerate(blocks))
-    size = blocks[0].shape[0]
+def scatter_begin(blocks, axis, low_first):
     bits = bits_of(len(blocks), low_first)
-    for bit in bits:
-        leaving = [j for j in sorted(held) if j & bit]
+    leaving = [j for j in range(len(blocks)) if j & bits[0]]
+    packed = jnp.concatenate([blocks[j].astype(jnp.bfloat16) for j in leaving], axis=0)
+    held = {j: blocks[j] for j in range(len(blocks)) if j not in leaving}
+    return [held, leaving, swap(packed, axis, bits[0])]
+
+
+def scatter_rest(held, leaving, packed, axis, low_first):
+    size = held[0].shape[0]
+    bits = bits_of(lax.axis_size(axis), low_first)
+    for bit, later in zip(bits, bits[1:]):
+        for k, j in enumerate(leaving):
+            piece = packed[k * size : (k + 1) * size]
+            held[j ^ bit] = held[j ^ bit] + piece.astype(jnp.float32)
+        leaving = [j for j in sorted(held) if j & later]
         packed = jnp.concatenate([held.pop(j).astype(jnp.bfloat16) for j in leaving], axis=0)
-        packed = swap(packed, axis, bit)
-        if bit == bits[-1]:
-            return held[0], packed
-        for k, j in enumerate(leaving):
-            held[j ^ bit] = held[j ^ bit] + packed[k * size : (k + 1) * size].astype(jnp.float32)
+        packed = swap(packed, axis, later)
+    return held[0], packed
 
 
 def gather_doubling(piece, axis, low_first):
@@ -114,10 +111,10 @@
     return result
 
 
-def limits(flops=0, moved=0):
+def limits(flops=0):
     return dict(
         compiler_params=pltpu.CompilerParams(vmem_limit_bytes=48 * 2**20),
-        cost_estimate=pl.CostEstimate(flops=flops, bytes_accessed=moved, transcendentals=0),
+        cost_estimate=pl.CostEstimate(flops=flops, bytes_accessed=0, transcendentals=0),
     )
 
 
@@ -181,7 +178,7 @@
         scratch_shapes=[pltpu.VMEM(teacher.shape[1:], jnp.bfloat16) for teacher in teachers]
         + [pltpu.SemaphoreType.DMA((len(teachers),))],
         name="pack",
-        **limits(moved=4 * rows * width),
+        **limits(),
     )(step_lags, owner_slot, group.reshape(1), *teachers)
 
 
@@ -227,7 +224,7 @@
         in_specs=[IN_SMEM] + [IN_VMEM] * (len(parts) + len(flat)),
         out_specs=[IN_VMEM] * len(terms),
         name="loss",
-        **limits(moved=10 * sum(last.size for _, last in terms)),
+        **limits(),
     )(member.reshape(1), *parts, *flat)
 
 
@@ -254,12 +251,12 @@
             even = full[2 * pair * cut : (2 * pair + 1) * cut, :]
             odd = full[(2 * pair + 1) * cut : (2 * pair + 2) * cut, :]
             at = base ^ reverse_bits(pair, groups // 2)
-            keep_ref[at, :cut, columns] = jnp.where(side, odd, even).astype(jnp.bfloat16)
-            send_ref[at, :cut, columns] = jnp.where(side, even, odd).astype(jnp.bfloat16)
             if cut < tall:
-                rest = jnp.zeros((tall - cut, wide), jnp.bfloat16)
-                keep_ref[at, cut:, columns] = rest
-                send_ref[at, cut:, columns] = rest
+                rest = jnp.zeros((tall - cut, wide), jnp.float32)
+                even = jnp.concatenate([even, rest], axis=0)
+                odd = jnp.concatenate([odd, rest], axis=0)
+            keep_ref[at, :, columns] = jnp.where(side, odd, even).astype(jnp.bfloat16)
+            send_ref[at, :, columns] = jnp.where(side, even, odd).astype(jnp.bfloat16)
 
 
 def product(pairs, groups, group):
@@ -275,7 +272,7 @@
         in_specs=[IN_SMEM] + [IN_VMEM] * len(flat),
         out_specs=(IN_VMEM, IN_VMEM),
         name="product",
-        **limits(2 * flat[0].shape[0] * tall * groups * wide, 4 * tall * groups * wide),
+        **limits(),
     )(spot, *flat)
 
 
@@ -283,25 +280,81 @@
     return lax.optimization_barrier(values)
 
 
+def merge_kernel(held_ref, came_ref, kept_ref, sent_ref):
+    half = kept_ref.shape[0]
+    for k in range(half):
+        low = held_ref[k].astype(jnp.float32) + came_ref[k].astype(jnp.float32)
+        high = held_ref[half + k].astype(jnp.float32) + came_ref[half + k].astype(jnp.float32)
+        kept_ref[k] = low
+        sent_ref[k] = high.astype(jnp.bfloat16)
+
+
+def merge(held, came):
+    shape = (held.shape[0] // 2, *held.shape[1:])
+    return pl.pallas_call(
+        merge_kernel,
+        out_shape=(
+            jax.ShapeDtypeStruct(shape, jnp.float32),
+            jax.ShapeDtypeStruct(shape, jnp.bfloat16),
+        ),
+        in_specs=[IN_VMEM, IN_VMEM],
+        out_specs=(IN_VMEM, IN_VMEM),
+        name="merge",
+        **limits(2**35),
+    )(held, came)
+
+
 def begin(halves):
     keep, send = halves
-    return (keep, swap(send, "dp", 1), 1)
-
-
-def advance(state):
-    keep, came, bit = state
-    if keep.shape[0] == 1:
+    bits = bits_of(2 * keep.shape[0], True)[1:]
+    return (keep, swap(send, "dp", 1), bits)
+
+
+def advance(state, kernel=False):
+    keep, came, bits = state
+    if not bits:
         return state
-    held = keep.astype(jnp.float32) + came.astype(jnp.float32)
-    half = held.shape[0] // 2
-    return (held[:half], swap(held[half:].astype(jnp.bfloat16), "dp", 2 * bit), 2 * bit)
-
-
-def complete(state):
-    while state[0].shape[0] > 1:
-        state = advance(state)
-    keep, came, _ = state
-    return keep[0].astype(jnp.float32) + came[0].astype(jnp.float32)
+    if kernel:
+        kept, sent = merge(keep, came)
+    else:
+        held = keep.astype(jnp.float32) + came.astype(jnp.float32)
+        half = held.shape[0] // 2
+        kept, sent = held[:half], held[half:].astype(jnp.bfloat16)
+    return (kept, swap(sent, "dp", bits[0]), bits[1:])
+
+
+def finish_kernel(cuts, *refs):
+    count = len(cuts)
+    outs = refs[2 * count :]
+    used = 0
+    for k in range(count):
+        total = refs[2 * k][0].astype(jnp.float32) + refs[2 * k + 1][0].astype(jnp.float32)
+        for rows, start, end in cuts[k]:
+            outs[used][...] = total[:rows, start:end]
+            used += 1
+
+
+def finish(states, cuts):
+    for state in states:
+        assert not state[2]
+    return pl.pallas_call(
+        functools.partial(finish_kernel, cuts),
+        out_shape=[
+            jax.ShapeDtypeStruct((rows, end - start), jnp.float32)
+            for cut in cuts
+            for rows, start, end in cut
+        ],
+        in_specs=[IN_VMEM] * (2 * len(states)),
+        out_specs=[IN_VMEM] * sum(len(cut) for cut in cuts),
+        name="finish",
+        **limits(2**35),
+    )(*[value for state in states for value in state[:2]])
+
+
+def settle(state, kernel=False):
+    while state[2]:
+        state = advance(state, kernel)
+    return state
 
 
 def arrive(state, came):
@@ -355,13 +408,16 @@
     active = smooth(widened).astype(jnp.bfloat16)
     mixed = jnp.dot(active, narrow_weight, **exact).reshape(members, block, -1)
     mixed, step_lags = pin(mixed, step_lags)
-    hidden = tokens[:block].astype(jnp.float32) + scatter_sum(list(mixed), "mp")
-
+    came = [swap(mixed[j].astype(jnp.bfloat16), "mp", j) for j in range(1, members)]
     kept, crossing = pack(step_lags, owner_slot, group, teachers, groups, images)
+    came[0], crossing = pin(came[0], swap(crossing, "dp", 1))
+    hidden = tokens[:block].astype(jnp.float32) + mixed[0]
+    for piece in came:
+        hidden = hidden + piece.astype(jnp.float32)
     pairs = jnp.stack(
         [
             kept.reshape(groups // 2, share * PATCH, -1),
-            swap(crossing, "dp", 1).reshape(groups // 2, share * PATCH, -1),
+            crossing.reshape(groups // 2, share * PATCH, -1),
         ],
         axis=1,
     ).reshape(groups // 2, 2 * share * PATCH, -1)
@@ -372,7 +428,7 @@
         in_specs=[IN_SMEM] + [IN_VMEM] * len(arrived),
         out_specs=IN_VMEM,
         name="place",
-        **limits(moved=4 * rows * sum(widths)),
+        **limits(),
     )(place, *arrived)
 
     final_rows, normal_rows, inverse_rows = normalize(hidden, final_gain)
@@ -387,15 +443,22 @@
         before = jnp.dot(final, adaptor_in[index], **exact)
         lifted = smooth(before).astype(jnp.bfloat16)
         partial = jnp.dot(lifted, heads[index], **exact).reshape(members, block, -1)
+        if index < 2:
+            final, partial = pin(final, partial)
         befores.append(before)
         lifteds.append(lifted)
         wide = partial.shape[-1] // len(ways[index])
         students.append(
             [
-                scatter_halving(list(partial[:, :, k * wide : (k + 1) * wide]), "mp", way)
+                scatter_begin(list(partial[:, :, k * wide : (k + 1) * wide]), "mp", way)
                 for k, way in enumerate(ways[index])
             ]
         )
+    students[0][0][2], parts[0] = pin(students[0][0][2], parts[0])
+    students = [
+        [scatter_rest(*term, "mp", way) for term, way in zip(terms, ways[index])]
+        for index, terms in enumerate(students)
+    ]
     slopes = []
     start = 0
     for index in range(3):
@@ -413,47 +476,62 @@
         inner = (back * smooth_slope(befores[index])).astype(jnp.bfloat16)
         inners.append(inner)
         upstream = upstream + jnp.einsum("rh,dh->rd", inner, adaptor_in[index], **exact)
+        if index == 1:
+            pairs = [(slopes[k], lifteds[k : k + 1]) for k in range(2)]
+            of_heads = begin(product(pairs, groups, group))
+            slopes[2][0], arrived = pin(slopes[2][0], of_heads[1])
+            of_heads = advance(arrive(of_heads, arrived))
     upstream = upstream.reshape(members, block, -1)
     came = [swap(upstream[j].astype(jnp.bfloat16), "mp", j) for j in range(1, members)]
 
-    of_heads = begin(product(list(zip(slopes, [[l] for l in lifteds])), groups, group))
-    *came, arrived = pin(*came, of_heads[1])
-    of_heads = advance(arrive(of_heads, arrived))
-    total = upstream[0]
+    mine, *inners = pin(upstream[0], *inners)
+    of_rest = begin(
+        product([([final], inners), (slopes[2], lifteds[2:])], groups, group)
+    )
+    came[0], one, two = pin(came[0], of_heads[1], of_rest[1])
+    of_heads = advance(arrive(of_heads, one))
+    of_rest = advance(arrive(of_rest, two))
+    total = mine
     for piece in came:
         total = total + piece.astype(jnp.float32)
     through_rows = normalize_back(total, final_gain, normal_rows, inverse_rows)
     through_rows = through_rows.astype(jnp.bfloat16)
     came = [swap(through_rows, "mp", j) for j in range(1, members)]
-    of_adaptor = begin(product([([final], inners)], groups, group))
-    *came, one, two = pin(*came, of_heads[1], of_adaptor[1])
-    of_heads = advance(arrive(of_heads, one))
-    of_adaptor = advance(arrive(of_adaptor, two))
+    came[-1], one = pin(came[-1], of_rest[1])
+    of_rest = advance(arrive(of_rest, one))
     through = jnp.concatenate([through_rows, *came], axis=0)
 
     of_narrow = begin(product([([through], [active])], groups, group))
     back_two = jnp.einsum("rd,fd->rf", through, narrow_weight, **exact)
     inner_two = (back_two * smooth_slope(widened)).astype(jnp.bfloat16)
-    inner_two, arrived = pin(inner_two, of_narrow[1])
-    of_narrow = advance(arrive(of_narrow, arrived))
-    of_widen = begin(product([([first], [inner_two])], groups, group))
-    one, two = pin(of_adaptor[1], of_widen[1])
-    of_adaptor = advance(arrive(of_adaptor, one))
-    of_widen = advance(arrive(of_widen, two))
-    one, two = pin(of_narrow[1], of_heads[1])
-    of_narrow = advance(arrive(of_narrow, one))
-    of_heads = arrive(of_heads, two)
-    one, two = pin(of_widen[1], of_adaptor[1])
-    of_widen = advance(arrive(of_widen, one))
-    of_adaptor = arrive(of_adaptor, two)
-    reduced = complete(of_heads)
+    inner_two, one = pin(inner_two, of_narrow[1])
+    of_narrow = advance(arrive(of_narrow, one), True)
+    of_widen = advance(begin(product([([first], [inner_two])], groups, group)), True)
+    of_narrow = settle(of_narrow, True)
+    of_widen = settle(of_widen, True)
+    of_heads, of_rest = settle(of_heads), settle(of_rest)
+    keep, *landed = pin(of_widen[0], of_narrow[1], of_heads[1], of_rest[1])
+    of_widen = (keep, *of_widen[1:])
+    of_narrow, of_heads, of_rest = [
+        arrive(state, one) for state, one in zip((of_narrow, of_heads, of_rest), landed)
+    ]
     wide = lifteds[0].shape[1]
-    head_grads = [
-        reduced[: heads[k].shape[1] // groups, k * wide : (k + 1) * wide].T for k in range(3)
-    ]
-    grad_adaptor = jnp.stack(jnp.split(complete(of_adaptor), 3, axis=-1))
-    grad_narrow = complete(of_narrow).T
-    grad_widen = complete(of_widen).T
+    cuts = [head.shape[1] // groups for head in heads]
+    deep = final.shape[1] // groups
+    spans = [(k * wide, (k + 1) * wide) for k in range(4)]
+    made = finish(
+        [of_heads, of_rest, of_narrow],
+        [
+            [(cuts[0], *spans[0]), (cuts[1], *spans[1])],
+            [(deep, *span) for span in spans[:3]] + [(cuts[2], *spans[3])],
+            [(deep, 0, active.shape[1])],
+        ],
+    )
+    head_grads = [made[0].T, made[1].T, made[5].T]
+    grad_adaptor = jnp.stack(made[2:5])
+    grad_narrow = made[6].T
+    keep, came, _ = of_widen
+    grad_widen = (keep[0].astype(jnp.float32) + came[0].astype(jnp.float32)).T
     return (grad_widen, grad_narrow, grad_adaptor, *head_grads)
 
 

time: 307 us -> 287 us (0.935); the launches traced: 302 us -> 286 us
  starting transfers between devices: 56.5 us -> 48.8 us
  other arithmetic: 20.1 us -> 13.6 us
  matrix products: 28.6 us -> 24.6 us
    ppermute x47, starting transfers between devices: 56.5 us -> 48.8 us  [swap(): return lax.ppermute(value, axis, [(i, i ^ offset) for i in range(count)])]
    add x8 -> x4, other arithmetic: 5.14 us -> 0.73 us  [advance(): held = keep.astype(jnp.float32) + came.astype(jnp.float32)]
    pallas_call x0 -> x5, Pallas kernels: none -> 3.34 us  [the longest x1 2.38 us: finish(): pl.pallas_call(functools.partial(finish_kernel, cuts), out_shape=[jax.Sha...]
  transfers between devices with their start and end apart: 47 -> 47, of which waited for: 25 -> 25; matrix products, arithmetic and copies ran while one was open for 15% -> 11% of each run, Pallas kernels for 3% -> 4%
where the time goes in v1:
time: 287 us; the launch traced here: 286 us
  waiting for transfers between devices  168 us (59%)
  starting transfers between devices  48.8 us (17%)
  matrix products  24.6 us (9%)
  Pallas kernels  20.4 us (7%)
  other arithmetic  13.6 us (5%)
  local copies, waits for them, and re-layouts  9.1 us (3%)
    ppermute x47, waiting for transfers between devices, swap(): return lax.ppermute(value, axis, [(i, i ^ offset) for i in range(count)])  168 us
    ppermute x47, starting transfers between devices, swap(): return lax.ppermute(value, axis, [(i, i ^ offset) for i in range(count)])  48.8 us
    pallas_call x4, Pallas kernels, product(): pl.pallas_call(functools.partial(product_kernel, groups, [(len(l), len(r)...  11.6 us
  transfers between devices with their start and end apart: 47, of which 25 were waited for; matrix products, arithmetic and copies ran while one was open for 11% of the time, Pallas kernels for 4%

profile of v1, /device:TPU:0, one launch (start us, length us, event | category | flops | bytes accessed | tf_op | source)
XLA Modules:
  0.0 286.0 jit_solution(493858240185560144)
XLA Ops:
  0.7 1.5 dynamic-slice_bitcast_fusion.3
  3.5 3.6 %multiply_convert_fusion = (bf16[512,1280]{1,0:T(8,128)(2,1)S(1)}, f32[512,1280]{1,0:T(8,128)}) fusion(bf16[512,1280]{1,0:T(8,128)(2,1)S(1)} %fusion.5.refs_0_, bf16[1280,1280]{1,0:T(8,128)(2,1)S(1)} %copy-done), kind=kOutput, calls=%fused_computation.19 | convolution fusion | flops 1683619840 | bytes 8519680 | tf_op jit(solution)/shard_map/dot_general | solution.py:407
  7.1 1.9 fusion.69
  9.1 3.5 %pack.1 = (bf16[256,992]{1,0:T(8,128)(2,1)S(1)}, bf16[256,992]{1,0:T(8,128)(2,1)S(1)}) custom-call(s32[3]{0:T(128)S(1)} %copy-done.10, s32[128]{0:T(128)S(1)} %copy-done.9, s32[1]{0:T(128)} %bitcast.10.group_ref, bf16[2,512,384]{2,1,0:T(8,128)(2,1)S(1)} %copy-done.6, bf16[2,288,512]{2,1,0:T(8,128)(2,1)S(1)} %bitcast.129, bf16[2,320,512]{2,1,0:T(8,128)(2,1)S(1)} %bitcast.128), custom_call_target="tpu_custom_call" | custom-call | tf_op jit(solution)/shard_map/pack/pallas_call | solution.py:173
  14.1 2.5 collective-permute-start
  19.0 6.4 %collective-permute-done = bf16[128,1280]{1,0:T(8,128)(2,1)S(1)} collective-permute-done((bf16[128,1280]{1,0:T(8,128)(2,1)}, bf16[128,1280]{1,0:T(8,128)(2,1)S(1)}, u32[]{:S(2)}, u32[]{:S(2)}) %collective-permute-start) | collective-permute-done | bytes 327712 | tf_op jit(solution)/shard_map/ppermute | solution.py:53
  26.6 4.1 %collective-permute-start.10 = (bf16[128,992]{1,0:T(8,128)(2,1)S(1)}, bf16[128,992]{1,0:T(8,128)(2,1)S(1)}, u32[]{:S(2)}, u32[]{:S(2)}) collective-permute-start(bf16[128,992]{1,0:T(8,128)(2,1)S(1)} %bitcast.143), channel_id=1, source_target_pairs={{0,24},{4,28},{8,16},{12,20},{16,8},{20,12},{24,0},{28,4},{1,25},{... | collective-permute-start | bytes 761864 | tf_op jit(solution)/shard_map/ppermute | solution.py:53
  31.4 2.2 collective-permute-done.3
  38.0 1.5 collective-permute-start.5
  40.2 3.0 %collective-permute-done.8.refs_1_ = bf16[128,992]{1,0:T(8,128)(2,1)S(1)} collective-permute-done((bf16[128,992]{1,0:T(8,128)(2,1)S(1)}, bf16[128,992]{1,0:T(8,128)(2,1)S(1)}, u32[]{:S(2)}, u32[]{:S(2)}) %collective-permute-start.8) | collective-permute-done | bytes 253984 | tf_op jit(solution)/shard_map/ppermute | solution.py:53
  43.1 9.4 %collective-permute-done.9.refs_2_ = bf16[128,992]{1,0:T(8,128)(2,1)S(1)} collective-permute-done((bf16[128,992]{1,0:T(8,128)(2,1)S(1)}, bf16[128,992]{1,0:T(8,128)(2,1)S(1)}, u32[]{:S(2)}, u32[]{:S(2)}) %collective-permute-start.9) | collective-permute-done | bytes 253984 | tf_op jit(solution)/shard_map/ppermute | solution.py:53
  53.2 2.5 collective-permute-start.13
  56.8 1.8 multiply_convert_fusion.3
  59.6 1.8 multiply_convert_fusion.2
  61.7 1.6 collective-permute-start.7
  63.2 1.6 collective-permute-start.15
  65.9 1.7 multiply_convert_fusion.1
  67.6 8.0 %collective-permute-done.7 = bf16[256,768]{1,0:T(8,128)(2,1)S(1)} collective-permute-done((bf16[256,768]{1,0:T(8,128)(2,1)S(1)}, bf16[256,768]{1,0:T(8,128)(2,1)S(1)}, u32[]{:S(2)}, u32[]{:S(2)}) %collective-permute-start.7) | collective-permute-done | bytes 393248 | tf_op jit(solution)/shard_map/ppermute | solution.py:53
  79.4 1.6 collective-permute-start.25
  81.1 12.2 %collective-permute-done.16.refs_7_ = bf16[128,768]{1,0:T(8,128)(2,1)S(1)} collective-permute-done((bf16[128,768]{1,0:T(8,128)(2,1)S(1)}, bf16[128,768]{1,0:T(8,128)(2,1)S(1)}, u32[]{:S(2)}, u32[]{:S(2)}) %collective-permute-start.16) | collective-permute-done | bytes 196640 | tf_op jit(solution)/shard_map/ppermute | solution.py:53
  93.7 1.6 collective-permute-start.17
  96.9 1.6 collective-permute-start.22
  102.6 5.9 %collective-permute-done.22.refs_5_ = bf16[128,1152]{1,0:T(8,128)(2,1)S(1)} collective-permute-done((bf16[128,1152]{1,0:T(8,128)(2,1)S(1)}, bf16[128,1152]{1,0:T(8,128)(2,1)S(1)}, u32[]{:S(2)}, u32[]{:S(2)}) %collective-permute-start.22) | collective-permute-done | bytes 294944 | tf_op jit(solution)/shard_map/ppermute | solution.py:53
  112.1 1.7 collective-permute-start.27
  113.8 5.1 %collective-permute-done.23 = bf16[128,1152]{1,0:T(8,128)(2,1)S(1)} collective-permute-done((bf16[128,1152]{1,0:T(8,128)(2,1)S(1)}, bf16[128,1152]{1,0:T(8,128)(2,1)S(1)}, u32[]{:S(2)}, u32[]{:S(2)}) %collective-permute-start.23) | collective-permute-done | bytes 294944 | tf_op jit(solution)/shard_map/ppermute | solution.py:53
  119.4 5.1 %collective-permute-done.20 = bf16[256,768]{1,0:T(8,128)(2,1)S(1)} collective-permute-done((bf16[256,768]{1,0:T(8,128)(2,1)S(1)}, bf16[256,768]{1,0:T(8,128)(2,1)S(1)}, u32[]{:S(2)}, u32[]{:S(2)}) %collective-permute-start.20) | collective-permute-done | bytes 393248 | tf_op jit(solution)/shard_map/ppermute | solution.py:53
  127.6 2.6 collective-permute-done.27
  131.8 7.8 %collective-permute-done.24 = bf16[256,1152]{1,0:T(8,128)(2,1)} collective-permute-done((bf16[256,1152]{1,0:T(8,128)(2,1)S(1)}, bf16[256,1152]{1,0:T(8,128)(2,1)}, u32[]{:S(2)}, u32[]{:S(2)}) %collective-permute-start.24) | collective-permute-done | bytes 589856 | tf_op jit(solution)/shard_map/ppermute | solution.py:53
  140.8 2.3 product.4
  143.1 2.4 fusion.14.refs_2_
  150.0 4.2 %product.5 = (bf16[4,160,1280]{2,1,0:T(8,128)(2,1)S(1)}, bf16[4,160,1280]{2,1,0:T(8,128)(2,1)}) custom-call(s32[2]{0:T(128)S(1)} %pad_add_fusion.spot_ref, bf16[512,1280]{1,0:T(8,128)(2,1)S(1)} %pad_maximum_fusion.1.refs_0_, bf16[512,320]{1,0:T(8,128)(2,1)S(1)} %fusion.13.refs_1_, bf16[512,320]{1,0:T(8,128)(2,1)S(1)} %fusion.14.refs_2_, ...), custom_call_target="tpu_custom_call" | custom-call | tf_op jit(solution)/shard_map/product/pallas_call | solution.py:269
  155.5 1.6 collective-permute-start.34
  157.1 1.6 collective-permute-start.33
  158.7 7.1 %collective-permute-done.30 = bf16[128,1280]{1,0:T(8,128)(2,1)S(1)} collective-permute-done((bf16[128,1280]{1,0:T(8,128)(2,1)S(1)}, bf16[128,1280]{1,0:T(8,128)(2,1)S(1)}, u32[]{:S(2)}, u32[]{:S(2)}) %collective-permute-start.30) | collective-permute-done | bytes 327712 | tf_op jit(solution)/shard_map/ppermute | solution.py:53
  165.8 2.4 collective-permute-done.31
  169.0 2.9 %collective-permute-done.34 = bf16[128,1280]{1,0:T(8,128)(2,1)S(1)} collective-permute-done((bf16[128,1280]{1,0:T(8,128)(2,1)S(1)}, bf16[128,1280]{1,0:T(8,128)(2,1)S(1)}, u32[]{:S(2)}, u32[]{:S(2)}) %collective-permute-start.34) | collective-permute-done | bytes 327712 | tf_op jit(solution)/shard_map/ppermute | solution.py:53
  175.3 1.7 collective-permute-start.36
  177.4 8.1 %collective-permute-done.37 = bf16[128,1280]{1,0:T(8,128)(2,1)S(1)} collective-permute-done((bf16[128,1280]{1,0:T(8,128)(2,1)S(1)}, bf16[128,1280]{1,0:T(8,128)(2,1)S(1)}, u32[]{:S(2)}, u32[]{:S(2)}) %collective-permute-start.37) | collective-permute-done | bytes 327712 | tf_op jit(solution)/shard_map/ppermute | solution.py:53
  185.5 2.5 collective-permute-done.38
  189.4 2.5 product.6
  192.9 1.7 collective-permute-start.44
  194.9 1.6 collective-permute-start.45
  196.5 3.5 %fusion.2.refs_1_ = bf16[512,1280]{1,0:T(8,128)(2,1)S(1)} fusion(bf16[1280,1280]{1,0:T(8,128)(2,1)S(1)} %copy-done.26, f32[512,1280]{1,0:T(8,128)S(1)} %copy-done.29, bf16[128,1280]{1,0:T(8,128)(2,1)S(1)} %collective-permute-done.37, bf16[128,1280]{1,0:T(8,128)(2,1)S(1)} %collective-permute-done.36, bf16[128,1280]{1,0:T(8,128)(2,1)S(1)} %collective-permute-done.35, ...), kind=kOutput, calls=%fused_computation.10 | convolution fusion | flops 1695416320 | bytes 8519680 | tf_op jit(solution)/shard_map/rd,fd->rf/dot_general | solution.py:505
  200.1 2.5 product.7
  208.0 30.3 %collective-permute-done.42.came_ref = bf16[2,160,1280]{2,1,0:T(8,128)(2,1)S(1)} collective-permute-done((bf16[2,160,1280]{2,1,0:T(8,128)(2,1)S(1)}, bf16[2,160,1280]{2,1,0:T(8,128)(2,1)S(1)}, u32[]{:S(2)}, u32[]{:S(2)}) %collective-permute-start.42) | collective-permute-done | bytes 819232 | tf_op jit(solution)/shard_map/ppermute | solution.py:53
  238.6 25.7 %collective-permute-done.41.came_ref = bf16[2,160,1280]{2,1,0:T(8,128)(2,1)S(1)} collective-permute-done((bf16[2,160,1280]{2,1,0:T(8,128)(2,1)S(1)}, bf16[2,160,1280]{2,1,0:T(8,128)(2,1)S(1)}, u32[]{:S(2)}, u32[]{:S(2)}) %collective-permute-start.41) | collective-permute-done | bytes 819232 | tf_op jit(solution)/shard_map/ppermute | solution.py:53
  266.2 2.4 finish.1
  269.5 15.5 %collective-permute-done.46 = bf16[1,160,1280]{2,1,0:T(8,128)(2,1)S(1)} collective-permute-done((bf16[1,160,1280]{2,1,0:T(8,128)(2,1)S(1)}, bf16[1,160,1280]{2,1,0:T(8,128)(2,1)S(1)}, u32[]{:S(2)}, u32[]{:S(2)}) %collective-permute-start.46) | collective-permute-done | bytes 409632 | tf_op jit(solution)/shard_map/ppermute | solution.py:53
  (205 shorter events, 58.2 us)
Async XLA Ops:
  12.6 12.8 %collective-permute-start.1 = (bf16[256,992]{1,0:T(8,128)(2,1)S(1)}, bf16[256,992]{1,0:T(8,128)(2,1)}, u32[]{:S(2)}, u32[]{:S(2)}) collective-permute-start(bf16[256,992]{1,0:T(8,128)(2,1)S(1)} %get-tuple-element.62), channel_id=1, source_target_pairs={{0,4},{4,0},{8,12},{12,8},{16,20},{20,16},{24,28},{28,24},{1,5},{5... | collective-permute-start | bytes 1523720 | tf_op jit(solution)/shard_map/ppermute | solution.py:53
  14.1 11.3 %collective-permute-start = (bf16[128,1280]{1,0:T(8,128)(2,1)}, bf16[128,1280]{1,0:T(8,128)(2,1)S(1)}, u32[]{:S(2)}, u32[]{:S(2)}) collective-permute-start(bf16[128,1280]{1,0:T(8,128)(2,1)} %get-tuple-element.136), channel_id=1, source_target_pairs={{0,1},{1,0},{2,3},{3,2},{4,5},{5,4},{6,7},{7,6},{8,9},{9,8},{10,11... | collective-permute-start | bytes 983048 | tf_op jit(solution)/shard_map/ppermute | solution.py:53
  16.6 16.9 %collective-permute-start.3 = (bf16[128,1280]{1,0:T(8,128)(2,1)}, bf16[128,1280]{1,0:T(8,128)(2,1)S(1)}, u32[]{:S(2)}, u32[]{:S(2)}) collective-permute-start(bf16[128,1280]{1,0:T(8,128)(2,1)} %get-tuple-element.137), channel_id=1, source_target_pairs={{0,3},{1,2},{2,1},{3,0},{4,7},{5,6},{6,5},{7,4},{8,11},{9,10},{10,... | collective-permute-start | bytes 983048 | tf_op jit(solution)/shard_map/ppermute | solution.py:53
  18.1 16.6 %collective-permute-start.2 = (bf16[128,1280]{1,0:T(8,128)(2,1)S(1)}, bf16[128,1280]{1,0:T(8,128)(2,1)S(1)}, u32[]{:S(2)}, u32[]{:S(2)}) collective-permute-start(bf16[128,1280]{1,0:T(8,128)(2,1)S(1)} %get-tuple-element.138), channel_id=1, source_target_pairs={{0,2},{1,3},{2,0},{3,1},{4,6},{5,7},{6,4},{7,5},{8,10},{9,11},{10,... | collective-permute-start | bytes 983048 | tf_op jit(solution)/shard_map/ppermute | solution.py:53
  26.6 12.9 %collective-permute-start.10 = (bf16[128,992]{1,0:T(8,128)(2,1)S(1)}, bf16[128,992]{1,0:T(8,128)(2,1)S(1)}, u32[]{:S(2)}, u32[]{:S(2)}) collective-permute-start(bf16[128,992]{1,0:T(8,128)(2,1)S(1)} %bitcast.143), channel_id=1, source_target_pairs={{0,24},{4,28},{8,16},{12,20},{16,8},{20,12},{24,0},{28,4},{1,25},{... | collective-permute-start | bytes 761864 | tf_op jit(solution)/shard_map/ppermute | solution.py:53
  30.7 12.4 %collective-permute-start.8 = (bf16[128,992]{1,0:T(8,128)(2,1)S(1)}, bf16[128,992]{1,0:T(8,128)(2,1)S(1)}, u32[]{:S(2)}, u32[]{:S(2)}) collective-permute-start(bf16[128,992]{1,0:T(8,128)(2,1)S(1)} %bitcast.142), channel_id=1, source_target_pairs={{0,8},{4,12},{8,0},{12,4},{16,24},{20,28},{24,16},{28,20},{1,9},{5... | collective-permute-start | bytes 761864 | tf_op jit(solution)/shard_map/ppermute | solution.py:53
  30.7 21.8 %collective-permute-start.9 = (bf16[128,992]{1,0:T(8,128)(2,1)S(1)}, bf16[128,992]{1,0:T(8,128)(2,1)S(1)}, u32[]{:S(2)}, u32[]{:S(2)}) collective-permute-start(bf16[128,992]{1,0:T(8,128)(2,1)S(1)} %bitcast.141), channel_id=1, source_target_pairs={{0,16},{4,20},{8,24},{12,28},{16,0},{20,4},{24,8},{28,12},{1,17},{... | collective-permute-start | bytes 761864 | tf_op jit(solution)/shard_map/ppermute | solution.py:53
  36.5 19.8 %collective-permute-start.6 = (bf16[128,1280]{1,0:T(8,128)(2,1)S(1)}, bf16[128,1280]{1,0:T(8,128)(2,1)S(1)}, u32[]{:S(2)}, u32[]{:S(2)}) collective-permute-start(bf16[128,1280]{1,0:T(8,128)(2,1)S(1)} %multiply_convert_fusion.5), channel_id=1, source_target_pairs={{0,3},{1,2},{2,1},{3,0},{4,7},{5,6},{6,5},{7,4},{8,11},{9,10},{10,... | collective-permute-start | bytes 983048 | tf_op jit(solution)/shard_map/ppermute | solution.py:53
  38.0 18.8 %collective-permute-start.5 = (bf16[128,1280]{1,0:T(8,128)(2,1)S(1)}, bf16[128,1280]{1,0:T(8,128)(2,1)S(1)}, u32[]{:S(2)}, u32[]{:S(2)}) collective-permute-start(bf16[128,1280]{1,0:T(8,128)(2,1)S(1)} %multiply_convert_fusion.5), channel_id=1, source_target_pairs={{0,2},{1,3},{2,0},{3,1},{4,6},{5,7},{6,4},{7,5},{8,10},{9,11},{10,... | collective-permute-start | bytes 983048 | tf_op jit(solution)/shard_map/ppermute | solution.py:53
  39.5 17.3 %collective-permute-start.4 = (bf16[128,1280]{1,0:T(8,128)(2,1)S(1)}, bf16[128,1280]{1,0:T(8,128)(2,1)S(1)}, u32[]{:S(2)}, u32[]{:S(2)}) collective-permute-start(bf16[128,1280]{1,0:T(8,128)(2,1)S(1)} %multiply_convert_fusion.5), channel_id=1, source_target_pairs={{0,1},{1,0},{2,3},{3,2},{4,5},{5,4},{6,7},{7,6},{8,9},{9,8},{10,11... | collective-permute-start | bytes 983048 | tf_op jit(solution)/shard_map/ppermute | solution.py:53
  53.2 24.7 %collective-permute-start.13 = (bf16[128,992]{1,0:T(8,128)(2,1)S(1)}, bf16[128,992]{1,0:T(8,128)(2,1)S(1)}, u32[]{:S(2)}, u32[]{:S(2)}) collective-permute-start(bf16[128,992]{1,0:T(8,128)(2,1)S(1)} %get-tuple-element.145), channel_id=1, source_target_pairs={{0,3},{1,2},{2,1},{3,0},{4,7},{5,6},{6,5},{7,4},{8,11},{9,10},{10,... | collective-permute-start | bytes 761864 | tf_op jit(solution)/shard_map/ppermute | solution.py:53
  55.7 23.7 %collective-permute-start.12 = (bf16[128,992]{1,0:T(8,128)(2,1)S(1)}, bf16[128,992]{1,0:T(8,128)(2,1)S(1)}, u32[]{:S(2)}, u32[]{:S(2)}) collective-permute-start(bf16[128,992]{1,0:T(8,128)(2,1)S(1)} %get-tuple-element.146), channel_id=1, source_target_pairs={{0,2},{1,3},{2,0},{3,1},{4,6},{5,7},{6,4},{7,5},{8,10},{9,11},{10,... | collective-permute-start | bytes 761864 | tf_op jit(solution)/shard_map/ppermute | solution.py:53
  56.2 24.8 %collective-permute-start.11 = (bf16[128,992]{1,0:T(8,128)(2,1)S(1)}, bf16[128,992]{1,0:T(8,128)(2,1)S(1)}, u32[]{:S(2)}, u32[]{:S(2)}) collective-permute-start(bf16[128,992]{1,0:T(8,128)(2,1)S(1)} %get-tuple-element.147), channel_id=1, source_target_pairs={{0,1},{1,0},{2,3},{3,2},{4,5},{5,4},{6,7},{7,6},{8,9},{9,8},{10,11... | collective-permute-start | bytes 761864 | tf_op jit(solution)/shard_map/ppermute | solution.py:53
  61.7 14.0 %collective-permute-start.7 = (bf16[256,768]{1,0:T(8,128)(2,1)S(1)}, bf16[256,768]{1,0:T(8,128)(2,1)S(1)}, u32[]{:S(2)}, u32[]{:S(2)}) collective-permute-start(bf16[256,768]{1,0:T(8,128)(2,1)S(1)} %pad_maximum_fusion.10), channel_id=1, source_target_pairs={{0,1},{1,0},{2,3},{3,2},{4,5},{5,4},{6,7},{7,6},{8,9},{9,8},{10,11... | collective-permute-start | bytes 1179656 | tf_op jit(solution)/shard_map/ppermute | solution.py:53
  63.2 13.9 %collective-permute-start.15 = (bf16[256,768]{1,0:T(8,128)(2,1)S(1)}, bf16[256,768]{1,0:T(8,128)(2,1)S(1)}, u32[]{:S(2)}, u32[]{:S(2)}) collective-permute-start(bf16[256,768]{1,0:T(8,128)(2,1)S(1)} %pad_maximum_fusion.11), channel_id=1, source_target_pairs={{0,2},{1,3},{2,0},{3,1},{4,6},{5,7},{6,4},{7,5},{8,10},{9,11},{10,... | collective-permute-start | bytes 1179656 | tf_op jit(solution)/shard_map/ppermute | solution.py:53
  75.6 20.2 %collective-permute-start.21 = (bf16[256,1152]{1,0:T(8,128)(2,1)S(1)}, bf16[256,1152]{1,0:T(8,128)(2,1)}, u32[]{:S(2)}, u32[]{:S(2)}) collective-permute-start(bf16[256,1152]{1,0:T(8,128)(2,1)S(1)} %pad_maximum_fusion.8), channel_id=1, source_target_pairs={{0,1},{1,0},{2,3},{3,2},{4,5},{5,4},{6,7},{7,6},{8,9},{9,8},{10,11... | collective-permute-start | bytes 1769480 | tf_op jit(solution)/shard_map/ppermute | solution.py:53
  77.4 15.9 %collective-permute-start.16 = (bf16[128,768]{1,0:T(8,128)(2,1)S(1)}, bf16[128,768]{1,0:T(8,128)(2,1)S(1)}, u32[]{:S(2)}, u32[]{:S(2)}) collective-permute-start(bf16[128,768]{1,0:T(8,128)(2,1)S(1)} %get-tuple-element.119), channel_id=1, source_target_pairs={{0,1},{1,0},{2,3},{3,2},{4,5},{5,4},{6,7},{7,6},{8,9},{9,8},{10,11... | collective-permute-start | bytes 589832 | tf_op jit(solution)/shard_map/ppermute | solution.py:53
  78.0 15.3 %collective-permute-start.14 = (bf16[128,768]{1,0:T(8,128)(2,1)S(1)}, bf16[128,768]{1,0:T(8,128)(2,1)S(1)}, u32[]{:S(2)}, u32[]{:S(2)}) collective-permute-start(bf16[128,768]{1,0:T(8,128)(2,1)S(1)} %get-tuple-element.126), channel_id=1, source_target_pairs={{0,2},{1,3},{2,0},{3,1},{4,6},{5,7},{6,4},{7,5},{8,10},{9,11},{10,... | collective-permute-start | bytes 589832 | tf_op jit(solution)/shard_map/ppermute | solution.py:53
  79.4 20.5 %collective-permute-start.25 = (bf16[256,1280]{1,0:T(8,128)(2,1)S(1)}, bf16[256,1280]{1,0:T(8,128)(2,1)}, u32[]{:S(2)}, u32[]{:S(2)}) collective-permute-start(bf16[256,1280]{1,0:T(8,128)(2,1)S(1)} %slice.314), channel_id=1, source_target_pairs={{0,2},{1,3},{2,0},{3,1},{4,6},{5,7},{6,4},{7,5},{8,10},{9,11},{10,... | collective-permute-start | bytes 1966088 | tf_op jit(solution)/shard_map/ppermute | solution.py:53
  93.7 17.4 %collective-permute-start.17 = (bf16[128,768]{1,0:T(8,128)(2,1)S(1)}, bf16[128,768]{1,0:T(8,128)(2,1)S(1)}, u32[]{:S(2)}, u32[]{:S(2)}) collective-permute-start(bf16[128,768]{1,0:T(8,128)(2,1)S(1)} %get-tuple-element.69), channel_id=1, source_target_pairs={{0,1},{1,0},{2,3},{3,2},{4,5},{5,4},{6,7},{7,6},{8,9},{9,8},{10,11... | collective-permute-start | bytes 589832 | tf_op jit(solution)/shard_map/ppermute | solution.py:53
  95.3 14.3 %collective-permute-start.19 = (bf16[128,768]{1,0:T(8,128)(2,1)S(1)}, bf16[128,768]{1,0:T(8,128)(2,1)S(1)}, u32[]{:S(2)}, u32[]{:S(2)}) collective-permute-start(bf16[128,768]{1,0:T(8,128)(2,1)S(1)} %get-tuple-element.70), channel_id=1, source_target_pairs={{0,2},{1,3},{2,0},{3,1},{4,6},{5,7},{6,4},{7,5},{8,10},{9,11},{10,... | collective-permute-start | bytes 589832 | tf_op jit(solution)/shard_map/ppermute | solution.py:53
  96.9 11.5 %collective-permute-start.22 = (bf16[128,1152]{1,0:T(8,128)(2,1)S(1)}, bf16[128,1152]{1,0:T(8,128)(2,1)S(1)}, u32[]{:S(2)}, u32[]{:S(2)}) collective-permute-start(bf16[128,1152]{1,0:T(8,128)(2,1)S(1)} %get-tuple-element.127), channel_id=1, source_target_pairs={{0,2},{1,3},{2,0},{3,1},{4,6},{5,7},{6,4},{7,5},{8,10},{9,11},{10,... | collective-permute-start | bytes 884744 | tf_op jit(solution)/shard_map/ppermute | solution.py:53
  101.1 10.5 %collective-permute-start.26 = (bf16[128,1280]{1,0:T(8,128)(2,1)S(1)}, bf16[128,1280]{1,0:T(8,128)(2,1)S(1)}, u32[]{:S(2)}, u32[]{:S(2)}) collective-permute-start(bf16[128,1280]{1,0:T(8,128)(2,1)S(1)} %get-tuple-element.123), channel_id=1, source_target_pairs={{0,1},{1,0},{2,3},{3,2},{4,5},{5,4},{6,7},{7,6},{8,9},{9,8},{10,11... | collective-permute-start | bytes 983048 | tf_op jit(solution)/shard_map/ppermute | solution.py:53
  108.9 10.0 %collective-permute-start.23 = (bf16[128,1152]{1,0:T(8,128)(2,1)S(1)}, bf16[128,1152]{1,0:T(8,128)(2,1)S(1)}, u32[]{:S(2)}, u32[]{:S(2)}) collective-permute-start(bf16[128,1152]{1,0:T(8,128)(2,1)S(1)} %loss.4), channel_id=1, source_target_pairs={{0,1},{1,0},{2,3},{3,2},{4,5},{5,4},{6,7},{7,6},{8,9},{9,8},{10,11... | collective-permute-start | bytes 884744 | tf_op jit(solution)/shard_map/ppermute | solution.py:53
  109.7 14.8 %collective-permute-start.20 = (bf16[256,768]{1,0:T(8,128)(2,1)S(1)}, bf16[256,768]{1,0:T(8,128)(2,1)S(1)}, u32[]{:S(2)}, u32[]{:S(2)}) collective-permute-start(bf16[256,768]{1,0:T(8,128)(2,1)S(1)} %pad_maximum_fusion.13), channel_id=1, source_target_pairs={{0,1},{1,0},{2,3},{3,2},{4,5},{5,4},{6,7},{7,6},{8,9},{9,8},{10,11... | collective-permute-start | bytes 1179656 | tf_op jit(solution)/shard_map/ppermute | solution.py:53
  111.1 13.4 %collective-permute-start.18 = (bf16[256,768]{1,0:T(8,128)(2,1)S(1)}, bf16[256,768]{1,0:T(8,128)(2,1)S(1)}, u32[]{:S(2)}, u32[]{:S(2)}) collective-permute-start(bf16[256,768]{1,0:T(8,128)(2,1)S(1)} %pad_maximum_fusion.12), channel_id=1, source_target_pairs={{0,2},{1,3},{2,0},{3,1},{4,6},{5,7},{6,4},{7,5},{8,10},{9,11},{10,... | collective-permute-start | bytes 1179656 | tf_op jit(solution)/shard_map/ppermute | solution.py:53
  112.1 18.2 %collective-permute-start.27 = (bf16[128,1280]{1,0:T(8,128)(2,1)S(1)}, bf16[128,1280]{1,0:T(8,128)(2,1)S(1)}, u32[]{:S(2)}, u32[]{:S(2)}) collective-permute-start(bf16[128,1280]{1,0:T(8,128)(2,1)S(1)} %loss.5), channel_id=1, source_target_pairs={{0,2},{1,3},{2,0},{3,1},{4,6},{5,7},{6,4},{7,5},{8,10},{9,11},{10,... | collective-permute-start | bytes 983048 | tf_op jit(solution)/shard_map/ppermute | solution.py:53
  119.0 20.6 %collective-permute-start.24 = (bf16[256,1152]{1,0:T(8,128)(2,1)S(1)}, bf16[256,1152]{1,0:T(8,128)(2,1)}, u32[]{:S(2)}, u32[]{:S(2)}) collective-permute-start(bf16[256,1152]{1,0:T(8,128)(2,1)S(1)} %pad_maximum_fusion.9), channel_id=1, source_target_pairs={{0,2},{1,3},{2,0},{3,1},{4,6},{5,7},{6,4},{7,5},{8,10},{9,11},{10,... | collective-permute-start | bytes 1769480 | tf_op jit(solution)/shard_map/ppermute | solution.py:53
  131.1 15.3 %collective-permute-start.28 = (bf16[256,1280]{1,0:T(8,128)(2,1)}, bf16[256,1280]{1,0:T(8,128)(2,1)}, u32[]{:S(2)}, u32[]{:S(2)}) collective-permute-start(bf16[256,1280]{1,0:T(8,128)(2,1)} %pad_maximum_fusion.7), channel_id=1, source_target_pairs={{0,1},{1,0},{2,3},{3,2},{4,5},{5,4},{6,7},{7,6},{8,9},{9,8},{10,11... | collective-permute-start | bytes 1966088 | tf_op jit(solution)/shard_map/ppermute | solution.py:53
  143.0 4.7 %collective-permute-start.29 = (bf16[4,192,640]{2,1,0:T(8,128)(2,1)S(1)}, bf16[4,192,640]{2,1,0:T(8,128)(2,1)S(1)}, u32[]{:S(2)}, u32[]{:S(2)}) collective-permute-start(bf16[4,192,640]{2,1,0:T(8,128)(2,1)S(1)} %get-tuple-element.74), channel_id=1, source_target_pairs={{0,4},{4,0},{8,12},{12,8},{16,20},{20,16},{24,28},{28,24},{1,5},{5... | collective-permute-start | bytes 2949128 | tf_op jit(solution)/shard_map/ppermute | solution.py:53
  154.2 14.0 %collective-permute-start.32 = (bf16[4,160,1280]{2,1,0:T(8,128)(2,1)}, bf16[4,160,1280]{2,1,0:T(8,128)(2,1)S(1)}, u32[]{:S(2)}, u32[]{:S(2)}) collective-permute-start(bf16[4,160,1280]{2,1,0:T(8,128)(2,1)} %get-tuple-element.82), channel_id=1, source_target_pairs={{0,4},{4,0},{8,12},{12,8},{16,20},{20,16},{24,28},{28,24},{1,5},{5... | collective-permute-start | bytes 4915208 | tf_op jit(solution)/shard_map/ppermute | solution.py:53
  155.0 13.2 %collective-permute-start.31 = (bf16[2,192,640]{2,1,0:T(8,128)(2,1)S(1)}, bf16[2,192,640]{2,1,0:T(8,128)(2,1)S(1)}, u32[]{:S(2)}, u32[]{:S(2)}) collective-permute-start(bf16[2,192,640]{2,1,0:T(8,128)(2,1)S(1)} %slice.315), channel_id=1, source_target_pairs={{0,8},{4,12},{8,0},{12,4},{16,24},{20,28},{24,16},{28,20},{1,9},{5... | collective-permute-start | bytes 1474568 | tf_op jit(solution)/shard_map/ppermute | solution.py:53
  155.1 10.6 %collective-permute-start.30 = (bf16[128,1280]{1,0:T(8,128)(2,1)S(1)}, bf16[128,1280]{1,0:T(8,128)(2,1)S(1)}, u32[]{:S(2)}, u32[]{:S(2)}) collective-permute-start(bf16[128,1280]{1,0:T(8,128)(2,1)S(1)} %get-tuple-element.133), channel_id=1, source_target_pairs={{0,1},{1,0},{2,3},{3,2},{4,5},{5,4},{6,7},{7,6},{8,9},{9,8},{10,11... | collective-permute-start | bytes 983048 | tf_op jit(solution)/shard_map/ppermute | solution.py:53
  155.5 16.3 %collective-permute-start.34 = (bf16[128,1280]{1,0:T(8,128)(2,1)S(1)}, bf16[128,1280]{1,0:T(8,128)(2,1)S(1)}, u32[]{:S(2)}, u32[]{:S(2)}) collective-permute-start(bf16[128,1280]{1,0:T(8,128)(2,1)S(1)} %get-tuple-element.134), channel_id=1, source_target_pairs={{0,3},{1,2},{2,1},{3,0},{4,7},{5,6},{6,5},{7,4},{8,11},{9,10},{10,... | collective-permute-start | bytes 983048 | tf_op jit(solution)/shard_map/ppermute | solution.py:53
  157.1 16.1 %collective-permute-start.33 = (bf16[128,1280]{1,0:T(8,128)(2,1)S(1)}, bf16[128,1280]{1,0:T(8,128)(2,1)S(1)}, u32[]{:S(2)}, u32[]{:S(2)}) collective-permute-start(bf16[128,1280]{1,0:T(8,128)(2,1)S(1)} %get-tuple-element.135), channel_id=1, source_target_pairs={{0,2},{1,3},{2,0},{3,1},{4,6},{5,7},{6,4},{7,5},{8,10},{9,11},{10,... | collective-permute-start | bytes 983048 | tf_op jit(solution)/shard_map/ppermute | solution.py:53
  168.6 19.4 %collective-permute-start.38 = (bf16[2,160,1280]{2,1,0:T(8,128)(2,1)S(1)}, bf16[2,160,1280]{2,1,0:T(8,128)(2,1)S(1)}, u32[]{:S(2)}, u32[]{:S(2)}) collective-permute-start(bf16[2,160,1280]{2,1,0:T(8,128)(2,1)S(1)} %slice.313), channel_id=1, source_target_pairs={{0,8},{4,12},{8,0},{12,4},{16,24},{20,28},{24,16},{28,20},{1,9},{5... | collective-permute-start | bytes 2457608 | tf_op jit(solution)/shard_map/ppermute | solution.py:53
  173.9 11.6 %collective-permute-start.37 = (bf16[128,1280]{1,0:T(8,128)(2,1)S(1)}, bf16[128,1280]{1,0:T(8,128)(2,1)S(1)}, u32[]{:S(2)}, u32[]{:S(2)}) collective-permute-start(bf16[128,1280]{1,0:T(8,128)(2,1)S(1)} %multiply_convert_fusion.4), channel_id=1, source_target_pairs={{0,3},{1,2},{2,1},{3,0},{4,7},{5,6},{6,5},{7,4},{8,11},{9,10},{10,... | collective-permute-start | bytes 983048 | tf_op jit(solution)/shard_map/ppermute | solution.py:53
  175.3 13.9 %collective-permute-start.36 = (bf16[128,1280]{1,0:T(8,128)(2,1)S(1)}, bf16[128,1280]{1,0:T(8,128)(2,1)S(1)}, u32[]{:S(2)}, u32[]{:S(2)}) collective-permute-start(bf16[128,1280]{1,0:T(8,128)(2,1)S(1)} %multiply_convert_fusion.4), channel_id=1, source_target_pairs={{0,2},{1,3},{2,0},{3,1},{4,6},{5,7},{6,4},{7,5},{8,10},{9,11},{10,... | collective-permute-start | bytes 983048 | tf_op jit(solution)/shard_map/ppermute | solution.py:53
  177.0 12.4 %collective-permute-start.35 = (bf16[128,1280]{1,0:T(8,128)(2,1)S(1)}, bf16[128,1280]{1,0:T(8,128)(2,1)S(1)}, u32[]{:S(2)}, u32[]{:S(2)}) collective-permute-start(bf16[128,1280]{1,0:T(8,128)(2,1)S(1)} %multiply_convert_fusion.4), channel_id=1, source_target_pairs={{0,1},{1,0},{2,3},{3,2},{4,5},{5,4},{6,7},{7,6},{8,9},{9,8},{10,11... | collective-permute-start | bytes 983048 | tf_op jit(solution)/shard_map/ppermute | solution.py:53
  192.0 8.1 %collective-permute-start.39 = (bf16[4,160,1280]{2,1,0:T(8,128)(2,1)S(1)}, bf16[4,160,1280]{2,1,0:T(8,128)(2,1)S(1)}, u32[]{:S(2)}, u32[]{:S(2)}) collective-permute-start(bf16[4,160,1280]{2,1,0:T(8,128)(2,1)S(1)} %get-tuple-element.87), channel_id=1, source_target_pairs={{0,4},{4,0},{8,12},{12,8},{16,20},{20,16},{24,28},{28,24},{1,5},{5... | collective-permute-start | bytes 4915208 | tf_op jit(solution)/shard_map/ppermute | solution.py:53
  192.9 71.5 %collective-permute-start.44 = (bf16[1,192,640]{2,1,0:T(8,128)(2,1)}, bf16[1,192,640]{2,1,0:T(8,128)(2,1)}, u32[]{:S(2)}, u32[]{:S(2)}) collective-permute-start(bf16[1,192,640]{2,1,0:T(8,128)(2,1)} %slice.317), channel_id=1, source_target_pairs={{0,16},{4,20},{8,24},{12,28},{16,0},{20,4},{24,8},{28,12},{1,17},{... | collective-permute-start | bytes 737288 | tf_op jit(solution)/shard_map/ppermute | solution.py:53
  194.9 69.5 %collective-permute-start.45 = (bf16[1,160,1280]{2,1,0:T(8,128)(2,1)S(1)}, bf16[1,160,1280]{2,1,0:T(8,128)(2,1)S(1)}, u32[]{:S(2)}, u32[]{:S(2)}) collective-permute-start(bf16[1,160,1280]{2,1,0:T(8,128)(2,1)S(1)} %slice.316), channel_id=1, source_target_pairs={{0,16},{4,20},{8,24},{12,28},{16,0},{20,4},{24,8},{28,12},{1,17},{... | collective-permute-start | bytes 1228808 | tf_op jit(solution)/shard_map/ppermute | solution.py:53
  202.6 3.6 %collective-permute-start.40 = (bf16[4,160,1280]{2,1,0:T(8,128)(2,1)S(1)}, bf16[4,160,1280]{2,1,0:T(8,128)(2,1)S(1)}, u32[]{:S(2)}, u32[]{:S(2)}) collective-permute-start(bf16[4,160,1280]{2,1,0:T(8,128)(2,1)S(1)} %get-tuple-element.90), channel_id=1, source_target_pairs={{0,4},{4,0},{8,12},{12,8},{16,20},{20,16},{24,28},{28,24},{1,5},{5... | collective-permute-start | bytes 4915208 | tf_op jit(solution)/shard_map/ppermute | solution.py:53
  204.2 34.1 %collective-permute-start.42 = (bf16[2,160,1280]{2,1,0:T(8,128)(2,1)S(1)}, bf16[2,160,1280]{2,1,0:T(8,128)(2,1)S(1)}, u32[]{:S(2)}, u32[]{:S(2)}) collective-permute-start(bf16[2,160,1280]{2,1,0:T(8,128)(2,1)S(1)} %get-tuple-element.97), channel_id=1, source_target_pairs={{0,8},{4,12},{8,0},{12,4},{16,24},{20,28},{24,16},{28,20},{1,9},{5... | collective-permute-start | bytes 2457608 | tf_op jit(solution)/shard_map/ppermute | solution.py:53
  206.2 32.2 %copy-start.14 = (f32[2,160,1280]{2,1,0:T(8,128)S(1)}, f32[2,160,1280]{2,1,0:T(8,128)}, u32[]{:S(2)}) copy-start(f32[2,160,1280]{2,1,0:T(8,128)} %copy-done.13) | copy-start | bytes 4915204
  206.5 57.8 %collective-permute-start.41 = (bf16[2,160,1280]{2,1,0:T(8,128)(2,1)S(1)}, bf16[2,160,1280]{2,1,0:T(8,128)(2,1)S(1)}, u32[]{:S(2)}, u32[]{:S(2)}) collective-permute-start(bf16[2,160,1280]{2,1,0:T(8,128)(2,1)S(1)} %get-tuple-element.92), channel_id=1, source_target_pairs={{0,8},{4,12},{8,0},{12,4},{16,24},{20,28},{24,16},{28,20},{1,9},{5... | collective-permute-start | bytes 2457608 | tf_op jit(solution)/shard_map/ppermute | solution.py:53
  238.5 26.7 %collective-permute-start.43 = (bf16[1,160,1280]{2,1,0:T(8,128)(2,1)S(1)}, bf16[1,160,1280]{2,1,0:T(8,128)(2,1)S(1)}, u32[]{:S(2)}, u32[]{:S(2)}) collective-permute-start(bf16[1,160,1280]{2,1,0:T(8,128)(2,1)S(1)} %get-tuple-element.98), channel_id=1, source_target_pairs={{0,16},{4,20},{8,24},{12,28},{16,0},{20,4},{24,8},{28,12},{1,17},{... | collective-permute-start | bytes 1228808 | tf_op jit(solution)/shard_map/ppermute | solution.py:53
  265.2 19.9 %collective-permute-start.46 = (bf16[1,160,1280]{2,1,0:T(8,128)(2,1)S(1)}, bf16[1,160,1280]{2,1,0:T(8,128)(2,1)S(1)}, u32[]{:S(2)}, u32[]{:S(2)}) collective-permute-start(bf16[1,160,1280]{2,1,0:T(8,128)(2,1)S(1)} %get-tuple-element.102), channel_id=1, source_target_pairs={{0,16},{4,20},{8,24},{12,28},{16,0},{20,4},{24,8},{28,12},{1,17},{... | collective-permute-start | bytes 1228808 | tf_op jit(solution)/shard_map/ppermute | solution.py:53
  (29 other events, 152.1 us)

commit v2 on v1

--- a/solution.py
+++ b/solution.py
@@ -259,7 +259,7 @@
             send_ref[at, :, columns] = jnp.where(side, even, odd).astype(jnp.bfloat16)
 
 
-def product(pairs, groups, group):
+def product(pairs, groups, group, flops=0):
     talls = [sum(left.shape[1] for left in lefts) for lefts, _ in pairs]
     wides = [sum(right.shape[1] for right in rights) for _, rights in pairs]
     tall, wide = max(talls) // groups, sum(wides)
@@ -272,8 +272,40 @@
         in_specs=[IN_SMEM] + [IN_VMEM] * len(flat),
         out_specs=(IN_VMEM, IN_VMEM),
         name="product",
-        **limits(),
+        **limits(flops),
     )(spot, *flat)
+
+
+def narrow_kernel(count, group_ref, active_ref, *refs):
+    out_ref = refs[-1]
+    columns = jnp.concatenate([ref[0] for ref in refs[:count]], axis=1)
+    term = jnp.dot(columns, active_ref[0], preferred_element_type=jnp.float32)
+
+    @pl.when(pl.program_id(0) == 0)
+    def _():
+        out_ref[...] = term
+
+    @pl.when(pl.program_id(0) != 0)
+    def _():
+        out_ref[...] += term
+
+
+def narrow_sum(group, actives, columns):
+    groups, rows, units = actives.shape
+    cut = columns[0].shape[1]
+    return pl.pallas_call(
+        functools.partial(narrow_kernel, len(columns)),
+        out_shape=jax.ShapeDtypeStruct((cut, units), jnp.float32),
+        grid_spec=pltpu.PrefetchScalarGridSpec(
+            num_scalar_prefetch=1,
+            grid=(groups,),
+            in_specs=[pl.BlockSpec((1, rows, units), lambda o, g: (o ^ g[0], 0, 0))]
+            + [pl.BlockSpec((1, cut, column.shape[2]), lambda o, g: (o, 0, 0)) for column in columns],
+            out_specs=pl.BlockSpec((cut, units), lambda o, g: (0, 0)),
+        ),
+        name="narrow",
+        **limits(2**35),
+    )(group.reshape(1), actives, *columns)
 
 
 def pin(*values):
@@ -433,9 +465,11 @@
 
     final_rows, normal_rows, inverse_rows = normalize(hidden, final_gain)
     final = gather(final_rows.astype(jnp.bfloat16), "mp")
+    final, late, own = pin(final, active, owned[:block])
+    actives = lax.all_gather(late, "dp")
 
     owned = owned.reshape(members, block, -1)
-    parts = [owned[0]] + [swap(owned[j], "mp", j) for j in range(1, members)]
+    parts = [own] + [swap(owned[j], "mp", j) for j in range(1, members)]
 
     ways = ((True, False), (True,), (False,))
     befores, lifteds, students = [], [], []
@@ -497,40 +531,49 @@
     through_rows = normalize_back(total, final_gain, normal_rows, inverse_rows)
     through_rows = through_rows.astype(jnp.bfloat16)
     came = [swap(through_rows, "mp", j) for j in range(1, members)]
-    came[-1], one = pin(came[-1], of_rest[1])
+    turned = through_rows.T.reshape(groups, -1, block)
+    turned = [lax.dynamic_index_in_dim(turned, group ^ o, 0) for o in range(groups)]
+    odd = swap(jnp.concatenate(turned[1::2], axis=0), "dp", 1)
+    came[-1], odd, one, actives = pin(came[-1], odd, of_rest[1], actives)
     of_rest = advance(arrive(of_rest, one))
     through = jnp.concatenate([through_rows, *came], axis=0)
-
-    of_narrow = begin(product([([through], [active])], groups, group))
+    both = [jnp.concatenate([turned[2 * o], odd[o : o + 1]]) for o in range(groups // 2)]
+    both = [both[0]] + [swap(both[o], "dp", 2 * o) for o in range(1, groups // 2)]
+
     back_two = jnp.einsum("rd,fd->rf", through, narrow_weight, **exact)
     inner_two = (back_two * smooth_slope(widened)).astype(jnp.bfloat16)
-    inner_two, one = pin(inner_two, of_narrow[1])
-    of_narrow = advance(arrive(of_narrow, one), True)
-    of_widen = advance(begin(product([([first], [inner_two])], groups, group)), True)
-    of_narrow = settle(of_narrow, True)
-    of_widen = settle(of_widen, True)
+    of_heads = settle(of_heads)
+    inner_two, one, two = pin(inner_two, of_heads[1], of_rest[0])
+    of_heads, of_rest = arrive(of_heads, one), (two, *of_rest[1:])
+    of_widen = begin(product([([first], [inner_two])], groups, group, 2**35))
+    of_widen = advance(of_widen, True)
+    keep, *both = pin(of_widen[0], *both)
+    of_widen = (keep, *of_widen[1:])
+    columns = jnp.concatenate(both, axis=0)
+    columns = [columns] + [swap(columns, "mp", j) for j in range(1, members)]
     of_heads, of_rest = settle(of_heads), settle(of_rest)
-    keep, *landed = pin(of_widen[0], of_narrow[1], of_heads[1], of_rest[1])
-    of_widen = (keep, *of_widen[1:])
-    of_narrow, of_heads, of_rest = [
-        arrive(state, one) for state, one in zip((of_narrow, of_heads, of_rest), landed)
-    ]
+    while of_widen[2]:
+        one, two, *columns[1:] = pin(of_widen[1], of_rest[1], *columns[1:])
+        of_widen, of_rest = arrive(of_widen, one), arrive(of_rest, two)
+        of_widen = advance(of_widen, True)
     wide = lifteds[0].shape[1]
     cuts = [head.shape[1] // groups for head in heads]
     deep = final.shape[1] // groups
     spans = [(k * wide, (k + 1) * wide) for k in range(4)]
     made = finish(
-        [of_heads, of_rest, of_narrow],
+        [of_heads, of_rest],
         [
             [(cuts[0], *spans[0]), (cuts[1], *spans[1])],
             [(deep, *span) for span in spans[:3]] + [(cuts[2], *spans[3])],
-            [(deep, 0, active.shape[1])],
         ],
     )
     head_grads = [made[0].T, made[1].T, made[5].T]
     grad_adaptor = jnp.stack(made[2:5])
-    grad_narrow = made[6].T
+    grad_narrow = narrow_sum(group, actives, columns).T
     keep, came, _ = of_widen
+    came, grad_narrow, grad_adaptor, *head_grads = pin(
+        came, grad_narrow, grad_adaptor, *head_grads
+    )
     grad_widen = (keep[0].astype(jnp.float32) + came[0].astype(jnp.float32)).T
     return (grad_widen, grad_narrow, grad_adaptor, *head_grads)
 

time: 287 us -> 280 us (0.976)
  waiting for transfers between devices: 168 us -> 120 us
  between operations: 1.54 us -> 15 us
  starting transfers between devices: 48.8 us -> 60.4 us
  matrix products: 24.6 us -> 32.2 us
  Pallas kernels: 20.4 us -> 25.3 us
  local copies, waits for them, and re-layouts: 9.1 us -> 12.6 us
    ppermute x47 -> x51, waiting for transfers between devices: 168 us -> 120 us  [swap(): return lax.ppermute(value, axis, [(i, i ^ offset) for i in range(count)])]
    ppermute x47 -> x51, starting transfers between devices: 48.8 us -> 60.3 us  [swap(): return lax.ppermute(value, axis, [(i, i ^ offset) for i in range(count)])]
    pallas_call x0 -> x1, Pallas kernels: none -> 8.94 us  [narrow_sum(): pl.pallas_call(functools.partial(narrow_kernel, len(columns)), out_shape=...]
    add x4, other arithmetic: 0.73 us -> 4.67 us  [advance(): held = keep.astype(jnp.float32) + came.astype(jnp.float32)]
    pallas_call x4 -> x3, Pallas kernels: 11.6 us -> 9.37 us  [product(): pl.pallas_call(functools.partial(product_kernel, groups, [(len(l), len(r)...]
  transfers between devices with their start and end apart: 47 -> 52, of which waited for: 25 -> 27; matrix products, arithmetic and copies ran while one was open for 11% -> 14% of each run, Pallas kernels for 4% -> 8%
where the time goes in v2:
time: 280 us; the launch traced here: 279 us
  waiting for transfers between devices  120 us (43%)
  starting transfers between devices  60.4 us (22%)
  matrix products  32.2 us (12%)
  Pallas kernels  25.3 us (9%)
  between operations  15 us (5%)
  other arithmetic  13.3 us (5%)
  local copies, waits for them, and re-layouts  12.6 us (4%)
    ppermute x51, waiting for transfers between devices, swap(): return lax.ppermute(value, axis, [(i, i ^ offset) for i in range(count)])  120 us
    ppermute x51, starting transfers between devices, swap(): return lax.ppermute(value, axis, [(i, i ^ offset) for i in range(count)])  60.3 us
    pallas_call x3, Pallas kernels, product(): pl.pallas_call(functools.partial(product_kernel, groups, [(len(l), len(r)...  9.37 us
    pallas_call x1, Pallas kernels, narrow_sum(): pl.pallas_call(functools.partial(narrow_kernel, len(columns)), out_shape=...  8.94 us
    dot_general x3, matrix products, local(): before = jnp.dot(final, adaptor_in[index], **exact)  6.45 us
    dot_general x1, matrix products, local(): back_two = jnp.einsum('rd,fd->rf', through, narrow_weight, **exact)  6.29 us
  transfers between devices with their start and end apart: 52, of which 27 were waited for; matrix products, arithmetic and copies ran while one was open for 14% of the time, Pallas kernels for 8%

profile of v2, /device:TPU:0, one launch (start us, length us, event | category | flops | bytes accessed | tf_op | source)
XLA Modules:
  0.0 279.0 jit_solution(656542064400747748)
XLA Ops:
  10.0 4.0 %multiply_convert_fusion = (bf16[512,1280]{1,0:T(8,128)(2,1)}, f32[512,1280]{1,0:T(8,128)}) fusion(bf16[512,1280]{1,0:T(8,128)(2,1)S(1)} %fusion.5.refs_0_, bf16[1280,1280]{1,0:T(8,128)(2,1)S(1)} %copy-done), kind=kOutput, calls=%fused_computation.19 | convolution fusion | flops 1683619840 | bytes 8519680 | tf_op jit(solution)/shard_map/dot_general | solution.py:439
  14.1 4.2 %fusion.78 = f32[512,1280]{1,0:T(8,128)S(1)} fusion(bf16[512,1280]{1,0:T(8,128)(2,1)} %get-tuple-element.99, bf16[1280,1280]{1,0:T(8,128)(2,1)} %param.17), kind=kOutput, calls=%fused_computation.192 | convolution fusion | flops 1677721600 | bytes 7208960 | tf_op jit(solution)/shard_map/dot_general | solution.py:441
  20.7 2.9 %collective-permute-start = (bf16[128,1280]{1,0:T(8,128)(2,1)}, bf16[128,1280]{1,0:T(8,128)(2,1)}, u32[]{:S(2)}, u32[]{:S(2)}) collective-permute-start(bf16[128,1280]{1,0:T(8,128)(2,1)} %get-tuple-element.158), channel_id=1, source_target_pairs={{0,1},{1,0},{2,3},{3,2},{4,5},{5,4},{6,7},{7,6},{8,9},{9,8},{10,11... | collective-permute-start | bytes 983048 | tf_op jit(solution)/shard_map/ppermute | solution.py:53
  23.6 3.5 %pack.1 = (bf16[256,992]{1,0:T(8,128)(2,1)S(1)}, bf16[256,992]{1,0:T(8,128)(2,1)S(1)}) custom-call(s32[3]{0:T(128)S(1)} %copy-done.8, s32[128]{0:T(128)S(1)} %copy-done.7, s32[1]{0:T(128)} %bitcast.10.group_ref, bf16[2,512,384]{2,1,0:T(8,128)(2,1)S(1)} %copy-done.4, bf16[2,288,512]{2,1,0:T(8,128)(2,1)S(1)} %bitcast.133, bf16[2,320,512]{2,1,0:T(8,128)(2,1)S(1)} %bitcast.132), custom_call_target="tpu_custom_call" | custom-call | tf_op jit(solution)/shard_map/pack/pallas_call | solution.py:173
  29.8 2.3 collective-permute-done
  33.7 2.6 collective-permute-start.8
  36.6 7.9 %collective-permute-done.2 = bf16[128,1280]{1,0:T(8,128)(2,1)S(1)} collective-permute-done((bf16[128,1280]{1,0:T(8,128)(2,1)}, bf16[128,1280]{1,0:T(8,128)(2,1)S(1)}, u32[]{:S(2)}, u32[]{:S(2)}) %collective-permute-start.2) | collective-permute-done | bytes 327712 | tf_op jit(solution)/shard_map/ppermute | solution.py:53
  46.8 1.8 collective-permute-start.5
  50.1 4.9 %collective-permute-done.8.refs_2_ = bf16[128,992]{1,0:T(8,128)(2,1)S(1)} collective-permute-done((bf16[128,992]{1,0:T(8,128)(2,1)S(1)}, bf16[128,992]{1,0:T(8,128)(2,1)S(1)}, u32[]{:S(2)}, u32[]{:S(2)}) %collective-permute-start.8) | collective-permute-done | bytes 253984 | tf_op jit(solution)/shard_map/ppermute | solution.py:53
  57.2 5.0 %collective-permute-done.5 = bf16[128,1280]{1,0:T(8,128)(2,1)S(1)} collective-permute-done((bf16[128,1280]{1,0:T(8,128)(2,1)S(1)}, bf16[128,1280]{1,0:T(8,128)(2,1)S(1)}, u32[]{:S(2)}, u32[]{:S(2)}) %collective-permute-start.5) | collective-permute-done | bytes 327712 | tf_op jit(solution)/shard_map/ppermute | solution.py:53
  62.2 1.6 collective-permute-done.6
  67.5 2.9 %multiply_convert_fusion.3 = (bf16[512,320]{1,0:T(8,128)(2,1)S(1)}, f32[512,320]{1,0:T(8,128)}) fusion(bf16[512,1280]{1,0:T(8,128)(2,1)S(1)} %pad_maximum_fusion.1.refs_0_, bf16[3,1280,320]{1,2,0:T(8,128)(2,1)} %param.19), kind=kOutput, calls=%fused_computation.86 | convolution fusion | flops 420904960 | bytes 3112960 | tf_op jit(solution)/shard_map/dot_general | solution.py:477
  72.3 1.8 multiply_convert_fusion.2
  76.0 1.6 collective-permute-start.15
  77.7 1.8 multiply_convert_fusion.1
  79.5 5.8 %collective-permute-done.10 = bf16[256,768]{1,0:T(8,128)(2,1)S(1)} collective-permute-done((bf16[256,768]{1,0:T(8,128)(2,1)S(1)}, bf16[256,768]{1,0:T(8,128)(2,1)S(1)}, u32[]{:S(2)}, u32[]{:S(2)}) %collective-permute-start.10) | collective-permute-done | bytes 393248 | tf_op jit(solution)/shard_map/ppermute | solution.py:53
  90.6 3.2 %collective-permute-done.14.refs_5_ = bf16[128,768]{1,0:T(8,128)(2,1)S(1)} collective-permute-done((bf16[128,768]{1,0:T(8,128)(2,1)S(1)}, bf16[128,768]{1,0:T(8,128)(2,1)S(1)}, u32[]{:S(2)}, u32[]{:S(2)}) %collective-permute-start.14) | collective-permute-done | bytes 196640 | tf_op jit(solution)/shard_map/ppermute | solution.py:53
  93.8 9.0 %collective-permute-done.16.refs_7_ = bf16[128,768]{1,0:T(8,128)(2,1)S(1)} collective-permute-done((bf16[128,768]{1,0:T(8,128)(2,1)S(1)}, bf16[128,768]{1,0:T(8,128)(2,1)S(1)}, u32[]{:S(2)}, u32[]{:S(2)}) %collective-permute-start.16) | collective-permute-done | bytes 196640 | tf_op jit(solution)/shard_map/ppermute | solution.py:53
  104.2 1.9 collective-permute-start.22
  106.9 1.9 collective-permute-start.26
  108.7 6.8 %collective-permute-done.22.refs_5_ = bf16[128,1152]{1,0:T(8,128)(2,1)S(1)} collective-permute-done((bf16[128,1152]{1,0:T(8,128)(2,1)S(1)}, bf16[128,1152]{1,0:T(8,128)(2,1)S(1)}, u32[]{:S(2)}, u32[]{:S(2)}) %collective-permute-start.22) | collective-permute-done | bytes 294944 | tf_op jit(solution)/shard_map/ppermute | solution.py:53
  120.9 5.1 %collective-permute-done.23 = bf16[128,1152]{1,0:T(8,128)(2,1)S(1)} collective-permute-done((bf16[128,1152]{1,0:T(8,128)(2,1)S(1)}, bf16[128,1152]{1,0:T(8,128)(2,1)S(1)}, u32[]{:S(2)}, u32[]{:S(2)}) %collective-permute-start.23) | collective-permute-done | bytes 294944 | tf_op jit(solution)/shard_map/ppermute | solution.py:53
  126.1 1.6 collective-permute-start.24
  127.7 1.7 collective-permute-done.18
  129.4 2.2 collective-permute-done.20
  133.3 2.0 fusion.28
  138.1 7.4 %collective-permute-done.24 = bf16[256,1152]{1,0:T(8,128)(2,1)S(1)} collective-permute-done((bf16[256,1152]{1,0:T(8,128)(2,1)S(1)}, bf16[256,1152]{1,0:T(8,128)(2,1)S(1)}, u32[]{:S(2)}, u32[]{:S(2)}) %collective-permute-start.24) | collective-permute-done | bytes 589856 | tf_op jit(solution)/shard_map/ppermute | solution.py:53
  145.7 2.5 product.3
  148.3 2.4 fusion.21.refs_2_
  155.6 4.3 %product.4 = (bf16[4,160,1280]{2,1,0:T(8,128)(2,1)S(1)}, bf16[4,160,1280]{2,1,0:T(8,128)(2,1)}) custom-call(s32[2]{0:T(128)S(1)} %pad_add_fusion.spot_ref, bf16[512,1280]{1,0:T(8,128)(2,1)S(1)} %pad_maximum_fusion.1.refs_0_, bf16[512,320]{1,0:T(8,128)(2,1)S(1)} %fusion.20.refs_1_, bf16[512,320]{1,0:T(8,128)(2,1)S(1)} %fusion.21.refs_2_, ...), custom_call_target="tpu_custom_call" | custom-call | tf_op jit(solution)/shard_map/product/pallas_call | solution.py:269
  167.9 7.1 %collective-permute-done.30 = bf16[128,1280]{1,0:T(8,128)(2,1)S(1)} collective-permute-done((bf16[128,1280]{1,0:T(8,128)(2,1)S(1)}, bf16[128,1280]{1,0:T(8,128)(2,1)S(1)}, u32[]{:S(2)}, u32[]{:S(2)}) %collective-permute-start.30) | collective-permute-done | bytes 327712 | tf_op jit(solution)/shard_map/ppermute | solution.py:53
  175.2 2.0 convert_add_fusion
  179.8 2.2 collective-permute-done.33
  188.6 2.4 collective-permute-start.40
  191.1 3.4 %collective-permute-done.37 = bf16[128,1280]{1,0:T(8,128)(2,1)} collective-permute-done((bf16[128,1280]{1,0:T(8,128)(2,1)S(1)}, bf16[128,1280]{1,0:T(8,128)(2,1)}, u32[]{:S(2)}, u32[]{:S(2)}) %collective-permute-start.37) | collective-permute-done | bytes 327712 | tf_op jit(solution)/shard_map/ppermute | solution.py:53
  194.4 8.7 %collective-permute-done.39 = bf16[2,160,1280]{2,1,0:T(8,128)(2,1)} collective-permute-done((bf16[2,160,1280]{2,1,0:T(8,128)(2,1)}, bf16[2,160,1280]{2,1,0:T(8,128)(2,1)}, u32[]{:S(2)}, u32[]{:S(2)}) %collective-permute-start.39) | collective-permute-done | bytes 819232 | tf_op jit(solution)/shard_map/ppermute | solution.py:53
  203.2 6.3 %fusion.2.refs_1_ = bf16[512,1280]{1,0:T(8,128)(2,1)S(1)} fusion(bf16[1280,1280]{1,0:T(8,128)(2,1)} %param.17, f32[512,1280]{1,0:T(8,128)} %get-tuple-element.192, bf16[128,1280]{1,0:T(8,128)(2,1)} %collective-permute-done.37, bf16[128,1280]{1,0:T(8,128)(2,1)} %collective-permute-done.36, bf16[128,1280]{1,0:T(8,128)(2,1)} %collective-permute-done.35, ...), kind=kOutput, calls=%fused_computation.10 | convolution fusion | flops 1695416320 | bytes 8519680 | tf_op jit(solution)/shard_map/rd,fd->rf/dot_general | solution.py:543
  211.0 2.5 product.5
  213.8 3.4 %collective-permute-start.44 = (bf16[2,160,128]{2,1,0:T(8,128)(2,1)S(1)}, bf16[2,160,128]{2,1,0:T(8,128)(2,1)S(1)}, u32[]{:S(2)}, u32[]{:S(2)}) collective-permute-start(bf16[2,160,128]{2,1,0:T(8,128)(2,1)S(1)} %pad_maximum_fusion.18), channel_id=1, source_target_pairs={{0,24},{4,28},{8,16},{12,20},{16,8},{20,12},{24,0},{28,4},{1,25},{... | collective-permute-start | bytes 245768 | tf_op jit(solution)/shard_map/ppermute | solution.py:53
  218.4 2.0 collective-permute-start.46
  220.7 2.0 collective-permute-start.45
  222.8 9.0 %collective-permute-done.43 = bf16[2,160,128]{2,1,0:T(8,128)(2,1)S(1)} collective-permute-done((bf16[2,160,128]{2,1,0:T(8,128)(2,1)S(1)}, bf16[2,160,128]{2,1,0:T(8,128)(2,1)S(1)}, u32[]{:S(2)}, u32[]{:S(2)}) %collective-permute-start.43) | collective-permute-done | bytes 81952 | tf_op jit(solution)/shard_map/ppermute | solution.py:53
  232.0 3.4 %collective-permute-start.49 = (bf16[8,160,128]{2,1,0:T(8,128)(2,1)S(1)}, bf16[8,160,128]{2,1,0:T(8,128)(2,1)S(1)}, u32[]{:S(2)}, u32[]{:S(2)}) collective-permute-start(bf16[8,160,128]{2,1,0:T(8,128)(2,1)S(1)} %constant_dynamic-update-slice_fusion.3.refs_0_), channel_id=1, source_target_pairs={{0,3},{1,2},{2,1},{3,0},{4,7},{5,6},{6,5},{7,4},{8,11},{9,10},{10,... | collective-permute-start | bytes 983048 | tf_op jit(solution)/shard_map/ppermute | solution.py:53
  235.5 6.2 %collective-permute-done.46.refs_3_ = bf16[1,160,1280]{2,1,0:T(8,128)(2,1)S(1)} collective-permute-done((bf16[1,160,1280]{2,1,0:T(8,128)(2,1)S(1)}, bf16[1,160,1280]{2,1,0:T(8,128)(2,1)S(1)}, u32[]{:S(2)}, u32[]{:S(2)}) %collective-permute-start.46) | collective-permute-done | bytes 409632 | tf_op jit(solution)/shard_map/ppermute | solution.py:53
  241.6 3.4 %collective-permute-done.48.refs_2_ = bf16[8,160,128]{2,1,0:T(8,128)(2,1)S(1)} collective-permute-done((bf16[8,160,128]{2,1,0:T(8,128)(2,1)S(1)}, bf16[8,160,128]{2,1,0:T(8,128)(2,1)S(1)}, u32[]{:S(2)}, u32[]{:S(2)}) %collective-permute-start.48) | collective-permute-done | bytes 327712 | tf_op jit(solution)/shard_map/ppermute | solution.py:53
  245.1 5.3 %collective-permute-done.45.came_ref = bf16[2,160,1280]{2,1,0:T(8,128)(2,1)S(1)} collective-permute-done((bf16[2,160,1280]{2,1,0:T(8,128)(2,1)S(1)}, bf16[2,160,1280]{2,1,0:T(8,128)(2,1)S(1)}, u32[]{:S(2)}, u32[]{:S(2)}) %collective-permute-start.45) | collective-permute-done | bytes 819232 | tf_op jit(solution)/shard_map/ppermute | solution.py:53
  252.4 8.9 %narrow.1 = f32[160,1280]{1,0:T(8,128)} custom-call(s32[1]{0:T(128)} %bitcast.10.group_ref, bf16[8,512,1280]{2,1,0:T(8,128)(2,1)} %bitcast.151, bf16[8,160,128]{2,1,0:T(8,128)(2,1)S(1)} %constant_dynamic-update-slice_fusion.3.refs_0_, bf16[8,160,128]{2,1,0:T(8,128)(2,1)S(1)} %collective-permute-done.47.refs_1_, ...), custom_call_target="tpu_custom_call" | custom-call | flops 34359738368 | tf_op jit(solution)/shard_map/narrow/pallas_call | solution.py:296
  262.2 8.9 %collective-permute-done.50 = bf16[1,160,1280]{2,1,0:T(8,128)(2,1)S(1)} collective-permute-done((bf16[1,160,1280]{2,1,0:T(8,128)(2,1)S(1)}, bf16[1,160,1280]{2,1,0:T(8,128)(2,1)S(1)}, u32[]{:S(2)}, u32[]{:S(2)}) %collective-permute-start.50) | collective-permute-done | bytes 409632 | tf_op jit(solution)/shard_map/ppermute | solution.py:53
  (241 shorter events, 70.0 us)
Async XLA Ops:
  7.2 195.9 %all-gather.3.cloned.1.call-start = ((), (), s32[]{:S(2)}) async-start(), calls=%async_computation | async-start | bytes 11796480 | tf_op jit(solution)/shard_map/all_gather | solution.py:469
  20.7 11.4 %collective-permute-start = (bf16[128,1280]{1,0:T(8,128)(2,1)}, bf16[128,1280]{1,0:T(8,128)(2,1)}, u32[]{:S(2)}, u32[]{:S(2)}) collective-permute-start(bf16[128,1280]{1,0:T(8,128)(2,1)} %get-tuple-element.158), channel_id=1, source_target_pairs={{0,1},{1,0},{2,3},{3,2},{4,5},{5,4},{6,7},{7,6},{8,9},{9,8},{10,11... | collective-permute-start | bytes 983048 | tf_op jit(solution)/shard_map/ppermute | solution.py:53
  27.2 17.4 %collective-permute-start.2 = (bf16[128,1280]{1,0:T(8,128)(2,1)}, bf16[128,1280]{1,0:T(8,128)(2,1)S(1)}, u32[]{:S(2)}, u32[]{:S(2)}) collective-permute-start(bf16[128,1280]{1,0:T(8,128)(2,1)} %get-tuple-element.160), channel_id=1, source_target_pairs={{0,2},{1,3},{2,0},{3,1},{4,6},{5,7},{6,4},{7,5},{8,10},{9,11},{10,... | collective-permute-start | bytes 983048 | tf_op jit(solution)/shard_map/ppermute | solution.py:53
  28.8 15.8 %collective-permute-start.3 = (bf16[128,1280]{1,0:T(8,128)(2,1)}, bf16[128,1280]{1,0:T(8,128)(2,1)S(1)}, u32[]{:S(2)}, u32[]{:S(2)}) collective-permute-start(bf16[128,1280]{1,0:T(8,128)(2,1)} %get-tuple-element.159), channel_id=1, source_target_pairs={{0,3},{1,2},{2,1},{3,0},{4,7},{5,6},{6,5},{7,4},{8,11},{9,10},{10,... | collective-permute-start | bytes 983048 | tf_op jit(solution)/shard_map/ppermute | solution.py:53
  32.2 16.4 %collective-permute-start.7 = (bf16[128,992]{1,0:T(8,128)(2,1)S(1)}, bf16[128,992]{1,0:T(8,128)(2,1)S(1)}, u32[]{:S(2)}, u32[]{:S(2)}) collective-permute-start(bf16[128,992]{1,0:T(8,128)(2,1)S(1)} %bitcast.150), channel_id=1, source_target_pairs={{0,8},{4,12},{8,0},{12,4},{16,24},{20,28},{24,16},{28,20},{1,9},{5... | collective-permute-start | bytes 761864 | tf_op jit(solution)/shard_map/ppermute | solution.py:53
  33.7 21.4 %collective-permute-start.8 = (bf16[128,992]{1,0:T(8,128)(2,1)S(1)}, bf16[128,992]{1,0:T(8,128)(2,1)S(1)}, u32[]{:S(2)}, u32[]{:S(2)}) collective-permute-start(bf16[128,992]{1,0:T(8,128)(2,1)S(1)} %bitcast.149), channel_id=1, source_target_pairs={{0,16},{4,20},{8,24},{12,28},{16,0},{20,4},{24,8},{28,12},{1,17},{... | collective-permute-start | bytes 761864 | tf_op jit(solution)/shard_map/ppermute | solution.py:53
  36.3 18.8 %collective-permute-start.9 = (bf16[128,992]{1,0:T(8,128)(2,1)S(1)}, bf16[128,992]{1,0:T(8,128)(2,1)S(1)}, u32[]{:S(2)}, u32[]{:S(2)}) collective-permute-start(bf16[128,992]{1,0:T(8,128)(2,1)S(1)} %bitcast.148), channel_id=1, source_target_pairs={{0,24},{4,28},{8,16},{12,20},{16,8},{20,12},{24,0},{28,4},{1,25},{... | collective-permute-start | bytes 761864 | tf_op jit(solution)/shard_map/ppermute | solution.py:53
  46.5 10.7 %collective-permute-start.4 = (bf16[128,1280]{1,0:T(8,128)(2,1)S(1)}, bf16[128,1280]{1,0:T(8,128)(2,1)S(1)}, u32[]{:S(2)}, u32[]{:S(2)}) collective-permute-start(bf16[128,1280]{1,0:T(8,128)(2,1)S(1)} %multiply_convert_fusion.5), channel_id=1, source_target_pairs={{0,1},{1,0},{2,3},{3,2},{4,5},{5,4},{6,7},{7,6},{8,9},{9,8},{10,11... | collective-permute-start | bytes 983048 | tf_op jit(solution)/shard_map/ppermute | solution.py:53
  46.8 15.3 %collective-permute-start.5 = (bf16[128,1280]{1,0:T(8,128)(2,1)S(1)}, bf16[128,1280]{1,0:T(8,128)(2,1)S(1)}, u32[]{:S(2)}, u32[]{:S(2)}) collective-permute-start(bf16[128,1280]{1,0:T(8,128)(2,1)S(1)} %multiply_convert_fusion.5), channel_id=1, source_target_pairs={{0,2},{1,3},{2,0},{3,1},{4,6},{5,7},{6,4},{7,5},{8,10},{9,11},{10,... | collective-permute-start | bytes 983048 | tf_op jit(solution)/shard_map/ppermute | solution.py:53
  48.6 15.2 %collective-permute-start.6 = (bf16[128,1280]{1,0:T(8,128)(2,1)S(1)}, bf16[128,1280]{1,0:T(8,128)(2,1)S(1)}, u32[]{:S(2)}, u32[]{:S(2)}) collective-permute-start(bf16[128,1280]{1,0:T(8,128)(2,1)S(1)} %multiply_convert_fusion.5), channel_id=1, source_target_pairs={{0,3},{1,2},{2,1},{3,0},{4,7},{5,6},{6,5},{7,4},{8,11},{9,10},{10,... | collective-permute-start | bytes 983048 | tf_op jit(solution)/shard_map/ppermute | solution.py:53
  63.9 23.2 %collective-permute-start.11 = (bf16[128,992]{1,0:T(8,128)(2,1)}, bf16[128,992]{1,0:T(8,128)(2,1)S(1)}, u32[]{:S(2)}, u32[]{:S(2)}) collective-permute-start(bf16[128,992]{1,0:T(8,128)(2,1)} %get-tuple-element.169), channel_id=1, source_target_pairs={{0,1},{1,0},{2,3},{3,2},{4,5},{5,4},{6,7},{7,6},{8,9},{9,8},{10,11... | collective-permute-start | bytes 761864 | tf_op jit(solution)/shard_map/ppermute | solution.py:53
  64.8 24.2 %collective-permute-start.12 = (bf16[128,992]{1,0:T(8,128)(2,1)}, bf16[128,992]{1,0:T(8,128)(2,1)S(1)}, u32[]{:S(2)}, u32[]{:S(2)}) collective-permute-start(bf16[128,992]{1,0:T(8,128)(2,1)} %get-tuple-element.168), channel_id=1, source_target_pairs={{0,2},{1,3},{2,0},{3,1},{4,6},{5,7},{6,4},{7,5},{8,10},{9,11},{10,... | collective-permute-start | bytes 761864 | tf_op jit(solution)/shard_map/ppermute | solution.py:53
  66.3 24.3 %collective-permute-start.13 = (bf16[128,992]{1,0:T(8,128)(2,1)}, bf16[128,992]{1,0:T(8,128)(2,1)S(1)}, u32[]{:S(2)}, u32[]{:S(2)}) collective-permute-start(bf16[128,992]{1,0:T(8,128)(2,1)} %get-tuple-element.167), channel_id=1, source_target_pairs={{0,3},{1,2},{2,1},{3,0},{4,7},{5,6},{6,5},{7,4},{8,11},{9,10},{10,... | collective-permute-start | bytes 761864 | tf_op jit(solution)/shard_map/ppermute | solution.py:53
  75.3 10.0 %collective-permute-start.10 = (bf16[256,768]{1,0:T(8,128)(2,1)S(1)}, bf16[256,768]{1,0:T(8,128)(2,1)S(1)}, u32[]{:S(2)}, u32[]{:S(2)}) collective-permute-start(bf16[256,768]{1,0:T(8,128)(2,1)S(1)} %pad_maximum_fusion.9), channel_id=1, source_target_pairs={{0,1},{1,0},{2,3},{3,2},{4,5},{5,4},{6,7},{7,6},{8,9},{9,8},{10,11... | collective-permute-start | bytes 1179656 | tf_op jit(solution)/shard_map/ppermute | solution.py:53
  76.0 9.9 %collective-permute-start.15 = (bf16[256,768]{1,0:T(8,128)(2,1)S(1)}, bf16[256,768]{1,0:T(8,128)(2,1)S(1)}, u32[]{:S(2)}, u32[]{:S(2)}) collective-permute-start(bf16[256,768]{1,0:T(8,128)(2,1)S(1)} %pad_maximum_fusion.10), channel_id=1, source_target_pairs={{0,2},{1,3},{2,0},{3,1},{4,6},{5,7},{6,4},{7,5},{8,10},{9,11},{10,... | collective-permute-start | bytes 1179656 | tf_op jit(solution)/shard_map/ppermute | solution.py:53
  85.3 18.8 %collective-permute-start.21 = (bf16[256,1152]{1,0:T(8,128)(2,1)S(1)}, bf16[256,1152]{1,0:T(8,128)(2,1)S(1)}, u32[]{:S(2)}, u32[]{:S(2)}) collective-permute-start(bf16[256,1152]{1,0:T(8,128)(2,1)S(1)} %pad_maximum_fusion.7), channel_id=1, source_target_pairs={{0,1},{1,0},{2,3},{3,2},{4,5},{5,4},{6,7},{7,6},{8,9},{9,8},{10,11... | collective-permute-start | bytes 1769480 | tf_op jit(solution)/shard_map/ppermute | solution.py:53
  86.0 7.8 %collective-permute-start.14 = (bf16[128,768]{1,0:T(8,128)(2,1)S(1)}, bf16[128,768]{1,0:T(8,128)(2,1)S(1)}, u32[]{:S(2)}, u32[]{:S(2)}) collective-permute-start(bf16[128,768]{1,0:T(8,128)(2,1)S(1)} %get-tuple-element.148), channel_id=1, source_target_pairs={{0,2},{1,3},{2,0},{3,1},{4,6},{5,7},{6,4},{7,5},{8,10},{9,11},{10,... | collective-permute-start | bytes 589832 | tf_op jit(solution)/shard_map/ppermute | solution.py:53
  87.2 15.6 %collective-permute-start.16 = (bf16[128,768]{1,0:T(8,128)(2,1)S(1)}, bf16[128,768]{1,0:T(8,128)(2,1)S(1)}, u32[]{:S(2)}, u32[]{:S(2)}) collective-permute-start(bf16[128,768]{1,0:T(8,128)(2,1)S(1)} %get-tuple-element.141), channel_id=1, source_target_pairs={{0,1},{1,0},{2,3},{3,2},{4,5},{5,4},{6,7},{7,6},{8,9},{9,8},{10,11... | collective-permute-start | bytes 589832 | tf_op jit(solution)/shard_map/ppermute | solution.py:53
  89.0 17.7 %collective-permute-start.25 = (bf16[256,1280]{1,0:T(8,128)(2,1)S(1)}, bf16[256,1280]{1,0:T(8,128)(2,1)S(1)}, u32[]{:S(2)}, u32[]{:S(2)}) collective-permute-start(bf16[256,1280]{1,0:T(8,128)(2,1)S(1)} %slice.329), channel_id=1, source_target_pairs={{0,2},{1,3},{2,0},{3,1},{4,6},{5,7},{6,4},{7,5},{8,10},{9,11},{10,... | collective-permute-start | bytes 1966088 | tf_op jit(solution)/shard_map/ppermute | solution.py:53
  103.2 15.0 %collective-permute-start.19 = (bf16[128,768]{1,0:T(8,128)(2,1)S(1)}, bf16[128,768]{1,0:T(8,128)(2,1)S(1)}, u32[]{:S(2)}, u32[]{:S(2)}) collective-permute-start(bf16[128,768]{1,0:T(8,128)(2,1)S(1)} %get-tuple-element.83), channel_id=1, source_target_pairs={{0,2},{1,3},{2,0},{3,1},{4,6},{5,7},{6,4},{7,5},{8,10},{9,11},{10,... | collective-permute-start | bytes 589832 | tf_op jit(solution)/shard_map/ppermute | solution.py:53
  103.8 13.5 %collective-permute-start.17 = (bf16[128,768]{1,0:T(8,128)(2,1)S(1)}, bf16[128,768]{1,0:T(8,128)(2,1)S(1)}, u32[]{:S(2)}, u32[]{:S(2)}) collective-permute-start(bf16[128,768]{1,0:T(8,128)(2,1)S(1)} %get-tuple-element.82), channel_id=1, source_target_pairs={{0,1},{1,0},{2,3},{3,2},{4,5},{5,4},{6,7},{7,6},{8,9},{9,8},{10,11... | collective-permute-start | bytes 589832 | tf_op jit(solution)/shard_map/ppermute | solution.py:53
  104.2 11.3 %collective-permute-start.22 = (bf16[128,1152]{1,0:T(8,128)(2,1)S(1)}, bf16[128,1152]{1,0:T(8,128)(2,1)S(1)}, u32[]{:S(2)}, u32[]{:S(2)}) collective-permute-start(bf16[128,1152]{1,0:T(8,128)(2,1)S(1)} %get-tuple-element.149), channel_id=1, source_target_pairs={{0,2},{1,3},{2,0},{3,1},{4,6},{5,7},{6,4},{7,5},{8,10},{9,11},{10,... | collective-permute-start | bytes 884744 | tf_op jit(solution)/shard_map/ppermute | solution.py:53
  106.9 13.0 %collective-permute-start.26 = (bf16[128,1280]{1,0:T(8,128)(2,1)S(1)}, bf16[128,1280]{1,0:T(8,128)(2,1)S(1)}, u32[]{:S(2)}, u32[]{:S(2)}) collective-permute-start(bf16[128,1280]{1,0:T(8,128)(2,1)S(1)} %get-tuple-element.145), channel_id=1, source_target_pairs={{0,1},{1,0},{2,3},{3,2},{4,5},{5,4},{6,7},{7,6},{8,9},{9,8},{10,11... | collective-permute-start | bytes 983048 | tf_op jit(solution)/shard_map/ppermute | solution.py:53
  116.0 10.0 %collective-permute-start.23 = (bf16[128,1152]{1,0:T(8,128)(2,1)S(1)}, bf16[128,1152]{1,0:T(8,128)(2,1)S(1)}, u32[]{:S(2)}, u32[]{:S(2)}) collective-permute-start(bf16[128,1152]{1,0:T(8,128)(2,1)S(1)} %loss.4), channel_id=1, source_target_pairs={{0,1},{1,0},{2,3},{3,2},{4,5},{5,4},{6,7},{7,6},{8,9},{9,8},{10,11... | collective-permute-start | bytes 884744 | tf_op jit(solution)/shard_map/ppermute | solution.py:53
  117.3 12.1 %collective-permute-start.18 = (bf16[256,768]{1,0:T(8,128)(2,1)S(1)}, bf16[256,768]{1,0:T(8,128)(2,1)S(1)}, u32[]{:S(2)}, u32[]{:S(2)}) collective-permute-start(bf16[256,768]{1,0:T(8,128)(2,1)S(1)} %pad_maximum_fusion.11), channel_id=1, source_target_pairs={{0,2},{1,3},{2,0},{3,1},{4,6},{5,7},{6,4},{7,5},{8,10},{9,11},{10,... | collective-permute-start | bytes 1179656 | tf_op jit(solution)/shard_map/ppermute | solution.py:53
  118.3 13.4 %collective-permute-start.20 = (bf16[256,768]{1,0:T(8,128)(2,1)S(1)}, bf16[256,768]{1,0:T(8,128)(2,1)S(1)}, u32[]{:S(2)}, u32[]{:S(2)}) collective-permute-start(bf16[256,768]{1,0:T(8,128)(2,1)S(1)} %pad_maximum_fusion.12), channel_id=1, source_target_pairs={{0,1},{1,0},{2,3},{3,2},{4,5},{5,4},{6,7},{7,6},{8,9},{9,8},{10,11... | collective-permute-start | bytes 1179656 | tf_op jit(solution)/shard_map/ppermute | solution.py:53
  120.4 16.0 %collective-permute-start.27 = (bf16[128,1280]{1,0:T(8,128)(2,1)S(1)}, bf16[128,1280]{1,0:T(8,128)(2,1)S(1)}, u32[]{:S(2)}, u32[]{:S(2)}) collective-permute-start(bf16[128,1280]{1,0:T(8,128)(2,1)S(1)} %loss.5), channel_id=1, source_target_pairs={{0,2},{1,3},{2,0},{3,1},{4,6},{5,7},{6,4},{7,5},{8,10},{9,11},{10,... | collective-permute-start | bytes 983048 | tf_op jit(solution)/shard_map/ppermute | solution.py:53
  126.1 19.5 %collective-permute-start.24 = (bf16[256,1152]{1,0:T(8,128)(2,1)S(1)}, bf16[256,1152]{1,0:T(8,128)(2,1)S(1)}, u32[]{:S(2)}, u32[]{:S(2)}) collective-permute-start(bf16[256,1152]{1,0:T(8,128)(2,1)S(1)} %pad_maximum_fusion.8), channel_id=1, source_target_pairs={{0,2},{1,3},{2,0},{3,1},{4,6},{5,7},{6,4},{7,5},{8,10},{9,11},{10,... | collective-permute-start | bytes 1769480 | tf_op jit(solution)/shard_map/ppermute | solution.py:53
  137.3 14.3 %collective-permute-start.28 = (bf16[256,1280]{1,0:T(8,128)(2,1)}, bf16[256,1280]{1,0:T(8,128)(2,1)S(1)}, u32[]{:S(2)}, u32[]{:S(2)}) collective-permute-start(bf16[256,1280]{1,0:T(8,128)(2,1)} %pad_maximum_fusion.6), channel_id=1, source_target_pairs={{0,1},{1,0},{2,3},{3,2},{4,5},{5,4},{6,7},{7,6},{8,9},{9,8},{10,11... | collective-permute-start | bytes 1966088 | tf_op jit(solution)/shard_map/ppermute | solution.py:53
  159.9 15.3 %collective-permute-start.32 = (bf16[4,160,1280]{2,1,0:T(8,128)(2,1)}, bf16[4,160,1280]{2,1,0:T(8,128)(2,1)}, u32[]{:S(2)}, u32[]{:S(2)}) collective-permute-start(bf16[4,160,1280]{2,1,0:T(8,128)(2,1)} %get-tuple-element.95), channel_id=1, source_target_pairs={{0,4},{4,0},{8,12},{12,8},{16,20},{20,16},{24,28},{28,24},{1,5},{5... | collective-permute-start | bytes 4915208 | tf_op jit(solution)/shard_map/ppermute | solution.py:53
  161.9 13.2 %collective-permute-start.31 = (bf16[2,192,640]{2,1,0:T(8,128)(2,1)S(1)}, bf16[2,192,640]{2,1,0:T(8,128)(2,1)S(1)}, u32[]{:S(2)}, u32[]{:S(2)}) collective-permute-start(bf16[2,192,640]{2,1,0:T(8,128)(2,1)S(1)} %slice.330), channel_id=1, source_target_pairs={{0,8},{4,12},{8,0},{12,4},{16,24},{20,28},{24,16},{28,20},{1,9},{5... | collective-permute-start | bytes 1474568 | tf_op jit(solution)/shard_map/ppermute | solution.py:53
  164.4 10.6 %collective-permute-start.30 = (bf16[128,1280]{1,0:T(8,128)(2,1)S(1)}, bf16[128,1280]{1,0:T(8,128)(2,1)S(1)}, u32[]{:S(2)}, u32[]{:S(2)}) collective-permute-start(bf16[128,1280]{1,0:T(8,128)(2,1)S(1)} %get-tuple-element.155), channel_id=1, source_target_pairs={{0,1},{1,0},{2,3},{3,2},{4,5},{5,4},{6,7},{7,6},{8,9},{9,8},{10,11... | collective-permute-start | bytes 983048 | tf_op jit(solution)/shard_map/ppermute | solution.py:53
  165.7 16.3 %collective-permute-start.33 = (bf16[128,1280]{1,0:T(8,128)(2,1)}, bf16[128,1280]{1,0:T(8,128)(2,1)S(1)}, u32[]{:S(2)}, u32[]{:S(2)}) collective-permute-start(bf16[128,1280]{1,0:T(8,128)(2,1)} %get-tuple-element.157), channel_id=1, source_target_pairs={{0,2},{1,3},{2,0},{3,1},{4,6},{5,7},{6,4},{7,5},{8,10},{9,11},{10,... | collective-permute-start | bytes 983048 | tf_op jit(solution)/shard_map/ppermute | solution.py:53
  166.6 15.4 %collective-permute-start.34 = (bf16[128,1280]{1,0:T(8,128)(2,1)}, bf16[128,1280]{1,0:T(8,128)(2,1)S(1)}, u32[]{:S(2)}, u32[]{:S(2)}) collective-permute-start(bf16[128,1280]{1,0:T(8,128)(2,1)} %get-tuple-element.156), channel_id=1, source_target_pairs={{0,3},{1,2},{2,1},{3,0},{4,7},{5,6},{6,5},{7,4},{8,11},{9,10},{10,... | collective-permute-start | bytes 983048 | tf_op jit(solution)/shard_map/ppermute | solution.py:53
  178.2 24.9 %collective-permute-start.39 = (bf16[2,160,1280]{2,1,0:T(8,128)(2,1)}, bf16[2,160,1280]{2,1,0:T(8,128)(2,1)}, u32[]{:S(2)}, u32[]{:S(2)}) collective-permute-start(bf16[2,160,1280]{2,1,0:T(8,128)(2,1)} %slice.328), channel_id=1, source_target_pairs={{0,8},{4,12},{8,0},{12,4},{16,24},{20,28},{24,16},{28,20},{1,9},{5... | collective-permute-start | bytes 2457608 | tf_op jit(solution)/shard_map/ppermute | solution.py:53
  182.7 11.7 %collective-permute-start.37 = (bf16[128,1280]{1,0:T(8,128)(2,1)S(1)}, bf16[128,1280]{1,0:T(8,128)(2,1)}, u32[]{:S(2)}, u32[]{:S(2)}) collective-permute-start(bf16[128,1280]{1,0:T(8,128)(2,1)S(1)} %multiply_convert_fusion.4), channel_id=1, source_target_pairs={{0,3},{1,2},{2,1},{3,0},{4,7},{5,6},{6,5},{7,4},{8,11},{9,10},{10,... | collective-permute-start | bytes 983048 | tf_op jit(solution)/shard_map/ppermute | solution.py:53
  183.7 19.4 %collective-permute-start.35 = (bf16[128,1280]{1,0:T(8,128)(2,1)S(1)}, bf16[128,1280]{1,0:T(8,128)(2,1)}, u32[]{:S(2)}, u32[]{:S(2)}) collective-permute-start(bf16[128,1280]{1,0:T(8,128)(2,1)S(1)} %multiply_convert_fusion.4), channel_id=1, source_target_pairs={{0,1},{1,0},{2,3},{3,2},{4,5},{5,4},{6,7},{7,6},{8,9},{9,8},{10,11... | collective-permute-start | bytes 983048 | tf_op jit(solution)/shard_map/ppermute | solution.py:53
  185.1 18.0 %collective-permute-start.36 = (bf16[128,1280]{1,0:T(8,128)(2,1)S(1)}, bf16[128,1280]{1,0:T(8,128)(2,1)}, u32[]{:S(2)}, u32[]{:S(2)}) collective-permute-start(bf16[128,1280]{1,0:T(8,128)(2,1)S(1)} %multiply_convert_fusion.4), channel_id=1, source_target_pairs={{0,2},{1,3},{2,0},{3,1},{4,6},{5,7},{6,4},{7,5},{8,10},{9,11},{10,... | collective-permute-start | bytes 983048 | tf_op jit(solution)/shard_map/ppermute | solution.py:53
  188.6 22.4 %collective-permute-start.40 = (bf16[1,192,640]{2,1,0:T(8,128)(2,1)S(1)}, bf16[1,192,640]{2,1,0:T(8,128)(2,1)S(1)}, u32[]{:S(2)}, u32[]{:S(2)}) collective-permute-start(bf16[1,192,640]{2,1,0:T(8,128)(2,1)S(1)} %slice.332), channel_id=1, source_target_pairs={{0,16},{4,20},{8,24},{12,28},{16,0},{20,4},{24,8},{28,12},{1,17},{... | collective-permute-start | bytes 737288 | tf_op jit(solution)/shard_map/ppermute | solution.py:53
  213.8 9.0 %collective-permute-start.44 = (bf16[2,160,128]{2,1,0:T(8,128)(2,1)S(1)}, bf16[2,160,128]{2,1,0:T(8,128)(2,1)S(1)}, u32[]{:S(2)}, u32[]{:S(2)}) collective-permute-start(bf16[2,160,128]{2,1,0:T(8,128)(2,1)S(1)} %pad_maximum_fusion.18), channel_id=1, source_target_pairs={{0,24},{4,28},{8,16},{12,20},{16,8},{20,12},{24,0},{28,4},{1,25},{... | collective-permute-start | bytes 245768 | tf_op jit(solution)/shard_map/ppermute | solution.py:53
  217.2 14.6 %collective-permute-start.43 = (bf16[2,160,128]{2,1,0:T(8,128)(2,1)S(1)}, bf16[2,160,128]{2,1,0:T(8,128)(2,1)S(1)}, u32[]{:S(2)}, u32[]{:S(2)}) collective-permute-start(bf16[2,160,128]{2,1,0:T(8,128)(2,1)S(1)} %pad_maximum_fusion.17), channel_id=1, source_target_pairs={{0,16},{4,20},{8,24},{12,28},{16,0},{20,4},{24,8},{28,12},{1,17},{... | collective-permute-start | bytes 245768 | tf_op jit(solution)/shard_map/ppermute | solution.py:53
  217.3 14.5 %collective-permute-start.42 = (bf16[2,160,128]{2,1,0:T(8,128)(2,1)S(1)}, bf16[2,160,128]{2,1,0:T(8,128)(2,1)S(1)}, u32[]{:S(2)}, u32[]{:S(2)}) collective-permute-start(bf16[2,160,128]{2,1,0:T(8,128)(2,1)S(1)} %pad_maximum_fusion.16), channel_id=1, source_target_pairs={{0,8},{4,12},{8,0},{12,4},{16,24},{20,28},{24,16},{28,20},{1,9},{5... | collective-permute-start | bytes 245768 | tf_op jit(solution)/shard_map/ppermute | solution.py:53
  218.4 23.3 %collective-permute-start.46 = (bf16[1,160,1280]{2,1,0:T(8,128)(2,1)S(1)}, bf16[1,160,1280]{2,1,0:T(8,128)(2,1)S(1)}, u32[]{:S(2)}, u32[]{:S(2)}) collective-permute-start(bf16[1,160,1280]{2,1,0:T(8,128)(2,1)S(1)} %slice.331), channel_id=1, source_target_pairs={{0,16},{4,20},{8,24},{12,28},{16,0},{20,4},{24,8},{28,12},{1,17},{... | collective-permute-start | bytes 1228808 | tf_op jit(solution)/shard_map/ppermute | solution.py:53
  220.7 29.6 %collective-permute-start.45 = (bf16[2,160,1280]{2,1,0:T(8,128)(2,1)S(1)}, bf16[2,160,1280]{2,1,0:T(8,128)(2,1)S(1)}, u32[]{:S(2)}, u32[]{:S(2)}) collective-permute-start(bf16[2,160,1280]{2,1,0:T(8,128)(2,1)S(1)} %get-tuple-element.109), channel_id=1, source_target_pairs={{0,8},{4,12},{8,0},{12,4},{16,24},{20,28},{24,16},{28,20},{1,9},{5... | collective-permute-start | bytes 2457608 | tf_op jit(solution)/shard_map/ppermute | solution.py:53
  231.9 9.8 %collective-permute-start.47 = (bf16[8,160,128]{2,1,0:T(8,128)(2,1)S(1)}, bf16[8,160,128]{2,1,0:T(8,128)(2,1)S(1)}, u32[]{:S(2)}, u32[]{:S(2)}) collective-permute-start(bf16[8,160,128]{2,1,0:T(8,128)(2,1)S(1)} %constant_dynamic-update-slice_fusion.3.refs_0_), channel_id=1, source_target_pairs={{0,1},{1,0},{2,3},{3,2},{4,5},{5,4},{6,7},{7,6},{8,9},{9,8},{10,11... | collective-permute-start | bytes 983048 | tf_op jit(solution)/shard_map/ppermute | solution.py:53
  232.0 13.1 %collective-permute-start.48 = (bf16[8,160,128]{2,1,0:T(8,128)(2,1)S(1)}, bf16[8,160,128]{2,1,0:T(8,128)(2,1)S(1)}, u32[]{:S(2)}, u32[]{:S(2)}) collective-permute-start(bf16[8,160,128]{2,1,0:T(8,128)(2,1)S(1)} %constant_dynamic-update-slice_fusion.3.refs_0_), channel_id=1, source_target_pairs={{0,2},{1,3},{2,0},{3,1},{4,6},{5,7},{6,4},{7,5},{8,10},{9,11},{10,... | collective-permute-start | bytes 983048 | tf_op jit(solution)/shard_map/ppermute | solution.py:53
  232.0 13.1 %collective-permute-start.49 = (bf16[8,160,128]{2,1,0:T(8,128)(2,1)S(1)}, bf16[8,160,128]{2,1,0:T(8,128)(2,1)S(1)}, u32[]{:S(2)}, u32[]{:S(2)}) collective-permute-start(bf16[8,160,128]{2,1,0:T(8,128)(2,1)S(1)} %constant_dynamic-update-slice_fusion.3.refs_0_), channel_id=1, source_target_pairs={{0,3},{1,2},{2,1},{3,0},{4,7},{5,6},{6,5},{7,4},{8,11},{9,10},{10,... | collective-permute-start | bytes 983048 | tf_op jit(solution)/shard_map/ppermute | solution.py:53
  250.6 20.6 %collective-permute-start.50 = (bf16[1,160,1280]{2,1,0:T(8,128)(2,1)S(1)}, bf16[1,160,1280]{2,1,0:T(8,128)(2,1)S(1)}, u32[]{:S(2)}, u32[]{:S(2)}) collective-permute-start(bf16[1,160,1280]{2,1,0:T(8,128)(2,1)S(1)} %get-tuple-element.116), channel_id=1, source_target_pairs={{0,16},{4,20},{8,24},{12,28},{16,0},{20,4},{24,8},{28,12},{1,17},{... | collective-permute-start | bytes 1228808 | tf_op jit(solution)/shard_map/ppermute | solution.py:53
  (42 other events, 237.4 us)
Sparse Core Ops, SparseCore 0:
  64.0 99.9 all-gather.2

commit v3 on v2

--- a/solution.py
+++ b/solution.py
@@ -89,7 +89,7 @@
         leaving = [j for j in sorted(held) if j & later]
         packed = jnp.concatenate([held.pop(j).astype(jnp.bfloat16) for j in leaving], axis=0)
         packed = swap(packed, axis, later)
-    return held[0], packed
+    return [held[0], packed]
 
 
 def gather_doubling(piece, axis, low_first):
@@ -465,7 +465,8 @@
 
     final_rows, normal_rows, inverse_rows = normalize(hidden, final_gain)
     final = gather(final_rows.astype(jnp.bfloat16), "mp")
-    final, late, own = pin(final, active, owned[:block])
+    bend_two = smooth_slope(widened)
+    final, late, own, bend_two = pin(final, active, owned[:block], bend_two)
     actives = lax.all_gather(late, "dp")
 
     owned = owned.reshape(members, block, -1)
@@ -493,6 +494,8 @@
         [scatter_rest(*term, "mp", way) for term, way in zip(terms, ways[index])]
         for index, terms in enumerate(students)
     ]
+    bends = [smooth_slope(before) for before in befores]
+    students[0][0][1], *bends = pin(students[0][0][1], *bends)
     slopes = []
     start = 0
     for index in range(3):
@@ -507,7 +510,7 @@
         for k, slope in enumerate(slopes[index]):
             head = heads[index][:, k * wide : (k + 1) * wide]
             back = back + jnp.einsum("rc,hc->rh", slope, head, **exact)
-        inner = (back * smooth_slope(befores[index])).astype(jnp.bfloat16)
+        inner = (back * bends[index]).astype(jnp.bfloat16)
         inners.append(inner)
         upstream = upstream + jnp.einsum("rh,dh->rd", inner, adaptor_in[index], **exact)
         if index == 1:
@@ -523,7 +526,7 @@
         product([([final], inners), (slopes[2], lifteds[2:])], groups, group)
     )
     came[0], one, two = pin(came[0], of_heads[1], of_rest[1])
-    of_heads = advance(arrive(of_heads, one))
+    of_heads = arrive(of_heads, one)
     of_rest = advance(arrive(of_rest, two))
     total = mine
     for piece in came:
@@ -534,17 +537,16 @@
     turned = through_rows.T.reshape(groups, -1, block)
     turned = [lax.dynamic_index_in_dim(turned, group ^ o, 0) for o in range(groups)]
     odd = swap(jnp.concatenate(turned[1::2], axis=0), "dp", 1)
-    came[-1], odd, one, actives = pin(came[-1], odd, of_rest[1], actives)
-    of_rest = advance(arrive(of_rest, one))
+    came[-1], odd, one, two, actives = pin(came[-1], odd, of_heads[1], of_rest[1], actives)
+    of_heads, of_rest = arrive(of_heads, one), arrive(of_rest, two)
     through = jnp.concatenate([through_rows, *came], axis=0)
     both = [jnp.concatenate([turned[2 * o], odd[o : o + 1]]) for o in range(groups // 2)]
     both = [both[0]] + [swap(both[o], "dp", 2 * o) for o in range(1, groups // 2)]
 
     back_two = jnp.einsum("rd,fd->rf", through, narrow_weight, **exact)
-    inner_two = (back_two * smooth_slope(widened)).astype(jnp.bfloat16)
-    of_heads = settle(of_heads)
-    inner_two, one, two = pin(inner_two, of_heads[1], of_rest[0])
-    of_heads, of_rest = arrive(of_heads, one), (two, *of_rest[1:])
+    inner_two = (back_two * bend_two).astype(jnp.bfloat16)
+    inner_two, one, two = pin(inner_two, of_heads[1], of_rest[1])
+    of_heads, of_rest = settle(arrive(of_heads, one)), settle(arrive(of_rest, two))
     of_widen = begin(product([([first], [inner_two])], groups, group, 2**35))
     of_widen = advance(of_widen, True)
     keep, *both = pin(of_widen[0], *both)

time: 280 us -> 278 us (level)
  transfers between devices with their start and end apart: 52 -> 52, of which waited for: 27 -> 30; matrix products, arithmetic and copies ran while one was open for 14% -> 12% of each run, Pallas kernels for 8% -> 8%
where the time goes in v3:
time: 278 us
  waiting for transfers between devices  122 us (44%)
  starting transfers between devices  60.6 us (22%)
  matrix products  32.1 us (12%)
  Pallas kernels  25.2 us (9%)
  between operations  14.9 us (5%)
  other arithmetic  13 us (5%)
  local copies, waits for them, and re-layouts  10.1 us (4%)
    ppermute x51, waiting for transfers between devices, swap(): return lax.ppermute(value, axis, [(i, i ^ offset) for i in range(count)])  122 us
    ppermute x51, starting transfers between devices, swap(): return lax.ppermute(value, axis, [(i, i ^ offset) for i in range(count)])  60.6 us
    pallas_call x3, Pallas kernels, product(): pl.pallas_call(functools.partial(product_kernel, groups, [(len(l), len(r)...  9.4 us
    pallas_call x1, Pallas kernels, narrow_sum(): pl.pallas_call(functools.partial(narrow_kernel, len(columns)), out_shape=...  8.81 us
    dot_general x3, matrix products, local(): before = jnp.dot(final, adaptor_in[index], **exact)  7.39 us
  transfers between devices with their start and end apart: 52, of which 30 were waited for; matrix products, arithmetic and copies ran while one was open for 12% of the time, Pallas kernels for 8%

profile of v3, /device:TPU:0, one launch (start us, length us, event | category | flops | bytes accessed | tf_op | source)
XLA Modules:
  0.0 277.6 jit_solution(17015909161627536486)
XLA Ops:
  10.0 5.0 %fusion.10 = (f32[512,1280]{1,0:T(8,128)}, bf16[512,1280]{1,0:T(8,128)(2,1)}) fusion(bf16[512,1280]{1,0:T(8,128)(2,1)S(1)} %fusion.5.refs_0_, bf16[1280,1280]{1,0:T(8,128)(2,1)S(1)} %copy-done), kind=kOutput, calls=%fused_computation.18 | convolution fusion | flops 1690173440 | bytes 8519680 | tf_op jit(solution)/shard_map/dot_general | solution.py:439
  15.0 4.2 %fusion.78 = f32[512,1280]{1,0:T(8,128)S(1)} fusion(bf16[512,1280]{1,0:T(8,128)(2,1)} %get-tuple-element.110, bf16[1280,1280]{1,0:T(8,128)(2,1)} %param.17), kind=kOutput, calls=%fused_computation.192 | convolution fusion | flops 1677721600 | bytes 7208960 | tf_op jit(solution)/shard_map/dot_general | solution.py:441
  21.6 2.9 %collective-permute-start = (bf16[128,1280]{1,0:T(8,128)(2,1)}, bf16[128,1280]{1,0:T(8,128)(2,1)}, u32[]{:S(2)}, u32[]{:S(2)}) collective-permute-start(bf16[128,1280]{1,0:T(8,128)(2,1)} %get-tuple-element.172), channel_id=1, source_target_pairs={{0,1},{1,0},{2,3},{3,2},{4,5},{5,4},{6,7},{7,6},{8,9},{9,8},{10,11... | collective-permute-start | bytes 983048 | tf_op jit(solution)/shard_map/ppermute | solution.py:53
  24.6 3.5 %pack.1 = (bf16[256,992]{1,0:T(8,128)(2,1)S(1)}, bf16[256,992]{1,0:T(8,128)(2,1)S(1)}) custom-call(s32[3]{0:T(128)S(1)} %copy-done.8, s32[128]{0:T(128)S(1)} %copy-done.7, s32[1]{0:T(128)} %bitcast.10.group_ref, bf16[2,512,384]{2,1,0:T(8,128)(2,1)S(1)} %copy-done.4, bf16[2,288,512]{2,1,0:T(8,128)(2,1)S(1)} %bitcast.133, bf16[2,320,512]{2,1,0:T(8,128)(2,1)S(1)} %bitcast.132), custom_call_target="tpu_custom_call" | custom-call | tf_op jit(solution)/shard_map/pack/pallas_call | solution.py:173
  30.7 2.3 collective-permute-done
  34.6 2.6 collective-permute-start.8
  37.6 7.9 %collective-permute-done.2 = bf16[128,1280]{1,0:T(8,128)(2,1)S(1)} collective-permute-done((bf16[128,1280]{1,0:T(8,128)(2,1)}, bf16[128,1280]{1,0:T(8,128)(2,1)S(1)}, u32[]{:S(2)}, u32[]{:S(2)}) %collective-permute-start.2) | collective-permute-done | bytes 327712 | tf_op jit(solution)/shard_map/ppermute | solution.py:53
  47.8 1.8 collective-permute-start.5
  51.1 4.9 %collective-permute-done.8.refs_2_ = bf16[128,992]{1,0:T(8,128)(2,1)S(1)} collective-permute-done((bf16[128,992]{1,0:T(8,128)(2,1)S(1)}, bf16[128,992]{1,0:T(8,128)(2,1)S(1)}, u32[]{:S(2)}, u32[]{:S(2)}) %collective-permute-start.8) | collective-permute-done | bytes 253984 | tf_op jit(solution)/shard_map/ppermute | solution.py:53
  58.1 5.0 %collective-permute-done.5 = bf16[128,1280]{1,0:T(8,128)(2,1)S(1)} collective-permute-done((bf16[128,1280]{1,0:T(8,128)(2,1)S(1)}, bf16[128,1280]{1,0:T(8,128)(2,1)S(1)}, u32[]{:S(2)}, u32[]{:S(2)}) %collective-permute-start.5) | collective-permute-done | bytes 327712 | tf_op jit(solution)/shard_map/ppermute | solution.py:53
  68.5 3.2 %fusion.36 = (f32[512,320]{1,0:T(8,128)}, bf16[512,320]{1,0:T(8,128)(2,1)S(1)}) fusion(bf16[512,1280]{1,0:T(8,128)(2,1)S(1)} %pad_maximum_fusion.1.refs_0_, bf16[3,1280,320]{1,2,0:T(8,128)(2,1)} %param.19), kind=kOutput, calls=%fused_computation.72 | convolution fusion | flops 422543360 | bytes 3112960 | tf_op jit(solution)/shard_map/dot_general | solution.py:478
  73.6 2.1 multiply_convert_fusion.2
  79.4 2.1 multiply_convert_fusion.1
  81.5 4.7 %collective-permute-done.10 = bf16[256,768]{1,0:T(8,128)(2,1)S(1)} collective-permute-done((bf16[256,768]{1,0:T(8,128)(2,1)S(1)}, bf16[256,768]{1,0:T(8,128)(2,1)S(1)}, u32[]{:S(2)}, u32[]{:S(2)}) %collective-permute-start.10) | collective-permute-done | bytes 393248 | tf_op jit(solution)/shard_map/ppermute | solution.py:53
  90.1 3.8 %collective-permute-done.14.refs_5_ = bf16[128,768]{1,0:T(8,128)(2,1)S(1)} collective-permute-done((bf16[128,768]{1,0:T(8,128)(2,1)S(1)}, bf16[128,768]{1,0:T(8,128)(2,1)S(1)}, u32[]{:S(2)}, u32[]{:S(2)}) %collective-permute-start.14) | collective-permute-done | bytes 196640 | tf_op jit(solution)/shard_map/ppermute | solution.py:53
  95.5 7.7 %collective-permute-done.16.refs_7_ = bf16[128,768]{1,0:T(8,128)(2,1)S(1)} collective-permute-done((bf16[128,768]{1,0:T(8,128)(2,1)S(1)}, bf16[128,768]{1,0:T(8,128)(2,1)S(1)}, u32[]{:S(2)}, u32[]{:S(2)}) %collective-permute-start.16) | collective-permute-done | bytes 196640 | tf_op jit(solution)/shard_map/ppermute | solution.py:53
  106.6 4.2 %collective-permute-done.25 = bf16[256,1280]{1,0:T(8,128)(2,1)} collective-permute-done((bf16[256,1280]{1,0:T(8,128)(2,1)S(1)}, bf16[256,1280]{1,0:T(8,128)(2,1)}, u32[]{:S(2)}, u32[]{:S(2)}) %collective-permute-start.25) | collective-permute-done | bytes 655392 | tf_op jit(solution)/shard_map/ppermute | solution.py:53
  112.0 2.2 collective-permute-start.26
  114.2 3.1 %collective-permute-done.22.refs_5_ = bf16[128,1152]{1,0:T(8,128)(2,1)S(1)} collective-permute-done((bf16[128,1152]{1,0:T(8,128)(2,1)S(1)}, bf16[128,1152]{1,0:T(8,128)(2,1)S(1)}, u32[]{:S(2)}, u32[]{:S(2)}) %collective-permute-start.22) | collective-permute-done | bytes 294944 | tf_op jit(solution)/shard_map/ppermute | solution.py:53
  120.3 2.1 collective-permute-start.20
  123.0 2.5 collective-permute-start.27
  125.5 3.1 %collective-permute-done.23 = bf16[128,1152]{1,0:T(8,128)(2,1)S(1)} collective-permute-done((bf16[128,1152]{1,0:T(8,128)(2,1)S(1)}, bf16[128,1152]{1,0:T(8,128)(2,1)S(1)}, u32[]{:S(2)}, u32[]{:S(2)}) %collective-permute-start.23) | collective-permute-done | bytes 294944 | tf_op jit(solution)/shard_map/ppermute | solution.py:53
  128.7 2.7 collective-permute-start.24
  131.6 2.4 collective-permute-done.20
  135.3 2.2 fusion.28
  140.2 5.2 %collective-permute-done.24 = bf16[256,1152]{1,0:T(8,128)(2,1)S(1)} collective-permute-done((bf16[256,1152]{1,0:T(8,128)(2,1)S(1)}, bf16[256,1152]{1,0:T(8,128)(2,1)S(1)}, u32[]{:S(2)}, u32[]{:S(2)}) %collective-permute-start.24) | collective-permute-done | bytes 589856 | tf_op jit(solution)/shard_map/ppermute | solution.py:53
  145.5 2.3 product.3
  147.9 2.1 fusion.21.refs_2_
  150.9 2.1 collective-permute-done.28
  155.7 4.3 %product.4 = (bf16[4,160,1280]{2,1,0:T(8,128)(2,1)S(1)}, bf16[4,160,1280]{2,1,0:T(8,128)(2,1)}) custom-call(s32[2]{0:T(128)S(1)} %pad_add_fusion.spot_ref, bf16[512,1280]{1,0:T(8,128)(2,1)S(1)} %pad_maximum_fusion.1.refs_0_, bf16[512,320]{1,0:T(8,128)(2,1)S(1)} %fusion.20.refs_1_, bf16[512,320]{1,0:T(8,128)(2,1)S(1)} %fusion.21.refs_2_, ...), custom_call_target="tpu_custom_call" | custom-call | tf_op jit(solution)/shard_map/product/pallas_call | solution.py:269
  165.5 2.1 collective-permute-start.34
  167.6 7.1 %collective-permute-done.30 = bf16[128,1280]{1,0:T(8,128)(2,1)S(1)} collective-permute-done((bf16[128,1280]{1,0:T(8,128)(2,1)S(1)}, bf16[128,1280]{1,0:T(8,128)(2,1)S(1)}, u32[]{:S(2)}, u32[]{:S(2)}) %collective-permute-start.30) | collective-permute-done | bytes 327712 | tf_op jit(solution)/shard_map/ppermute | solution.py:53
  175.4 1.9 convert_add_fusion
  178.9 2.4 collective-permute-done.33
  188.2 6.3 %collective-permute-done.37 = bf16[128,1280]{1,0:T(8,128)(2,1)S(1)} collective-permute-done((bf16[128,1280]{1,0:T(8,128)(2,1)S(1)}, bf16[128,1280]{1,0:T(8,128)(2,1)S(1)}, u32[]{:S(2)}, u32[]{:S(2)}) %collective-permute-start.37) | collective-permute-done | bytes 327712 | tf_op jit(solution)/shard_map/ppermute | solution.py:53
  194.6 2.7 collective-permute-done.39
  197.3 2.5 collective-permute-done.35
  199.8 4.8 %fusion.2.refs_1_ = bf16[512,1280]{1,0:T(8,128)(2,1)S(1)} fusion(f32[512,1280]{1,0:T(8,128)} %get-tuple-element.112, bf16[1280,1280]{1,0:T(8,128)(2,1)} %param.17, bf16[128,1280]{1,0:T(8,128)(2,1)S(1)} %collective-permute-done.37, bf16[128,1280]{1,0:T(8,128)(2,1)} %collective-permute-done.36, bf16[128,1280]{1,0:T(8,128)(2,1)} %collective-permute-done.35, ...), kind=kOutput, calls=%fused_computation.10 | convolution fusion | flops 1684275200 | bytes 8519680 | tf_op jit(solution)/shard_map/rd,fd->rf/dot_general | solution.py:546
  204.6 2.8 %product.5 = (bf16[4,160,1280]{2,1,0:T(8,128)(2,1)S(1)}, bf16[4,160,1280]{2,1,0:T(8,128)(2,1)S(1)}) custom-call(s32[2]{0:T(128)S(1)} %pad_add_fusion.spot_ref, bf16[512,1280]{1,0:T(8,128)(2,1)S(1)} %copy-done.3, bf16[512,1280]{1,0:T(8,128)(2,1)S(1)} %fusion.2.refs_1_), custom_call_target="tpu_custom_call" | custom-call | flops 34359738368 | tf_op jit(solution)/shard_map/product/pallas_call | solution.py:269
  207.6 2.7 collective-permute-start.43
  212.4 1.9 collective-permute-start.45
  216.1 11.7 %collective-permute-done.42 = bf16[2,160,128]{2,1,0:T(8,128)(2,1)S(1)} collective-permute-done((bf16[2,160,128]{2,1,0:T(8,128)(2,1)S(1)}, bf16[2,160,128]{2,1,0:T(8,128)(2,1)S(1)}, u32[]{:S(2)}, u32[]{:S(2)}) %collective-permute-start.42) | collective-permute-done | bytes 81952 | tf_op jit(solution)/shard_map/ppermute | solution.py:53
  231.6 4.7 %collective-permute-done.45.refs_3_ = bf16[1,160,1280]{2,1,0:T(8,128)(2,1)S(1)} collective-permute-done((bf16[1,160,1280]{2,1,0:T(8,128)(2,1)S(1)}, bf16[1,160,1280]{2,1,0:T(8,128)(2,1)S(1)}, u32[]{:S(2)}, u32[]{:S(2)}) %collective-permute-start.45) | collective-permute-done | bytes 409632 | tf_op jit(solution)/shard_map/ppermute | solution.py:53
  236.4 2.2 collective-permute-done.46.refs_1_
  238.5 6.9 %collective-permute-done.47.refs_2_ = bf16[8,160,128]{2,1,0:T(8,128)(2,1)S(1)} collective-permute-done((bf16[8,160,128]{2,1,0:T(8,128)(2,1)S(1)}, bf16[8,160,128]{2,1,0:T(8,128)(2,1)S(1)}, u32[]{:S(2)}, u32[]{:S(2)}) %collective-permute-start.47) | collective-permute-done | bytes 327712 | tf_op jit(solution)/shard_map/ppermute | solution.py:53
  245.5 3.8 %collective-permute-done.44.came_ref = bf16[2,160,1280]{2,1,0:T(8,128)(2,1)S(1)} collective-permute-done((bf16[2,160,1280]{2,1,0:T(8,128)(2,1)S(1)}, bf16[2,160,1280]{2,1,0:T(8,128)(2,1)S(1)}, u32[]{:S(2)}, u32[]{:S(2)}) %collective-permute-start.44) | collective-permute-done | bytes 819232 | tf_op jit(solution)/shard_map/ppermute | solution.py:53
  249.8 8.8 %narrow.1 = f32[160,1280]{1,0:T(8,128)} custom-call(s32[1]{0:T(128)} %bitcast.10.group_ref, bf16[8,512,1280]{2,1,0:T(8,128)(2,1)} %bitcast.151, bf16[8,160,128]{2,1,0:T(8,128)(2,1)S(1)} %constant_dynamic-update-slice_fusion.3.refs_0_, bf16[8,160,128]{2,1,0:T(8,128)(2,1)S(1)} %collective-permute-done.46.refs_1_, ...), custom_call_target="tpu_custom_call" | custom-call | flops 34359738368 | tf_op jit(solution)/shard_map/narrow/pallas_call | solution.py:296
  260.6 9.2 %collective-permute-done.49 = bf16[1,160,1280]{2,1,0:T(8,128)(2,1)S(1)} collective-permute-done((bf16[1,160,1280]{2,1,0:T(8,128)(2,1)S(1)}, bf16[1,160,1280]{2,1,0:T(8,128)(2,1)S(1)}, u32[]{:S(2)}, u32[]{:S(2)}) %collective-permute-start.49) | collective-permute-done | bytes 409632 | tf_op jit(solution)/shard_map/ppermute | solution.py:53
  (229 shorter events, 73.9 us)
Async XLA Ops:
  7.2 190.1 %all-gather.3.cloned.1.call-start = ((), (), s32[]{:S(2)}) async-start(), calls=%async_computation | async-start | bytes 11796480 | tf_op jit(solution)/shard_map/all_gather | solution.py:470
  21.6 11.4 %collective-permute-start = (bf16[128,1280]{1,0:T(8,128)(2,1)}, bf16[128,1280]{1,0:T(8,128)(2,1)}, u32[]{:S(2)}, u32[]{:S(2)}) collective-permute-start(bf16[128,1280]{1,0:T(8,128)(2,1)} %get-tuple-element.172), channel_id=1, source_target_pairs={{0,1},{1,0},{2,3},{3,2},{4,5},{5,4},{6,7},{7,6},{8,9},{9,8},{10,11... | collective-permute-start | bytes 983048 | tf_op jit(solution)/shard_map/ppermute | solution.py:53
  28.1 17.4 %collective-permute-start.2 = (bf16[128,1280]{1,0:T(8,128)(2,1)}, bf16[128,1280]{1,0:T(8,128)(2,1)S(1)}, u32[]{:S(2)}, u32[]{:S(2)}) collective-permute-start(bf16[128,1280]{1,0:T(8,128)(2,1)} %get-tuple-element.174), channel_id=1, source_target_pairs={{0,2},{1,3},{2,0},{3,1},{4,6},{5,7},{6,4},{7,5},{8,10},{9,11},{10,... | collective-permute-start | bytes 983048 | tf_op jit(solution)/shard_map/ppermute | solution.py:53
  29.7 15.8 %collective-permute-start.3 = (bf16[128,1280]{1,0:T(8,128)(2,1)}, bf16[128,1280]{1,0:T(8,128)(2,1)S(1)}, u32[]{:S(2)}, u32[]{:S(2)}) collective-permute-start(bf16[128,1280]{1,0:T(8,128)(2,1)} %get-tuple-element.173), channel_id=1, source_target_pairs={{0,3},{1,2},{2,1},{3,0},{4,7},{5,6},{6,5},{7,4},{8,11},{9,10},{10,... | collective-permute-start | bytes 983048 | tf_op jit(solution)/shard_map/ppermute | solution.py:53
  33.1 16.4 %collective-permute-start.7 = (bf16[128,992]{1,0:T(8,128)(2,1)S(1)}, bf16[128,992]{1,0:T(8,128)(2,1)S(1)}, u32[]{:S(2)}, u32[]{:S(2)}) collective-permute-start(bf16[128,992]{1,0:T(8,128)(2,1)S(1)} %bitcast.150), channel_id=1, source_target_pairs={{0,8},{4,12},{8,0},{12,4},{16,24},{20,28},{24,16},{28,20},{1,9},{5... | collective-permute-start | bytes 761864 | tf_op jit(solution)/shard_map/ppermute | solution.py:53
  34.6 21.4 %collective-permute-start.8 = (bf16[128,992]{1,0:T(8,128)(2,1)S(1)}, bf16[128,992]{1,0:T(8,128)(2,1)S(1)}, u32[]{:S(2)}, u32[]{:S(2)}) collective-permute-start(bf16[128,992]{1,0:T(8,128)(2,1)S(1)} %bitcast.149), channel_id=1, source_target_pairs={{0,16},{4,20},{8,24},{12,28},{16,0},{20,4},{24,8},{28,12},{1,17},{... | collective-permute-start | bytes 761864 | tf_op jit(solution)/shard_map/ppermute | solution.py:53
  37.2 18.8 %collective-permute-start.9 = (bf16[128,992]{1,0:T(8,128)(2,1)S(1)}, bf16[128,992]{1,0:T(8,128)(2,1)S(1)}, u32[]{:S(2)}, u32[]{:S(2)}) collective-permute-start(bf16[128,992]{1,0:T(8,128)(2,1)S(1)} %bitcast.148), channel_id=1, source_target_pairs={{0,24},{4,28},{8,16},{12,20},{16,8},{20,12},{24,0},{28,4},{1,25},{... | collective-permute-start | bytes 761864 | tf_op jit(solution)/shard_map/ppermute | solution.py:53
  47.4 10.7 %collective-permute-start.4 = (bf16[128,1280]{1,0:T(8,128)(2,1)S(1)}, bf16[128,1280]{1,0:T(8,128)(2,1)S(1)}, u32[]{:S(2)}, u32[]{:S(2)}) collective-permute-start(bf16[128,1280]{1,0:T(8,128)(2,1)S(1)} %multiply_convert_fusion.5), channel_id=1, source_target_pairs={{0,1},{1,0},{2,3},{3,2},{4,5},{5,4},{6,7},{7,6},{8,9},{9,8},{10,11... | collective-permute-start | bytes 983048 | tf_op jit(solution)/shard_map/ppermute | solution.py:53
  47.8 15.3 %collective-permute-start.5 = (bf16[128,1280]{1,0:T(8,128)(2,1)S(1)}, bf16[128,1280]{1,0:T(8,128)(2,1)S(1)}, u32[]{:S(2)}, u32[]{:S(2)}) collective-permute-start(bf16[128,1280]{1,0:T(8,128)(2,1)S(1)} %multiply_convert_fusion.5), channel_id=1, source_target_pairs={{0,2},{1,3},{2,0},{3,1},{4,6},{5,7},{6,4},{7,5},{8,10},{9,11},{10,... | collective-permute-start | bytes 983048 | tf_op jit(solution)/shard_map/ppermute | solution.py:53
  49.5 15.2 %collective-permute-start.6 = (bf16[128,1280]{1,0:T(8,128)(2,1)S(1)}, bf16[128,1280]{1,0:T(8,128)(2,1)S(1)}, u32[]{:S(2)}, u32[]{:S(2)}) collective-permute-start(bf16[128,1280]{1,0:T(8,128)(2,1)S(1)} %multiply_convert_fusion.5), channel_id=1, source_target_pairs={{0,3},{1,2},{2,1},{3,0},{4,7},{5,6},{6,5},{7,4},{8,11},{9,10},{10,... | collective-permute-start | bytes 983048 | tf_op jit(solution)/shard_map/ppermute | solution.py:53
  64.9 23.5 %collective-permute-start.11 = (bf16[128,992]{1,0:T(8,128)(2,1)}, bf16[128,992]{1,0:T(8,128)(2,1)S(1)}, u32[]{:S(2)}, u32[]{:S(2)}) collective-permute-start(bf16[128,992]{1,0:T(8,128)(2,1)} %get-tuple-element.183), channel_id=1, source_target_pairs={{0,1},{1,0},{2,3},{3,2},{4,5},{5,4},{6,7},{7,6},{8,9},{9,8},{10,11... | collective-permute-start | bytes 761864 | tf_op jit(solution)/shard_map/ppermute | solution.py:53
  65.8 29.7 %collective-permute-start.12 = (bf16[128,992]{1,0:T(8,128)(2,1)}, bf16[128,992]{1,0:T(8,128)(2,1)S(1)}, u32[]{:S(2)}, u32[]{:S(2)}) collective-permute-start(bf16[128,992]{1,0:T(8,128)(2,1)} %get-tuple-element.182), channel_id=1, source_target_pairs={{0,2},{1,3},{2,0},{3,1},{4,6},{5,7},{6,4},{7,5},{8,10},{9,11},{10,... | collective-permute-start | bytes 761864 | tf_op jit(solution)/shard_map/ppermute | solution.py:53
  67.3 28.2 %collective-permute-start.13 = (bf16[128,992]{1,0:T(8,128)(2,1)}, bf16[128,992]{1,0:T(8,128)(2,1)S(1)}, u32[]{:S(2)}, u32[]{:S(2)}) collective-permute-start(bf16[128,992]{1,0:T(8,128)(2,1)} %get-tuple-element.181), channel_id=1, source_target_pairs={{0,3},{1,2},{2,1},{3,0},{4,7},{5,6},{6,5},{7,4},{8,11},{9,10},{10,... | collective-permute-start | bytes 761864 | tf_op jit(solution)/shard_map/ppermute | solution.py:53
  76.9 9.3 %collective-permute-start.10 = (bf16[256,768]{1,0:T(8,128)(2,1)S(1)}, bf16[256,768]{1,0:T(8,128)(2,1)S(1)}, u32[]{:S(2)}, u32[]{:S(2)}) collective-permute-start(bf16[256,768]{1,0:T(8,128)(2,1)S(1)} %pad_maximum_fusion.9), channel_id=1, source_target_pairs={{0,1},{1,0},{2,3},{3,2},{4,5},{5,4},{6,7},{7,6},{8,9},{9,8},{10,11... | collective-permute-start | bytes 1179656 | tf_op jit(solution)/shard_map/ppermute | solution.py:53
  77.7 9.1 %collective-permute-start.15 = (bf16[256,768]{1,0:T(8,128)(2,1)S(1)}, bf16[256,768]{1,0:T(8,128)(2,1)S(1)}, u32[]{:S(2)}, u32[]{:S(2)}) collective-permute-start(bf16[256,768]{1,0:T(8,128)(2,1)S(1)} %pad_maximum_fusion.10), channel_id=1, source_target_pairs={{0,2},{1,3},{2,0},{3,1},{4,6},{5,7},{6,4},{7,5},{8,10},{9,11},{10,... | collective-permute-start | bytes 1179656 | tf_op jit(solution)/shard_map/ppermute | solution.py:53
  86.2 18.5 %collective-permute-start.21 = (bf16[256,1152]{1,0:T(8,128)(2,1)S(1)}, bf16[256,1152]{1,0:T(8,128)(2,1)S(1)}, u32[]{:S(2)}, u32[]{:S(2)}) collective-permute-start(bf16[256,1152]{1,0:T(8,128)(2,1)S(1)} %pad_maximum_fusion.7), channel_id=1, source_target_pairs={{0,1},{1,0},{2,3},{3,2},{4,5},{5,4},{6,7},{7,6},{8,9},{9,8},{10,11... | collective-permute-start | bytes 1769480 | tf_op jit(solution)/shard_map/ppermute | solution.py:53
  87.0 6.9 %collective-permute-start.14 = (bf16[128,768]{1,0:T(8,128)(2,1)S(1)}, bf16[128,768]{1,0:T(8,128)(2,1)S(1)}, u32[]{:S(2)}, u32[]{:S(2)}) collective-permute-start(bf16[128,768]{1,0:T(8,128)(2,1)S(1)} %get-tuple-element.159), channel_id=1, source_target_pairs={{0,2},{1,3},{2,0},{3,1},{4,6},{5,7},{6,4},{7,5},{8,10},{9,11},{10,... | collective-permute-start | bytes 589832 | tf_op jit(solution)/shard_map/ppermute | solution.py:53
  88.4 14.7 %collective-permute-start.16 = (bf16[128,768]{1,0:T(8,128)(2,1)S(1)}, bf16[128,768]{1,0:T(8,128)(2,1)S(1)}, u32[]{:S(2)}, u32[]{:S(2)}) collective-permute-start(bf16[128,768]{1,0:T(8,128)(2,1)S(1)} %get-tuple-element.153), channel_id=1, source_target_pairs={{0,1},{1,0},{2,3},{3,2},{4,5},{5,4},{6,7},{7,6},{8,9},{9,8},{10,11... | collective-permute-start | bytes 589832 | tf_op jit(solution)/shard_map/ppermute | solution.py:53
  93.9 16.9 %collective-permute-start.25 = (bf16[256,1280]{1,0:T(8,128)(2,1)S(1)}, bf16[256,1280]{1,0:T(8,128)(2,1)}, u32[]{:S(2)}, u32[]{:S(2)}) collective-permute-start(bf16[256,1280]{1,0:T(8,128)(2,1)S(1)} %slice.329), channel_id=1, source_target_pairs={{0,2},{1,3},{2,0},{3,1},{4,6},{5,7},{6,4},{7,5},{8,10},{9,11},{10,... | collective-permute-start | bytes 1966088 | tf_op jit(solution)/shard_map/ppermute | solution.py:53
  103.6 16.7 %collective-permute-start.19 = (bf16[128,768]{1,0:T(8,128)(2,1)S(1)}, bf16[128,768]{1,0:T(8,128)(2,1)S(1)}, u32[]{:S(2)}, u32[]{:S(2)}) collective-permute-start(bf16[128,768]{1,0:T(8,128)(2,1)S(1)} %get-tuple-element.92), channel_id=1, source_target_pairs={{0,2},{1,3},{2,0},{3,1},{4,6},{5,7},{6,4},{7,5},{8,10},{9,11},{10,... | collective-permute-start | bytes 589832 | tf_op jit(solution)/shard_map/ppermute | solution.py:53
  104.1 15.2 %collective-permute-start.17 = (bf16[128,768]{1,0:T(8,128)(2,1)S(1)}, bf16[128,768]{1,0:T(8,128)(2,1)S(1)}, u32[]{:S(2)}, u32[]{:S(2)}) collective-permute-start(bf16[128,768]{1,0:T(8,128)(2,1)S(1)} %get-tuple-element.91), channel_id=1, source_target_pairs={{0,1},{1,0},{2,3},{3,2},{4,5},{5,4},{6,7},{7,6},{8,9},{9,8},{10,11... | collective-permute-start | bytes 589832 | tf_op jit(solution)/shard_map/ppermute | solution.py:53
  104.9 12.5 %collective-permute-start.22 = (bf16[128,1152]{1,0:T(8,128)(2,1)S(1)}, bf16[128,1152]{1,0:T(8,128)(2,1)S(1)}, u32[]{:S(2)}, u32[]{:S(2)}) collective-permute-start(bf16[128,1152]{1,0:T(8,128)(2,1)S(1)} %get-tuple-element.161), channel_id=1, source_target_pairs={{0,2},{1,3},{2,0},{3,1},{4,6},{5,7},{6,4},{7,5},{8,10},{9,11},{10,... | collective-permute-start | bytes 884744 | tf_op jit(solution)/shard_map/ppermute | solution.py:53
  112.0 10.4 %collective-permute-start.26 = (bf16[128,1280]{1,0:T(8,128)(2,1)S(1)}, bf16[128,1280]{1,0:T(8,128)(2,1)S(1)}, u32[]{:S(2)}, u32[]{:S(2)}) collective-permute-start(bf16[128,1280]{1,0:T(8,128)(2,1)S(1)} %get-tuple-element.157), channel_id=1, source_target_pairs={{0,1},{1,0},{2,3},{3,2},{4,5},{5,4},{6,7},{7,6},{8,9},{9,8},{10,11... | collective-permute-start | bytes 983048 | tf_op jit(solution)/shard_map/ppermute | solution.py:53
  117.8 10.8 %collective-permute-start.23 = (bf16[128,1152]{1,0:T(8,128)(2,1)S(1)}, bf16[128,1152]{1,0:T(8,128)(2,1)S(1)}, u32[]{:S(2)}, u32[]{:S(2)}) collective-permute-start(bf16[128,1152]{1,0:T(8,128)(2,1)S(1)} %loss.4), channel_id=1, source_target_pairs={{0,1},{1,0},{2,3},{3,2},{4,5},{5,4},{6,7},{7,6},{8,9},{9,8},{10,11... | collective-permute-start | bytes 884744 | tf_op jit(solution)/shard_map/ppermute | solution.py:53
  119.4 12.1 %collective-permute-start.18 = (bf16[256,768]{1,0:T(8,128)(2,1)S(1)}, bf16[256,768]{1,0:T(8,128)(2,1)S(1)}, u32[]{:S(2)}, u32[]{:S(2)}) collective-permute-start(bf16[256,768]{1,0:T(8,128)(2,1)S(1)} %pad_maximum_fusion.11), channel_id=1, source_target_pairs={{0,2},{1,3},{2,0},{3,1},{4,6},{5,7},{6,4},{7,5},{8,10},{9,11},{10,... | collective-permute-start | bytes 1179656 | tf_op jit(solution)/shard_map/ppermute | solution.py:53
  120.3 13.7 %collective-permute-start.20 = (bf16[256,768]{1,0:T(8,128)(2,1)S(1)}, bf16[256,768]{1,0:T(8,128)(2,1)S(1)}, u32[]{:S(2)}, u32[]{:S(2)}) collective-permute-start(bf16[256,768]{1,0:T(8,128)(2,1)S(1)} %pad_maximum_fusion.12), channel_id=1, source_target_pairs={{0,1},{1,0},{2,3},{3,2},{4,5},{5,4},{6,7},{7,6},{8,9},{9,8},{10,11... | collective-permute-start | bytes 1179656 | tf_op jit(solution)/shard_map/ppermute | solution.py:53
  123.0 15.6 %collective-permute-start.27 = (bf16[128,1280]{1,0:T(8,128)(2,1)S(1)}, bf16[128,1280]{1,0:T(8,128)(2,1)S(1)}, u32[]{:S(2)}, u32[]{:S(2)}) collective-permute-start(bf16[128,1280]{1,0:T(8,128)(2,1)S(1)} %loss.5), channel_id=1, source_target_pairs={{0,2},{1,3},{2,0},{3,1},{4,6},{5,7},{6,4},{7,5},{8,10},{9,11},{10,... | collective-permute-start | bytes 983048 | tf_op jit(solution)/shard_map/ppermute | solution.py:53
  128.7 16.7 %collective-permute-start.24 = (bf16[256,1152]{1,0:T(8,128)(2,1)S(1)}, bf16[256,1152]{1,0:T(8,128)(2,1)S(1)}, u32[]{:S(2)}, u32[]{:S(2)}) collective-permute-start(bf16[256,1152]{1,0:T(8,128)(2,1)S(1)} %pad_maximum_fusion.8), channel_id=1, source_target_pairs={{0,2},{1,3},{2,0},{3,1},{4,6},{5,7},{6,4},{7,5},{8,10},{9,11},{10,... | collective-permute-start | bytes 1769480 | tf_op jit(solution)/shard_map/ppermute | solution.py:53
  139.4 13.5 %collective-permute-start.28 = (bf16[256,1280]{1,0:T(8,128)(2,1)}, bf16[256,1280]{1,0:T(8,128)(2,1)S(1)}, u32[]{:S(2)}, u32[]{:S(2)}) collective-permute-start(bf16[256,1280]{1,0:T(8,128)(2,1)} %pad_maximum_fusion.6), channel_id=1, source_target_pairs={{0,1},{1,0},{2,3},{3,2},{4,5},{5,4},{6,7},{7,6},{8,9},{9,8},{10,11... | collective-permute-start | bytes 1966088 | tf_op jit(solution)/shard_map/ppermute | solution.py:53
  160.1 15.3 %collective-permute-start.32 = (bf16[4,160,1280]{2,1,0:T(8,128)(2,1)}, bf16[4,160,1280]{2,1,0:T(8,128)(2,1)}, u32[]{:S(2)}, u32[]{:S(2)}) collective-permute-start(bf16[4,160,1280]{2,1,0:T(8,128)(2,1)} %get-tuple-element.105), channel_id=1, source_target_pairs={{0,4},{4,0},{8,12},{12,8},{16,20},{20,16},{24,28},{28,24},{1,5},{5... | collective-permute-start | bytes 4915208 | tf_op jit(solution)/shard_map/ppermute | solution.py:53
  161.6 13.7 %collective-permute-start.31 = (bf16[2,192,640]{2,1,0:T(8,128)(2,1)S(1)}, bf16[2,192,640]{2,1,0:T(8,128)(2,1)S(1)}, u32[]{:S(2)}, u32[]{:S(2)}) collective-permute-start(bf16[2,192,640]{2,1,0:T(8,128)(2,1)S(1)} %slice.330), channel_id=1, source_target_pairs={{0,8},{4,12},{8,0},{12,4},{16,24},{20,28},{24,16},{28,20},{1,9},{5... | collective-permute-start | bytes 1474568 | tf_op jit(solution)/shard_map/ppermute | solution.py:53
  164.1 10.5 %collective-permute-start.30 = (bf16[128,1280]{1,0:T(8,128)(2,1)S(1)}, bf16[128,1280]{1,0:T(8,128)(2,1)S(1)}, u32[]{:S(2)}, u32[]{:S(2)}) collective-permute-start(bf16[128,1280]{1,0:T(8,128)(2,1)S(1)} %get-tuple-element.169), channel_id=1, source_target_pairs={{0,1},{1,0},{2,3},{3,2},{4,5},{5,4},{6,7},{7,6},{8,9},{9,8},{10,11... | collective-permute-start | bytes 983048 | tf_op jit(solution)/shard_map/ppermute | solution.py:53
  164.8 16.5 %collective-permute-start.33 = (bf16[128,1280]{1,0:T(8,128)(2,1)}, bf16[128,1280]{1,0:T(8,128)(2,1)S(1)}, u32[]{:S(2)}, u32[]{:S(2)}) collective-permute-start(bf16[128,1280]{1,0:T(8,128)(2,1)} %get-tuple-element.171), channel_id=1, source_target_pairs={{0,2},{1,3},{2,0},{3,1},{4,6},{5,7},{6,4},{7,5},{8,10},{9,11},{10,... | collective-permute-start | bytes 983048 | tf_op jit(solution)/shard_map/ppermute | solution.py:53
  165.5 15.8 %collective-permute-start.34 = (bf16[128,1280]{1,0:T(8,128)(2,1)}, bf16[128,1280]{1,0:T(8,128)(2,1)S(1)}, u32[]{:S(2)}, u32[]{:S(2)}) collective-permute-start(bf16[128,1280]{1,0:T(8,128)(2,1)} %get-tuple-element.170), channel_id=1, source_target_pairs={{0,3},{1,2},{2,1},{3,0},{4,7},{5,6},{6,5},{7,4},{8,11},{9,10},{10,... | collective-permute-start | bytes 983048 | tf_op jit(solution)/shard_map/ppermute | solution.py:53
  177.3 19.9 %collective-permute-start.39 = (bf16[2,160,1280]{2,1,0:T(8,128)(2,1)S(1)}, bf16[2,160,1280]{2,1,0:T(8,128)(2,1)S(1)}, u32[]{:S(2)}, u32[]{:S(2)}) collective-permute-start(bf16[2,160,1280]{2,1,0:T(8,128)(2,1)S(1)} %slice.328), channel_id=1, source_target_pairs={{0,8},{4,12},{8,0},{12,4},{16,24},{20,28},{24,16},{28,20},{1,9},{5... | collective-permute-start | bytes 2457608 | tf_op jit(solution)/shard_map/ppermute | solution.py:53
  182.9 11.7 %collective-permute-start.37 = (bf16[128,1280]{1,0:T(8,128)(2,1)S(1)}, bf16[128,1280]{1,0:T(8,128)(2,1)S(1)}, u32[]{:S(2)}, u32[]{:S(2)}) collective-permute-start(bf16[128,1280]{1,0:T(8,128)(2,1)S(1)} %multiply_convert_fusion.4), channel_id=1, source_target_pairs={{0,3},{1,2},{2,1},{3,0},{4,7},{5,6},{6,5},{7,4},{8,11},{9,10},{10,... | collective-permute-start | bytes 983048 | tf_op jit(solution)/shard_map/ppermute | solution.py:53
  184.4 15.3 %collective-permute-start.35 = (bf16[128,1280]{1,0:T(8,128)(2,1)S(1)}, bf16[128,1280]{1,0:T(8,128)(2,1)}, u32[]{:S(2)}, u32[]{:S(2)}) collective-permute-start(bf16[128,1280]{1,0:T(8,128)(2,1)S(1)} %multiply_convert_fusion.4), channel_id=1, source_target_pairs={{0,1},{1,0},{2,3},{3,2},{4,5},{5,4},{6,7},{7,6},{8,9},{9,8},{10,11... | collective-permute-start | bytes 983048 | tf_op jit(solution)/shard_map/ppermute | solution.py:53
  185.6 14.2 %collective-permute-start.36 = (bf16[128,1280]{1,0:T(8,128)(2,1)S(1)}, bf16[128,1280]{1,0:T(8,128)(2,1)}, u32[]{:S(2)}, u32[]{:S(2)}) collective-permute-start(bf16[128,1280]{1,0:T(8,128)(2,1)S(1)} %multiply_convert_fusion.4), channel_id=1, source_target_pairs={{0,2},{1,3},{2,0},{3,1},{4,6},{5,7},{6,4},{7,5},{8,10},{9,11},{10,... | collective-permute-start | bytes 983048 | tf_op jit(solution)/shard_map/ppermute | solution.py:53
  207.6 8.5 %collective-permute-start.43 = (bf16[2,160,128]{2,1,0:T(8,128)(2,1)S(1)}, bf16[2,160,128]{2,1,0:T(8,128)(2,1)S(1)}, u32[]{:S(2)}, u32[]{:S(2)}) collective-permute-start(bf16[2,160,128]{2,1,0:T(8,128)(2,1)S(1)} %pad_maximum_fusion.18), channel_id=1, source_target_pairs={{0,24},{4,28},{8,16},{12,20},{16,8},{20,12},{24,0},{28,4},{1,25},{... | collective-permute-start | bytes 245768 | tf_op jit(solution)/shard_map/ppermute | solution.py:53
  210.2 17.5 %collective-permute-start.42 = (bf16[2,160,128]{2,1,0:T(8,128)(2,1)S(1)}, bf16[2,160,128]{2,1,0:T(8,128)(2,1)S(1)}, u32[]{:S(2)}, u32[]{:S(2)}) collective-permute-start(bf16[2,160,128]{2,1,0:T(8,128)(2,1)S(1)} %pad_maximum_fusion.17), channel_id=1, source_target_pairs={{0,16},{4,20},{8,24},{12,28},{16,0},{20,4},{24,8},{28,12},{1,17},{... | collective-permute-start | bytes 245768 | tf_op jit(solution)/shard_map/ppermute | solution.py:53
  210.4 17.3 %collective-permute-start.41 = (bf16[2,160,128]{2,1,0:T(8,128)(2,1)S(1)}, bf16[2,160,128]{2,1,0:T(8,128)(2,1)S(1)}, u32[]{:S(2)}, u32[]{:S(2)}) collective-permute-start(bf16[2,160,128]{2,1,0:T(8,128)(2,1)S(1)} %pad_maximum_fusion.16), channel_id=1, source_target_pairs={{0,8},{4,12},{8,0},{12,4},{16,24},{20,28},{24,16},{28,20},{1,9},{5... | collective-permute-start | bytes 245768 | tf_op jit(solution)/shard_map/ppermute | solution.py:53
  212.4 24.0 %collective-permute-start.45 = (bf16[1,160,1280]{2,1,0:T(8,128)(2,1)S(1)}, bf16[1,160,1280]{2,1,0:T(8,128)(2,1)S(1)}, u32[]{:S(2)}, u32[]{:S(2)}) collective-permute-start(bf16[1,160,1280]{2,1,0:T(8,128)(2,1)S(1)} %slice.331), channel_id=1, source_target_pairs={{0,16},{4,20},{8,24},{12,28},{16,0},{20,4},{24,8},{28,12},{1,17},{... | collective-permute-start | bytes 1228808 | tf_op jit(solution)/shard_map/ppermute | solution.py:53
  214.6 34.7 %collective-permute-start.44 = (bf16[2,160,1280]{2,1,0:T(8,128)(2,1)S(1)}, bf16[2,160,1280]{2,1,0:T(8,128)(2,1)S(1)}, u32[]{:S(2)}, u32[]{:S(2)}) collective-permute-start(bf16[2,160,1280]{2,1,0:T(8,128)(2,1)S(1)} %get-tuple-element.121), channel_id=1, source_target_pairs={{0,8},{4,12},{8,0},{12,4},{16,24},{20,28},{24,16},{28,20},{1,9},{5... | collective-permute-start | bytes 2457608 | tf_op jit(solution)/shard_map/ppermute | solution.py:53
  227.8 10.7 %collective-permute-start.46 = (bf16[8,160,128]{2,1,0:T(8,128)(2,1)S(1)}, bf16[8,160,128]{2,1,0:T(8,128)(2,1)S(1)}, u32[]{:S(2)}, u32[]{:S(2)}) collective-permute-start(bf16[8,160,128]{2,1,0:T(8,128)(2,1)S(1)} %constant_dynamic-update-slice_fusion.3.refs_0_), channel_id=1, source_target_pairs={{0,1},{1,0},{2,3},{3,2},{4,5},{5,4},{6,7},{7,6},{8,9},{9,8},{10,11... | collective-permute-start | bytes 983048 | tf_op jit(solution)/shard_map/ppermute | solution.py:53
  229.5 16.0 %collective-permute-start.47 = (bf16[8,160,128]{2,1,0:T(8,128)(2,1)S(1)}, bf16[8,160,128]{2,1,0:T(8,128)(2,1)S(1)}, u32[]{:S(2)}, u32[]{:S(2)}) collective-permute-start(bf16[8,160,128]{2,1,0:T(8,128)(2,1)S(1)} %constant_dynamic-update-slice_fusion.3.refs_0_), channel_id=1, source_target_pairs={{0,2},{1,3},{2,0},{3,1},{4,6},{5,7},{6,4},{7,5},{8,10},{9,11},{10,... | collective-permute-start | bytes 983048 | tf_op jit(solution)/shard_map/ppermute | solution.py:53
  230.1 15.4 %collective-permute-start.48 = (bf16[8,160,128]{2,1,0:T(8,128)(2,1)S(1)}, bf16[8,160,128]{2,1,0:T(8,128)(2,1)S(1)}, u32[]{:S(2)}, u32[]{:S(2)}) collective-permute-start(bf16[8,160,128]{2,1,0:T(8,128)(2,1)S(1)} %constant_dynamic-update-slice_fusion.3.refs_0_), channel_id=1, source_target_pairs={{0,3},{1,2},{2,1},{3,0},{4,7},{5,6},{6,5},{7,4},{8,11},{9,10},{10,... | collective-permute-start | bytes 983048 | tf_op jit(solution)/shard_map/ppermute | solution.py:53
  236.3 22.3 %collective-permute-start.50 = (bf16[1,192,640]{2,1,0:T(8,128)(2,1)S(1)}, bf16[1,192,640]{2,1,0:T(8,128)(2,1)S(1)}, u32[]{:S(2)}, u32[]{:S(2)}) collective-permute-start(bf16[1,192,640]{2,1,0:T(8,128)(2,1)S(1)} %slice.332), channel_id=1, source_target_pairs={{0,16},{4,20},{8,24},{12,28},{16,0},{20,4},{24,8},{28,12},{1,17},{... | collective-permute-start | bytes 737288 | tf_op jit(solution)/shard_map/ppermute | solution.py:53
  249.5 20.3 %collective-permute-start.49 = (bf16[1,160,1280]{2,1,0:T(8,128)(2,1)S(1)}, bf16[1,160,1280]{2,1,0:T(8,128)(2,1)S(1)}, u32[]{:S(2)}, u32[]{:S(2)}) collective-permute-start(bf16[1,160,1280]{2,1,0:T(8,128)(2,1)S(1)} %get-tuple-element.129), channel_id=1, source_target_pairs={{0,16},{4,20},{8,24},{12,28},{16,0},{20,4},{24,8},{28,12},{1,17},{... | collective-permute-start | bytes 1228808 | tf_op jit(solution)/shard_map/ppermute | solution.py:53
  (36 other events, 215.6 us)
Sparse Core Ops, SparseCore 0:
  65.0 99.9 all-gather.2

commit v4 on v3

--- a/solution.py
+++ b/solution.py
@@ -523,7 +523,7 @@
 
     mine, *inners = pin(upstream[0], *inners)
     of_rest = begin(
-        product([([final], inners), (slopes[2], lifteds[2:])], groups, group)
+        product([([final], inners), (slopes[2], lifteds[2:])], groups, group, 2**35)
     )
     came[0], one, two = pin(came[0], of_heads[1], of_rest[1])
     of_heads = arrive(of_heads, one)

time: 278 us -> 278 us (level)
  transfers between devices with their start and end apart: 52 -> 52, of which waited for: 30 -> 31; matrix products, arithmetic and copies ran while one was open for 12% -> 11% of each run, Pallas kernels for 8% -> 8%
where the time goes in v4:
time: 278 us; the launch traced here: 277 us
  waiting for transfers between devices  123 us (44%)
  starting transfers between devices  58.8 us (21%)
  matrix products  30.5 us (11%)
  Pallas kernels  25.2 us (9%)
  between operations  15 us (5%)
  local copies, waits for them, and re-layouts  12.2 us (4%)
  other arithmetic  12 us (4%)
    ppermute x51, waiting for transfers between devices, swap(): return lax.ppermute(value, axis, [(i, i ^ offset) for i in range(count)])  123 us
    ppermute x51, starting transfers between devices, swap(): return lax.ppermute(value, axis, [(i, i ^ offset) for i in range(count)])  58.8 us
    pallas_call x3, Pallas kernels, product(): pl.pallas_call(functools.partial(product_kernel, groups, [(len(l), len(r)...  9.41 us
    pallas_call x1, Pallas kernels, narrow_sum(): pl.pallas_call(functools.partial(narrow_kernel, len(columns)), out_shape=...  8.81 us
    dot_general x3, matrix products, local(): before = jnp.dot(final, adaptor_in[index], **exact)  7.39 us
  transfers between devices with their start and end apart: 52, of which 31 were waited for; matrix products, arithmetic and copies ran while one was open for 11% of the time, Pallas kernels for 8%

profile of v4, /device:TPU:0, one launch (start us, length us, event | category | flops | bytes accessed | tf_op | source)
XLA Modules:
  0.0 277.3 jit_solution(8126452456835294617)
XLA Ops:
  10.0 5.0 %fusion.10 = (f32[512,1280]{1,0:T(8,128)}, bf16[512,1280]{1,0:T(8,128)(2,1)}) fusion(bf16[512,1280]{1,0:T(8,128)(2,1)S(1)} %fusion.5.refs_0_, bf16[1280,1280]{1,0:T(8,128)(2,1)S(1)} %copy-done), kind=kOutput, calls=%fused_computation.18 | convolution fusion | flops 1690173440 | bytes 8519680 | tf_op jit(solution)/shard_map/dot_general | solution.py:439
  15.0 4.2 %fusion.78 = f32[512,1280]{1,0:T(8,128)S(1)} fusion(bf16[512,1280]{1,0:T(8,128)(2,1)} %get-tuple-element.110, bf16[1280,1280]{1,0:T(8,128)(2,1)} %param.17), kind=kOutput, calls=%fused_computation.192 | convolution fusion | flops 1677721600 | bytes 7208960 | tf_op jit(solution)/shard_map/dot_general | solution.py:441
  21.6 2.9 %collective-permute-start = (bf16[128,1280]{1,0:T(8,128)(2,1)}, bf16[128,1280]{1,0:T(8,128)(2,1)}, u32[]{:S(2)}, u32[]{:S(2)}) collective-permute-start(bf16[128,1280]{1,0:T(8,128)(2,1)} %get-tuple-element.172), channel_id=1, source_target_pairs={{0,1},{1,0},{2,3},{3,2},{4,5},{5,4},{6,7},{7,6},{8,9},{9,8},{10,11... | collective-permute-start | bytes 983048 | tf_op jit(solution)/shard_map/ppermute | solution.py:53
  24.6 3.5 %pack.1 = (bf16[256,992]{1,0:T(8,128)(2,1)S(1)}, bf16[256,992]{1,0:T(8,128)(2,1)S(1)}) custom-call(s32[3]{0:T(128)S(1)} %copy-done.8, s32[128]{0:T(128)S(1)} %copy-done.7, s32[1]{0:T(128)} %bitcast.10.group_ref, bf16[2,512,384]{2,1,0:T(8,128)(2,1)S(1)} %copy-done.4, bf16[2,288,512]{2,1,0:T(8,128)(2,1)S(1)} %bitcast.133, bf16[2,320,512]{2,1,0:T(8,128)(2,1)S(1)} %bitcast.132), custom_call_target="tpu_custom_call" | custom-call | tf_op jit(solution)/shard_map/pack/pallas_call | solution.py:173
  30.7 2.3 collective-permute-done
  34.6 2.6 collective-permute-start.8
  37.6 7.9 %collective-permute-done.2 = bf16[128,1280]{1,0:T(8,128)(2,1)S(1)} collective-permute-done((bf16[128,1280]{1,0:T(8,128)(2,1)}, bf16[128,1280]{1,0:T(8,128)(2,1)S(1)}, u32[]{:S(2)}, u32[]{:S(2)}) %collective-permute-start.2) | collective-permute-done | bytes 327712 | tf_op jit(solution)/shard_map/ppermute | solution.py:53
  47.8 1.8 collective-permute-start.5
  51.1 4.9 %collective-permute-done.8.refs_2_ = bf16[128,992]{1,0:T(8,128)(2,1)S(1)} collective-permute-done((bf16[128,992]{1,0:T(8,128)(2,1)S(1)}, bf16[128,992]{1,0:T(8,128)(2,1)S(1)}, u32[]{:S(2)}, u32[]{:S(2)}) %collective-permute-start.8) | collective-permute-done | bytes 253984 | tf_op jit(solution)/shard_map/ppermute | solution.py:53
  58.1 5.0 %collective-permute-done.5 = bf16[128,1280]{1,0:T(8,128)(2,1)S(1)} collective-permute-done((bf16[128,1280]{1,0:T(8,128)(2,1)S(1)}, bf16[128,1280]{1,0:T(8,128)(2,1)S(1)}, u32[]{:S(2)}, u32[]{:S(2)}) %collective-permute-start.5) | collective-permute-done | bytes 327712 | tf_op jit(solution)/shard_map/ppermute | solution.py:53
  68.4 3.2 %fusion.36 = (f32[512,320]{1,0:T(8,128)}, bf16[512,320]{1,0:T(8,128)(2,1)S(1)}) fusion(bf16[512,1280]{1,0:T(8,128)(2,1)S(1)} %pad_maximum_fusion.1.refs_0_, bf16[3,1280,320]{1,2,0:T(8,128)(2,1)} %param.19), kind=kOutput, calls=%fused_computation.72 | convolution fusion | flops 422543360 | bytes 3112960 | tf_op jit(solution)/shard_map/dot_general | solution.py:478
  73.6 2.1 multiply_convert_fusion.2
  79.4 2.1 multiply_convert_fusion.1
  81.5 4.7 %collective-permute-done.10 = bf16[256,768]{1,0:T(8,128)(2,1)S(1)} collective-permute-done((bf16[256,768]{1,0:T(8,128)(2,1)S(1)}, bf16[256,768]{1,0:T(8,128)(2,1)S(1)}, u32[]{:S(2)}, u32[]{:S(2)}) %collective-permute-start.10) | collective-permute-done | bytes 393248 | tf_op jit(solution)/shard_map/ppermute | solution.py:53
  90.0 3.8 %collective-permute-done.14.refs_5_ = bf16[128,768]{1,0:T(8,128)(2,1)S(1)} collective-permute-done((bf16[128,768]{1,0:T(8,128)(2,1)S(1)}, bf16[128,768]{1,0:T(8,128)(2,1)S(1)}, u32[]{:S(2)}, u32[]{:S(2)}) %collective-permute-start.14) | collective-permute-done | bytes 196640 | tf_op jit(solution)/shard_map/ppermute | solution.py:53
  95.5 7.7 %collective-permute-done.16.refs_7_ = bf16[128,768]{1,0:T(8,128)(2,1)S(1)} collective-permute-done((bf16[128,768]{1,0:T(8,128)(2,1)S(1)}, bf16[128,768]{1,0:T(8,128)(2,1)S(1)}, u32[]{:S(2)}, u32[]{:S(2)}) %collective-permute-start.16) | collective-permute-done | bytes 196640 | tf_op jit(solution)/shard_map/ppermute | solution.py:53
  104.8 1.8 collective-permute-start.22
  106.6 4.1 %collective-permute-done.25 = bf16[256,1280]{1,0:T(8,128)(2,1)S(1)} collective-permute-done((bf16[256,1280]{1,0:T(8,128)(2,1)S(1)}, bf16[256,1280]{1,0:T(8,128)(2,1)S(1)}, u32[]{:S(2)}, u32[]{:S(2)}) %collective-permute-start.25) | collective-permute-done | bytes 655392 | tf_op jit(solution)/shard_map/ppermute | solution.py:53
  110.7 2.2 collective-permute-start.26
  113.0 4.3 %collective-permute-done.22.refs_5_ = bf16[128,1152]{1,0:T(8,128)(2,1)S(1)} collective-permute-done((bf16[128,1152]{1,0:T(8,128)(2,1)S(1)}, bf16[128,1152]{1,0:T(8,128)(2,1)S(1)}, u32[]{:S(2)}, u32[]{:S(2)}) %collective-permute-start.22) | collective-permute-done | bytes 294944 | tf_op jit(solution)/shard_map/ppermute | solution.py:53
  120.4 2.1 collective-permute-start.20
  124.0 3.8 %collective-permute-done.23 = bf16[128,1152]{1,0:T(8,128)(2,1)S(1)} collective-permute-done((bf16[128,1152]{1,0:T(8,128)(2,1)S(1)}, bf16[128,1152]{1,0:T(8,128)(2,1)S(1)}, u32[]{:S(2)}, u32[]{:S(2)}) %collective-permute-start.23) | collective-permute-done | bytes 294944 | tf_op jit(solution)/shard_map/ppermute | solution.py:53
  127.8 2.5 collective-permute-start.24
  134.1 2.2 fusion.28
  136.3 2.2 collective-permute-done.27
  140.3 5.1 %collective-permute-done.24 = bf16[256,1152]{1,0:T(8,128)(2,1)S(1)} collective-permute-done((bf16[256,1152]{1,0:T(8,128)(2,1)S(1)}, bf16[256,1152]{1,0:T(8,128)(2,1)S(1)}, u32[]{:S(2)}, u32[]{:S(2)}) %collective-permute-start.24) | collective-permute-done | bytes 589856 | tf_op jit(solution)/shard_map/ppermute | solution.py:53
  145.5 2.3 product.3
  155.6 4.3 %product.4 = (bf16[4,160,1280]{2,1,0:T(8,128)(2,1)S(1)}, bf16[4,160,1280]{2,1,0:T(8,128)(2,1)}) custom-call(s32[2]{0:T(128)S(1)} %pad_add_fusion.spot_ref, bf16[512,1280]{1,0:T(8,128)(2,1)S(1)} %pad_maximum_fusion.1.refs_0_, bf16[512,320]{1,0:T(8,128)(2,1)S(1)} %fusion.20.refs_1_, bf16[512,320]{1,0:T(8,128)(2,1)S(1)} %fusion.21.refs_2_, ...), custom_call_target="tpu_custom_call" | custom-call | flops 34359738368 | tf_op jit(solution)/shard_map/product/pallas_call | solution.py:269
  161.5 1.7 collective-permute-start.31
  164.1 1.7 collective-permute-start.30
  167.5 7.3 %collective-permute-done.30 = bf16[128,1280]{1,0:T(8,128)(2,1)S(1)} collective-permute-done((bf16[128,1280]{1,0:T(8,128)(2,1)}, bf16[128,1280]{1,0:T(8,128)(2,1)S(1)}, u32[]{:S(2)}, u32[]{:S(2)}) %collective-permute-start.30) | collective-permute-done | bytes 327712 | tf_op jit(solution)/shard_map/ppermute | solution.py:53
  175.5 1.9 convert_add_fusion
  178.9 3.7 %collective-permute-done.33 = bf16[128,1280]{1,0:T(8,128)(2,1)S(1)} collective-permute-done((bf16[128,1280]{1,0:T(8,128)(2,1)}, bf16[128,1280]{1,0:T(8,128)(2,1)S(1)}, u32[]{:S(2)}, u32[]{:S(2)}) %collective-permute-start.33) | collective-permute-done | bytes 327712 | tf_op jit(solution)/shard_map/ppermute | solution.py:53
  188.6 6.3 %collective-permute-done.37 = bf16[128,1280]{1,0:T(8,128)(2,1)S(1)} collective-permute-done((bf16[128,1280]{1,0:T(8,128)(2,1)S(1)}, bf16[128,1280]{1,0:T(8,128)(2,1)S(1)}, u32[]{:S(2)}, u32[]{:S(2)}) %collective-permute-start.37) | collective-permute-done | bytes 327712 | tf_op jit(solution)/shard_map/ppermute | solution.py:53
  194.9 2.3 collective-permute-done.39
  197.2 1.6 collective-permute-done.35
  199.6 4.6 %fusion.2.refs_1_ = bf16[512,1280]{1,0:T(8,128)(2,1)S(1)} fusion(f32[512,1280]{1,0:T(8,128)} %get-tuple-element.112, bf16[1280,1280]{1,0:T(8,128)(2,1)} %param.17, bf16[128,1280]{1,0:T(8,128)(2,1)S(1)} %collective-permute-done.37, bf16[128,1280]{1,0:T(8,128)(2,1)S(1)} %collective-permute-done.36, bf16[128,1280]{1,0:T(8,128)(2,1)S(1)} %collective-permute-done.35, ...), kind=kOutput, calls=%fused_computation.10 | convolution fusion | flops 1684275200 | bytes 8519680 | tf_op jit(solution)/shard_map/rd,fd->rf/dot_general | solution.py:546
  204.3 2.8 %product.5 = (bf16[4,160,1280]{2,1,0:T(8,128)(2,1)S(1)}, bf16[4,160,1280]{2,1,0:T(8,128)(2,1)S(1)}) custom-call(s32[2]{0:T(128)S(1)} %pad_add_fusion.spot_ref, bf16[512,1280]{1,0:T(8,128)(2,1)S(1)} %copy-done.3, bf16[512,1280]{1,0:T(8,128)(2,1)S(1)} %fusion.2.refs_1_), custom_call_target="tpu_custom_call" | custom-call | flops 34359738368 | tf_op jit(solution)/shard_map/product/pallas_call | solution.py:269
  207.2 2.7 collective-permute-start.43
  210.2 1.7 collective-permute-start.41
  213.2 1.9 collective-permute-start.45
  216.9 10.6 %collective-permute-done.42 = bf16[2,160,128]{2,1,0:T(8,128)(2,1)S(1)} collective-permute-done((bf16[2,160,128]{2,1,0:T(8,128)(2,1)S(1)}, bf16[2,160,128]{2,1,0:T(8,128)(2,1)S(1)}, u32[]{:S(2)}, u32[]{:S(2)}) %collective-permute-start.42) | collective-permute-done | bytes 81952 | tf_op jit(solution)/shard_map/ppermute | solution.py:53
  231.4 4.7 %collective-permute-done.45.refs_3_ = bf16[1,160,1280]{2,1,0:T(8,128)(2,1)S(1)} collective-permute-done((bf16[1,160,1280]{2,1,0:T(8,128)(2,1)S(1)}, bf16[1,160,1280]{2,1,0:T(8,128)(2,1)S(1)}, u32[]{:S(2)}, u32[]{:S(2)}) %collective-permute-start.45) | collective-permute-done | bytes 409632 | tf_op jit(solution)/shard_map/ppermute | solution.py:53
  236.1 2.2 collective-permute-done.46.refs_1_
  238.3 6.1 %collective-permute-done.47.refs_2_ = bf16[8,160,128]{2,1,0:T(8,128)(2,1)S(1)} collective-permute-done((bf16[8,160,128]{2,1,0:T(8,128)(2,1)S(1)}, bf16[8,160,128]{2,1,0:T(8,128)(2,1)S(1)}, u32[]{:S(2)}, u32[]{:S(2)}) %collective-permute-start.47) | collective-permute-done | bytes 327712 | tf_op jit(solution)/shard_map/ppermute | solution.py:53
  244.4 6.0 %collective-permute-done.44.came_ref = bf16[2,160,1280]{2,1,0:T(8,128)(2,1)S(1)} collective-permute-done((bf16[2,160,1280]{2,1,0:T(8,128)(2,1)S(1)}, bf16[2,160,1280]{2,1,0:T(8,128)(2,1)S(1)}, u32[]{:S(2)}, u32[]{:S(2)}) %collective-permute-start.44) | collective-permute-done | bytes 819232 | tf_op jit(solution)/shard_map/ppermute | solution.py:53
  250.6 8.8 %narrow.1 = f32[160,1280]{1,0:T(8,128)} custom-call(s32[1]{0:T(128)} %bitcast.10.group_ref, bf16[8,512,1280]{2,1,0:T(8,128)(2,1)} %bitcast.151, bf16[8,160,128]{2,1,0:T(8,128)(2,1)S(1)} %constant_dynamic-update-slice_fusion.3.refs_0_, bf16[8,160,128]{2,1,0:T(8,128)(2,1)S(1)} %collective-permute-done.46.refs_1_, ...), custom_call_target="tpu_custom_call" | custom-call | flops 34359738368 | tf_op jit(solution)/shard_map/narrow/pallas_call | solution.py:296
  261.3 8.1 %collective-permute-done.49 = bf16[1,160,1280]{2,1,0:T(8,128)(2,1)S(1)} collective-permute-done((bf16[1,160,1280]{2,1,0:T(8,128)(2,1)S(1)}, bf16[1,160,1280]{2,1,0:T(8,128)(2,1)S(1)}, u32[]{:S(2)}, u32[]{:S(2)}) %collective-permute-start.49) | collective-permute-done | bytes 409632 | tf_op jit(solution)/shard_map/ppermute | solution.py:53
  (237 shorter events, 75.0 us)
Async XLA Ops:
  7.2 190.1 %all-gather.3.cloned.1.call-start = ((), (), s32[]{:S(2)}) async-start(), calls=%async_computation | async-start | bytes 11796480 | tf_op jit(solution)/shard_map/all_gather | solution.py:470
  21.6 11.4 %collective-permute-start = (bf16[128,1280]{1,0:T(8,128)(2,1)}, bf16[128,1280]{1,0:T(8,128)(2,1)}, u32[]{:S(2)}, u32[]{:S(2)}) collective-permute-start(bf16[128,1280]{1,0:T(8,128)(2,1)} %get-tuple-element.172), channel_id=1, source_target_pairs={{0,1},{1,0},{2,3},{3,2},{4,5},{5,4},{6,7},{7,6},{8,9},{9,8},{10,11... | collective-permute-start | bytes 983048 | tf_op jit(solution)/shard_map/ppermute | solution.py:53
  28.1 17.4 %collective-permute-start.2 = (bf16[128,1280]{1,0:T(8,128)(2,1)}, bf16[128,1280]{1,0:T(8,128)(2,1)S(1)}, u32[]{:S(2)}, u32[]{:S(2)}) collective-permute-start(bf16[128,1280]{1,0:T(8,128)(2,1)} %get-tuple-element.174), channel_id=1, source_target_pairs={{0,2},{1,3},{2,0},{3,1},{4,6},{5,7},{6,4},{7,5},{8,10},{9,11},{10,... | collective-permute-start | bytes 983048 | tf_op jit(solution)/shard_map/ppermute | solution.py:53
  29.7 15.8 %collective-permute-start.3 = (bf16[128,1280]{1,0:T(8,128)(2,1)}, bf16[128,1280]{1,0:T(8,128)(2,1)S(1)}, u32[]{:S(2)}, u32[]{:S(2)}) collective-permute-start(bf16[128,1280]{1,0:T(8,128)(2,1)} %get-tuple-element.173), channel_id=1, source_target_pairs={{0,3},{1,2},{2,1},{3,0},{4,7},{5,6},{6,5},{7,4},{8,11},{9,10},{10,... | collective-permute-start | bytes 983048 | tf_op jit(solution)/shard_map/ppermute | solution.py:53
  33.1 16.4 %collective-permute-start.7 = (bf16[128,992]{1,0:T(8,128)(2,1)S(1)}, bf16[128,992]{1,0:T(8,128)(2,1)S(1)}, u32[]{:S(2)}, u32[]{:S(2)}) collective-permute-start(bf16[128,992]{1,0:T(8,128)(2,1)S(1)} %bitcast.150), channel_id=1, source_target_pairs={{0,8},{4,12},{8,0},{12,4},{16,24},{20,28},{24,16},{28,20},{1,9},{5... | collective-permute-start | bytes 761864 | tf_op jit(solution)/shard_map/ppermute | solution.py:53
  34.6 21.4 %collective-permute-start.8 = (bf16[128,992]{1,0:T(8,128)(2,1)S(1)}, bf16[128,992]{1,0:T(8,128)(2,1)S(1)}, u32[]{:S(2)}, u32[]{:S(2)}) collective-permute-start(bf16[128,992]{1,0:T(8,128)(2,1)S(1)} %bitcast.149), channel_id=1, source_target_pairs={{0,16},{4,20},{8,24},{12,28},{16,0},{20,4},{24,8},{28,12},{1,17},{... | collective-permute-start | bytes 761864 | tf_op jit(solution)/shard_map/ppermute | solution.py:53
  37.2 18.8 %collective-permute-start.9 = (bf16[128,992]{1,0:T(8,128)(2,1)S(1)}, bf16[128,992]{1,0:T(8,128)(2,1)S(1)}, u32[]{:S(2)}, u32[]{:S(2)}) collective-permute-start(bf16[128,992]{1,0:T(8,128)(2,1)S(1)} %bitcast.148), channel_id=1, source_target_pairs={{0,24},{4,28},{8,16},{12,20},{16,8},{20,12},{24,0},{28,4},{1,25},{... | collective-permute-start | bytes 761864 | tf_op jit(solution)/shard_map/ppermute | solution.py:53
  47.4 10.7 %collective-permute-start.4 = (bf16[128,1280]{1,0:T(8,128)(2,1)S(1)}, bf16[128,1280]{1,0:T(8,128)(2,1)S(1)}, u32[]{:S(2)}, u32[]{:S(2)}) collective-permute-start(bf16[128,1280]{1,0:T(8,128)(2,1)S(1)} %multiply_convert_fusion.5), channel_id=1, source_target_pairs={{0,1},{1,0},{2,3},{3,2},{4,5},{5,4},{6,7},{7,6},{8,9},{9,8},{10,11... | collective-permute-start | bytes 983048 | tf_op jit(solution)/shard_map/ppermute | solution.py:53
  47.8 15.3 %collective-permute-start.5 = (bf16[128,1280]{1,0:T(8,128)(2,1)S(1)}, bf16[128,1280]{1,0:T(8,128)(2,1)S(1)}, u32[]{:S(2)}, u32[]{:S(2)}) collective-permute-start(bf16[128,1280]{1,0:T(8,128)(2,1)S(1)} %multiply_convert_fusion.5), channel_id=1, source_target_pairs={{0,2},{1,3},{2,0},{3,1},{4,6},{5,7},{6,4},{7,5},{8,10},{9,11},{10,... | collective-permute-start | bytes 983048 | tf_op jit(solution)/shard_map/ppermute | solution.py:53
  49.5 15.2 %collective-permute-start.6 = (bf16[128,1280]{1,0:T(8,128)(2,1)S(1)}, bf16[128,1280]{1,0:T(8,128)(2,1)S(1)}, u32[]{:S(2)}, u32[]{:S(2)}) collective-permute-start(bf16[128,1280]{1,0:T(8,128)(2,1)S(1)} %multiply_convert_fusion.5), channel_id=1, source_target_pairs={{0,3},{1,2},{2,1},{3,0},{4,7},{5,6},{6,5},{7,4},{8,11},{9,10},{10,... | collective-permute-start | bytes 983048 | tf_op jit(solution)/shard_map/ppermute | solution.py:53
  64.9 23.6 %collective-permute-start.11 = (bf16[128,992]{1,0:T(8,128)(2,1)}, bf16[128,992]{1,0:T(8,128)(2,1)S(1)}, u32[]{:S(2)}, u32[]{:S(2)}) collective-permute-start(bf16[128,992]{1,0:T(8,128)(2,1)} %get-tuple-element.183), channel_id=1, source_target_pairs={{0,1},{1,0},{2,3},{3,2},{4,5},{5,4},{6,7},{7,6},{8,9},{9,8},{10,11... | collective-permute-start | bytes 761864 | tf_op jit(solution)/shard_map/ppermute | solution.py:53
  65.8 29.8 %collective-permute-start.12 = (bf16[128,992]{1,0:T(8,128)(2,1)}, bf16[128,992]{1,0:T(8,128)(2,1)S(1)}, u32[]{:S(2)}, u32[]{:S(2)}) collective-permute-start(bf16[128,992]{1,0:T(8,128)(2,1)} %get-tuple-element.182), channel_id=1, source_target_pairs={{0,2},{1,3},{2,0},{3,1},{4,6},{5,7},{6,4},{7,5},{8,10},{9,11},{10,... | collective-permute-start | bytes 761864 | tf_op jit(solution)/shard_map/ppermute | solution.py:53
  67.3 28.2 %collective-permute-start.13 = (bf16[128,992]{1,0:T(8,128)(2,1)}, bf16[128,992]{1,0:T(8,128)(2,1)S(1)}, u32[]{:S(2)}, u32[]{:S(2)}) collective-permute-start(bf16[128,992]{1,0:T(8,128)(2,1)} %get-tuple-element.181), channel_id=1, source_target_pairs={{0,3},{1,2},{2,1},{3,0},{4,7},{5,6},{6,5},{7,4},{8,11},{9,10},{10,... | collective-permute-start | bytes 761864 | tf_op jit(solution)/shard_map/ppermute | solution.py:53
  76.9 9.3 %collective-permute-start.10 = (bf16[256,768]{1,0:T(8,128)(2,1)S(1)}, bf16[256,768]{1,0:T(8,128)(2,1)S(1)}, u32[]{:S(2)}, u32[]{:S(2)}) collective-permute-start(bf16[256,768]{1,0:T(8,128)(2,1)S(1)} %pad_maximum_fusion.9), channel_id=1, source_target_pairs={{0,1},{1,0},{2,3},{3,2},{4,5},{5,4},{6,7},{7,6},{8,9},{9,8},{10,11... | collective-permute-start | bytes 1179656 | tf_op jit(solution)/shard_map/ppermute | solution.py:53
  77.7 9.1 %collective-permute-start.15 = (bf16[256,768]{1,0:T(8,128)(2,1)S(1)}, bf16[256,768]{1,0:T(8,128)(2,1)S(1)}, u32[]{:S(2)}, u32[]{:S(2)}) collective-permute-start(bf16[256,768]{1,0:T(8,128)(2,1)S(1)} %pad_maximum_fusion.10), channel_id=1, source_target_pairs={{0,2},{1,3},{2,0},{3,1},{4,6},{5,7},{6,4},{7,5},{8,10},{9,11},{10,... | collective-permute-start | bytes 1179656 | tf_op jit(solution)/shard_map/ppermute | solution.py:53
  86.2 18.4 %collective-permute-start.21 = (bf16[256,1152]{1,0:T(8,128)(2,1)S(1)}, bf16[256,1152]{1,0:T(8,128)(2,1)S(1)}, u32[]{:S(2)}, u32[]{:S(2)}) collective-permute-start(bf16[256,1152]{1,0:T(8,128)(2,1)S(1)} %pad_maximum_fusion.7), channel_id=1, source_target_pairs={{0,1},{1,0},{2,3},{3,2},{4,5},{5,4},{6,7},{7,6},{8,9},{9,8},{10,11... | collective-permute-start | bytes 1769480 | tf_op jit(solution)/shard_map/ppermute | solution.py:53
  88.4 14.7 %collective-permute-start.16 = (bf16[128,768]{1,0:T(8,128)(2,1)S(1)}, bf16[128,768]{1,0:T(8,128)(2,1)S(1)}, u32[]{:S(2)}, u32[]{:S(2)}) collective-permute-start(bf16[128,768]{1,0:T(8,128)(2,1)S(1)} %get-tuple-element.153), channel_id=1, source_target_pairs={{0,1},{1,0},{2,3},{3,2},{4,5},{5,4},{6,7},{7,6},{8,9},{9,8},{10,11... | collective-permute-start | bytes 589832 | tf_op jit(solution)/shard_map/ppermute | solution.py:53
  93.8 16.8 %collective-permute-start.25 = (bf16[256,1280]{1,0:T(8,128)(2,1)S(1)}, bf16[256,1280]{1,0:T(8,128)(2,1)S(1)}, u32[]{:S(2)}, u32[]{:S(2)}) collective-permute-start(bf16[256,1280]{1,0:T(8,128)(2,1)S(1)} %slice.329), channel_id=1, source_target_pairs={{0,2},{1,3},{2,0},{3,1},{4,6},{5,7},{6,4},{7,5},{8,10},{9,11},{10,... | collective-permute-start | bytes 1966088 | tf_op jit(solution)/shard_map/ppermute | solution.py:53
  103.6 16.7 %collective-permute-start.19 = (bf16[128,768]{1,0:T(8,128)(2,1)S(1)}, bf16[128,768]{1,0:T(8,128)(2,1)S(1)}, u32[]{:S(2)}, u32[]{:S(2)}) collective-permute-start(bf16[128,768]{1,0:T(8,128)(2,1)S(1)} %get-tuple-element.92), channel_id=1, source_target_pairs={{0,2},{1,3},{2,0},{3,1},{4,6},{5,7},{6,4},{7,5},{8,10},{9,11},{10,... | collective-permute-start | bytes 589832 | tf_op jit(solution)/shard_map/ppermute | solution.py:53
  104.1 15.2 %collective-permute-start.17 = (bf16[128,768]{1,0:T(8,128)(2,1)S(1)}, bf16[128,768]{1,0:T(8,128)(2,1)S(1)}, u32[]{:S(2)}, u32[]{:S(2)}) collective-permute-start(bf16[128,768]{1,0:T(8,128)(2,1)S(1)} %get-tuple-element.91), channel_id=1, source_target_pairs={{0,1},{1,0},{2,3},{3,2},{4,5},{5,4},{6,7},{7,6},{8,9},{9,8},{10,11... | collective-permute-start | bytes 589832 | tf_op jit(solution)/shard_map/ppermute | solution.py:53
  104.8 12.5 %collective-permute-start.22 = (bf16[128,1152]{1,0:T(8,128)(2,1)S(1)}, bf16[128,1152]{1,0:T(8,128)(2,1)S(1)}, u32[]{:S(2)}, u32[]{:S(2)}) collective-permute-start(bf16[128,1152]{1,0:T(8,128)(2,1)S(1)} %get-tuple-element.161), channel_id=1, source_target_pairs={{0,2},{1,3},{2,0},{3,1},{4,6},{5,7},{6,4},{7,5},{8,10},{9,11},{10,... | collective-permute-start | bytes 884744 | tf_op jit(solution)/shard_map/ppermute | solution.py:53
  110.7 11.7 %collective-permute-start.26 = (bf16[128,1280]{1,0:T(8,128)(2,1)S(1)}, bf16[128,1280]{1,0:T(8,128)(2,1)S(1)}, u32[]{:S(2)}, u32[]{:S(2)}) collective-permute-start(bf16[128,1280]{1,0:T(8,128)(2,1)S(1)} %get-tuple-element.157), channel_id=1, source_target_pairs={{0,1},{1,0},{2,3},{3,2},{4,5},{5,4},{6,7},{7,6},{8,9},{9,8},{10,11... | collective-permute-start | bytes 983048 | tf_op jit(solution)/shard_map/ppermute | solution.py:53
  117.8 10.0 %collective-permute-start.23 = (bf16[128,1152]{1,0:T(8,128)(2,1)S(1)}, bf16[128,1152]{1,0:T(8,128)(2,1)S(1)}, u32[]{:S(2)}, u32[]{:S(2)}) collective-permute-start(bf16[128,1152]{1,0:T(8,128)(2,1)S(1)} %loss.4), channel_id=1, source_target_pairs={{0,1},{1,0},{2,3},{3,2},{4,5},{5,4},{6,7},{7,6},{8,9},{9,8},{10,11... | collective-permute-start | bytes 884744 | tf_op jit(solution)/shard_map/ppermute | solution.py:53
  119.3 12.1 %collective-permute-start.18 = (bf16[256,768]{1,0:T(8,128)(2,1)S(1)}, bf16[256,768]{1,0:T(8,128)(2,1)S(1)}, u32[]{:S(2)}, u32[]{:S(2)}) collective-permute-start(bf16[256,768]{1,0:T(8,128)(2,1)S(1)} %pad_maximum_fusion.11), channel_id=1, source_target_pairs={{0,2},{1,3},{2,0},{3,1},{4,6},{5,7},{6,4},{7,5},{8,10},{9,11},{10,... | collective-permute-start | bytes 1179656 | tf_op jit(solution)/shard_map/ppermute | solution.py:53
  120.4 12.4 %collective-permute-start.20 = (bf16[256,768]{1,0:T(8,128)(2,1)S(1)}, bf16[256,768]{1,0:T(8,128)(2,1)S(1)}, u32[]{:S(2)}, u32[]{:S(2)}) collective-permute-start(bf16[256,768]{1,0:T(8,128)(2,1)S(1)} %pad_maximum_fusion.12), channel_id=1, source_target_pairs={{0,1},{1,0},{2,3},{3,2},{4,5},{5,4},{6,7},{7,6},{8,9},{9,8},{10,11... | collective-permute-start | bytes 1179656 | tf_op jit(solution)/shard_map/ppermute | solution.py:53
  123.0 15.5 %collective-permute-start.27 = (bf16[128,1280]{1,0:T(8,128)(2,1)S(1)}, bf16[128,1280]{1,0:T(8,128)(2,1)S(1)}, u32[]{:S(2)}, u32[]{:S(2)}) collective-permute-start(bf16[128,1280]{1,0:T(8,128)(2,1)S(1)} %loss.5), channel_id=1, source_target_pairs={{0,2},{1,3},{2,0},{3,1},{4,6},{5,7},{6,4},{7,5},{8,10},{9,11},{10,... | collective-permute-start | bytes 983048 | tf_op jit(solution)/shard_map/ppermute | solution.py:53
  127.8 17.5 %collective-permute-start.24 = (bf16[256,1152]{1,0:T(8,128)(2,1)S(1)}, bf16[256,1152]{1,0:T(8,128)(2,1)S(1)}, u32[]{:S(2)}, u32[]{:S(2)}) collective-permute-start(bf16[256,1152]{1,0:T(8,128)(2,1)S(1)} %pad_maximum_fusion.8), channel_id=1, source_target_pairs={{0,2},{1,3},{2,0},{3,1},{4,6},{5,7},{6,4},{7,5},{8,10},{9,11},{10,... | collective-permute-start | bytes 1769480 | tf_op jit(solution)/shard_map/ppermute | solution.py:53
  139.4 12.4 %collective-permute-start.28 = (bf16[256,1280]{1,0:T(8,128)(2,1)}, bf16[256,1280]{1,0:T(8,128)(2,1)}, u32[]{:S(2)}, u32[]{:S(2)}) collective-permute-start(bf16[256,1280]{1,0:T(8,128)(2,1)} %pad_maximum_fusion.6), channel_id=1, source_target_pairs={{0,1},{1,0},{2,3},{3,2},{4,5},{5,4},{6,7},{7,6},{8,9},{9,8},{10,11... | collective-permute-start | bytes 1966088 | tf_op jit(solution)/shard_map/ppermute | solution.py:53
  159.9 15.3 %collective-permute-start.32 = (bf16[4,160,1280]{2,1,0:T(8,128)(2,1)}, bf16[4,160,1280]{2,1,0:T(8,128)(2,1)}, u32[]{:S(2)}, u32[]{:S(2)}) collective-permute-start(bf16[4,160,1280]{2,1,0:T(8,128)(2,1)} %get-tuple-element.105), channel_id=1, source_target_pairs={{0,4},{4,0},{8,12},{12,8},{16,20},{20,16},{24,28},{28,24},{1,5},{5... | collective-permute-start | bytes 4915208 | tf_op jit(solution)/shard_map/ppermute | solution.py:53
  161.5 13.7 %collective-permute-start.31 = (bf16[2,192,640]{2,1,0:T(8,128)(2,1)S(1)}, bf16[2,192,640]{2,1,0:T(8,128)(2,1)S(1)}, u32[]{:S(2)}, u32[]{:S(2)}) collective-permute-start(bf16[2,192,640]{2,1,0:T(8,128)(2,1)S(1)} %slice.330), channel_id=1, source_target_pairs={{0,8},{4,12},{8,0},{12,4},{16,24},{20,28},{24,16},{28,20},{1,9},{5... | collective-permute-start | bytes 1474568 | tf_op jit(solution)/shard_map/ppermute | solution.py:53
  164.1 10.8 %collective-permute-start.30 = (bf16[128,1280]{1,0:T(8,128)(2,1)}, bf16[128,1280]{1,0:T(8,128)(2,1)S(1)}, u32[]{:S(2)}, u32[]{:S(2)}) collective-permute-start(bf16[128,1280]{1,0:T(8,128)(2,1)} %get-tuple-element.169), channel_id=1, source_target_pairs={{0,1},{1,0},{2,3},{3,2},{4,5},{5,4},{6,7},{7,6},{8,9},{9,8},{10,11... | collective-permute-start | bytes 983048 | tf_op jit(solution)/shard_map/ppermute | solution.py:53
  165.8 16.8 %collective-permute-start.33 = (bf16[128,1280]{1,0:T(8,128)(2,1)}, bf16[128,1280]{1,0:T(8,128)(2,1)S(1)}, u32[]{:S(2)}, u32[]{:S(2)}) collective-permute-start(bf16[128,1280]{1,0:T(8,128)(2,1)} %get-tuple-element.171), channel_id=1, source_target_pairs={{0,2},{1,3},{2,0},{3,1},{4,6},{5,7},{6,4},{7,5},{8,10},{9,11},{10,... | collective-permute-start | bytes 983048 | tf_op jit(solution)/shard_map/ppermute | solution.py:53
  166.3 16.2 %collective-permute-start.34 = (bf16[128,1280]{1,0:T(8,128)(2,1)S(1)}, bf16[128,1280]{1,0:T(8,128)(2,1)S(1)}, u32[]{:S(2)}, u32[]{:S(2)}) collective-permute-start(bf16[128,1280]{1,0:T(8,128)(2,1)S(1)} %get-tuple-element.170), channel_id=1, source_target_pairs={{0,3},{1,2},{2,1},{3,0},{4,7},{5,6},{6,5},{7,4},{8,11},{9,10},{10,... | collective-permute-start | bytes 983048 | tf_op jit(solution)/shard_map/ppermute | solution.py:53
  177.5 19.7 %collective-permute-start.39 = (bf16[2,160,1280]{2,1,0:T(8,128)(2,1)S(1)}, bf16[2,160,1280]{2,1,0:T(8,128)(2,1)}, u32[]{:S(2)}, u32[]{:S(2)}) collective-permute-start(bf16[2,160,1280]{2,1,0:T(8,128)(2,1)S(1)} %slice.328), channel_id=1, source_target_pairs={{0,8},{4,12},{8,0},{12,4},{16,24},{20,28},{24,16},{28,20},{1,9},{5... | collective-permute-start | bytes 2457608 | tf_op jit(solution)/shard_map/ppermute | solution.py:53
  183.3 11.7 %collective-permute-start.37 = (bf16[128,1280]{1,0:T(8,128)(2,1)S(1)}, bf16[128,1280]{1,0:T(8,128)(2,1)S(1)}, u32[]{:S(2)}, u32[]{:S(2)}) collective-permute-start(bf16[128,1280]{1,0:T(8,128)(2,1)S(1)} %multiply_convert_fusion.4), channel_id=1, source_target_pairs={{0,3},{1,2},{2,1},{3,0},{4,7},{5,6},{6,5},{7,4},{8,11},{9,10},{10,... | collective-permute-start | bytes 983048 | tf_op jit(solution)/shard_map/ppermute | solution.py:53
  184.5 14.4 %collective-permute-start.35 = (bf16[128,1280]{1,0:T(8,128)(2,1)S(1)}, bf16[128,1280]{1,0:T(8,128)(2,1)S(1)}, u32[]{:S(2)}, u32[]{:S(2)}) collective-permute-start(bf16[128,1280]{1,0:T(8,128)(2,1)S(1)} %multiply_convert_fusion.4), channel_id=1, source_target_pairs={{0,1},{1,0},{2,3},{3,2},{4,5},{5,4},{6,7},{7,6},{8,9},{9,8},{10,11... | collective-permute-start | bytes 983048 | tf_op jit(solution)/shard_map/ppermute | solution.py:53
  185.3 14.3 %collective-permute-start.36 = (bf16[128,1280]{1,0:T(8,128)(2,1)S(1)}, bf16[128,1280]{1,0:T(8,128)(2,1)S(1)}, u32[]{:S(2)}, u32[]{:S(2)}) collective-permute-start(bf16[128,1280]{1,0:T(8,128)(2,1)S(1)} %multiply_convert_fusion.4), channel_id=1, source_target_pairs={{0,2},{1,3},{2,0},{3,1},{4,6},{5,7},{6,4},{7,5},{8,10},{9,11},{10,... | collective-permute-start | bytes 983048 | tf_op jit(solution)/shard_map/ppermute | solution.py:53
  207.1 8.0 %collective-permute-start.40 = (bf16[4,160,1280]{2,1,0:T(8,128)(2,1)S(1)}, bf16[4,160,1280]{2,1,0:T(8,128)(2,1)S(1)}, u32[]{:S(2)}, u32[]{:S(2)}) collective-permute-start(bf16[4,160,1280]{2,1,0:T(8,128)(2,1)S(1)} %get-tuple-element.117), channel_id=1, source_target_pairs={{0,4},{4,0},{8,12},{12,8},{16,20},{20,16},{24,28},{28,24},{1,5},{5... | collective-permute-start | bytes 4915208 | tf_op jit(solution)/shard_map/ppermute | solution.py:53
  207.2 9.7 %collective-permute-start.43 = (bf16[2,160,128]{2,1,0:T(8,128)(2,1)S(1)}, bf16[2,160,128]{2,1,0:T(8,128)(2,1)S(1)}, u32[]{:S(2)}, u32[]{:S(2)}) collective-permute-start(bf16[2,160,128]{2,1,0:T(8,128)(2,1)S(1)} %pad_maximum_fusion.18), channel_id=1, source_target_pairs={{0,24},{4,28},{8,16},{12,20},{16,8},{20,12},{24,0},{28,4},{1,25},{... | collective-permute-start | bytes 245768 | tf_op jit(solution)/shard_map/ppermute | solution.py:53
  209.9 17.6 %collective-permute-start.42 = (bf16[2,160,128]{2,1,0:T(8,128)(2,1)S(1)}, bf16[2,160,128]{2,1,0:T(8,128)(2,1)S(1)}, u32[]{:S(2)}, u32[]{:S(2)}) collective-permute-start(bf16[2,160,128]{2,1,0:T(8,128)(2,1)S(1)} %pad_maximum_fusion.17), channel_id=1, source_target_pairs={{0,16},{4,20},{8,24},{12,28},{16,0},{20,4},{24,8},{28,12},{1,17},{... | collective-permute-start | bytes 245768 | tf_op jit(solution)/shard_map/ppermute | solution.py:53
  210.2 17.3 %collective-permute-start.41 = (bf16[2,160,128]{2,1,0:T(8,128)(2,1)S(1)}, bf16[2,160,128]{2,1,0:T(8,128)(2,1)S(1)}, u32[]{:S(2)}, u32[]{:S(2)}) collective-permute-start(bf16[2,160,128]{2,1,0:T(8,128)(2,1)S(1)} %pad_maximum_fusion.16), channel_id=1, source_target_pairs={{0,8},{4,12},{8,0},{12,4},{16,24},{20,28},{24,16},{28,20},{1,9},{5... | collective-permute-start | bytes 245768 | tf_op jit(solution)/shard_map/ppermute | solution.py:53
  213.2 22.9 %collective-permute-start.45 = (bf16[1,160,1280]{2,1,0:T(8,128)(2,1)S(1)}, bf16[1,160,1280]{2,1,0:T(8,128)(2,1)S(1)}, u32[]{:S(2)}, u32[]{:S(2)}) collective-permute-start(bf16[1,160,1280]{2,1,0:T(8,128)(2,1)S(1)} %slice.331), channel_id=1, source_target_pairs={{0,16},{4,20},{8,24},{12,28},{16,0},{20,4},{24,8},{28,12},{1,17},{... | collective-permute-start | bytes 1228808 | tf_op jit(solution)/shard_map/ppermute | solution.py:53
  215.5 34.9 %collective-permute-start.44 = (bf16[2,160,1280]{2,1,0:T(8,128)(2,1)S(1)}, bf16[2,160,1280]{2,1,0:T(8,128)(2,1)S(1)}, u32[]{:S(2)}, u32[]{:S(2)}) collective-permute-start(bf16[2,160,1280]{2,1,0:T(8,128)(2,1)S(1)} %get-tuple-element.121), channel_id=1, source_target_pairs={{0,8},{4,12},{8,0},{12,4},{16,24},{20,28},{24,16},{28,20},{1,9},{5... | collective-permute-start | bytes 2457608 | tf_op jit(solution)/shard_map/ppermute | solution.py:53
  227.6 10.7 %collective-permute-start.46 = (bf16[8,160,128]{2,1,0:T(8,128)(2,1)S(1)}, bf16[8,160,128]{2,1,0:T(8,128)(2,1)S(1)}, u32[]{:S(2)}, u32[]{:S(2)}) collective-permute-start(bf16[8,160,128]{2,1,0:T(8,128)(2,1)S(1)} %constant_dynamic-update-slice_fusion.3.refs_0_), channel_id=1, source_target_pairs={{0,1},{1,0},{2,3},{3,2},{4,5},{5,4},{6,7},{7,6},{8,9},{9,8},{10,11... | collective-permute-start | bytes 983048 | tf_op jit(solution)/shard_map/ppermute | solution.py:53
  228.4 16.0 %collective-permute-start.47 = (bf16[8,160,128]{2,1,0:T(8,128)(2,1)S(1)}, bf16[8,160,128]{2,1,0:T(8,128)(2,1)S(1)}, u32[]{:S(2)}, u32[]{:S(2)}) collective-permute-start(bf16[8,160,128]{2,1,0:T(8,128)(2,1)S(1)} %constant_dynamic-update-slice_fusion.3.refs_0_), channel_id=1, source_target_pairs={{0,2},{1,3},{2,0},{3,1},{4,6},{5,7},{6,4},{7,5},{8,10},{9,11},{10,... | collective-permute-start | bytes 983048 | tf_op jit(solution)/shard_map/ppermute | solution.py:53
  229.8 14.6 %collective-permute-start.48 = (bf16[8,160,128]{2,1,0:T(8,128)(2,1)S(1)}, bf16[8,160,128]{2,1,0:T(8,128)(2,1)S(1)}, u32[]{:S(2)}, u32[]{:S(2)}) collective-permute-start(bf16[8,160,128]{2,1,0:T(8,128)(2,1)S(1)} %constant_dynamic-update-slice_fusion.3.refs_0_), channel_id=1, source_target_pairs={{0,3},{1,2},{2,1},{3,0},{4,7},{5,6},{6,5},{7,4},{8,11},{9,10},{10,... | collective-permute-start | bytes 983048 | tf_op jit(solution)/shard_map/ppermute | solution.py:53
  236.1 23.3 %collective-permute-start.50 = (bf16[1,192,640]{2,1,0:T(8,128)(2,1)S(1)}, bf16[1,192,640]{2,1,0:T(8,128)(2,1)S(1)}, u32[]{:S(2)}, u32[]{:S(2)}) collective-permute-start(bf16[1,192,640]{2,1,0:T(8,128)(2,1)S(1)} %slice.332), channel_id=1, source_target_pairs={{0,16},{4,20},{8,24},{12,28},{16,0},{20,4},{24,8},{28,12},{1,17},{... | collective-permute-start | bytes 737288 | tf_op jit(solution)/shard_map/ppermute | solution.py:53
  250.5 18.9 %collective-permute-start.49 = (bf16[1,160,1280]{2,1,0:T(8,128)(2,1)S(1)}, bf16[1,160,1280]{2,1,0:T(8,128)(2,1)S(1)}, u32[]{:S(2)}, u32[]{:S(2)}) collective-permute-start(bf16[1,160,1280]{2,1,0:T(8,128)(2,1)S(1)} %get-tuple-element.129), channel_id=1, source_target_pairs={{0,16},{4,20},{8,24},{12,28},{16,0},{20,4},{24,8},{28,12},{1,17},{... | collective-permute-start | bytes 1228808 | tf_op jit(solution)/shard_map/ppermute | solution.py:53
  (40 other events, 245.3 us)
Sparse Core Ops, SparseCore 0:
  65.0 99.9 all-gather.2
